TPU v7x, 32 devices: a whole 2x2x4 slice. The times are simulated.
32 devices in a mesh: seq: 8 (over z, core), tp: 4 (over y, x).
Axes of the slice: x: 2, y: 2, z: 4, core: 2. Of those that a mesh axis runs over, the one named last changes fastest.
Arguments:
- inputs: bfloat16 [24576, 1024], P('seq'), may hold values from -6 to 6
- w_in: bfloat16 [3, 1024, 1024], P(None, None, 'tp'), may hold values from -0.1875 to 0.1875
- conv_w: bfloat16 [3, 1024], P(None, 'tp'), may hold values from -3.5 to 3.5
- w_out: bfloat16 [1024, 1024], P('tp'), may hold values from -0.1875 to 0.1875
- norm_one: bfloat16 [1024], replicated, may hold values from 0.5 to 1.5
- norm_two: bfloat16 [1024], replicated, may hold values from 0.5 to 1.5
- w_gate: bfloat16 [1024, 4608], P(None, 'tp'), may hold values from -0.1875 to 0.1875
- w_up: bfloat16 [1024, 4608], P(None, 'tp'), may hold values from -0.1875 to 0.1875
- w_down: bfloat16 [4608, 1024], P('tp'), may hold values from -0.09375 to 0.09375
- lengths: int32 [6], replicated, may hold values from 2048 to 4096, as said below
- cotangent: bfloat16 [24576, 1024], P('seq'), may hold values from -6 to 6
Outputs:
- output: bfloat16 [24576, 1024], P('seq')
- grad_inputs: float32 [24576, 1024], P('seq')
- grad_w_in: float32 [3, 1024, 1024], P(None, None, 'tp')
- grad_conv: float32 [3, 1024], P(None, 'tp')
- grad_w_out: float32 [1024, 1024], P('tp')
- grad_norm_one: float32 [1024], replicated
- grad_norm_two: float32 [1024], replicated
- grad_w_gate: float32 [1024, 4608], P(None, 'tp')
- grad_w_up: float32 [1024, 4608], P(None, 'tp')
- grad_w_down: float32 [4608, 1024], P('tp')
Inputs may be any that keep to these rules, and one draw needn't show every extreme that they name: `lengths`: one sequence, drawn from the seed, has length 4096; the others at least half of it.
All inputs are finite; a program needn't handle non-finite values.
Results may differ from a plain program's by a relative error of at most 0.011.
Values may be sent and summed in bfloat16 or wider, within the bound.
No kernel may reach another device: no remote copies, remote signals or barrier semaphores. Data moves between devices by JAX's collectives and lax.ppermute only.
A program may use at most 256 MiB of HBM per device.

v0:
```python
import jax
import jax.numpy as jnp
from jax import lax
from jax.sharding import PartitionSpec as P

SEQS = 6


def passed_along(value, axis, steps):
    count = lax.axis_size(axis)
    leading, last = (max(0, -steps), min(count, count - steps))
    return lax.ppermute(value, axis, [(source, source + steps) for source in range(leading, last)])


def rms_scale(values):
    return lax.rsqrt(jnp.mean(values * values, axis=1, keepdims=True) + 1e-05)


def matmul(left, right):
    return jnp.dot(left, right, preferred_element_type=jnp.float32)


def left_matmul(left, right):
    return lax.dot_general(
        left, right, (((0,), (0,)), ((), ())), preferred_element_type=jnp.float32
    )


def right_matmul(left, right):
    return lax.dot_general(
        left, right, (((1,), (1,)), ((), ())), preferred_element_type=jnp.float32
    )


def per_device(
    inputs, w_in, conv_w, w_out, norm_one, norm_two, w_gate, w_up, w_down, lengths, cotangent
):
    floats = jnp.float32
    halves = jnp.bfloat16
    rows = inputs.shape[0]
    slot_len = rows * lax.axis_size("seq") // SEQS
    place = lax.axis_index("seq") * rows + jnp.arange(rows, dtype=jnp.int32)
    seq_of = place // slot_len
    offset = place - seq_of * slot_len
    limit = jnp.sum(
        jnp.where(
            seq_of[:, None] == jnp.arange(SEQS, dtype=jnp.int32)[None, :], lengths[None, :], 0
        ),
        axis=1,
    )
    real = (offset < limit).astype(floats)[:, None]
    first_lag = (offset >= 1).astype(floats)[:, None]
    second_lag = (offset >= 2).astype(floats)[:, None]
    gain_one = norm_one.astype(floats)[None, :]
    gain_two = norm_two.astype(floats)[None, :]
    kernel = conv_w.astype(floats)
    xfull = inputs.astype(floats)
    scale_one = rms_scale(xfull)
    normed_one = xfull * scale_one
    hidden_one = (normed_one * gain_one).astype(halves)
    proj_b = matmul(hidden_one, w_in[0])
    proj_c = matmul(hidden_one, w_in[1])
    proj_x = matmul(hidden_one, w_in[2])
    mixed_in = (proj_b * proj_x).astype(halves)
    rims = passed_along(mixed_in[rows - 2 :], "seq", 1)
    extended = jnp.concatenate([rims, mixed_in], axis=0).astype(floats)
    current = extended[2:]
    lag_one = extended[1 : rows + 1] * first_lag
    lag_two = extended[0:rows] * second_lag
    conved = (
        kernel[2][None, :] * current + kernel[1][None, :] * lag_one + kernel[0][None, :] * lag_two
    )
    gated = (proj_c * conved).astype(halves)
    grad_out = cotangent.astype(floats) * real
    grad_low = grad_out.astype(halves)
    mixer_out = lax.psum(matmul(gated, w_out), "tp")
    resid = xfull + mixer_out
    scale_two = rms_scale(resid)
    normed_two = resid * scale_two
    hidden_two = (normed_two * gain_two).astype(halves)
    gate_pre = matmul(hidden_two, w_gate)
    up_pre = matmul(hidden_two, w_up)
    sigmoid_val = jax.nn.sigmoid(gate_pre)
    silu_val = gate_pre * sigmoid_val
    activ = (silu_val * up_pre).astype(halves)
    d_activ = right_matmul(grad_low, w_down)
    grad_w_down = left_matmul(activ, grad_low)
    grad_gate_pre = (
        d_activ * up_pre * sigmoid_val * (1.0 + gate_pre * (1.0 - sigmoid_val))
    ).astype(halves)
    grad_up_pre = (d_activ * silu_val).astype(halves)
    grad_w_gate = left_matmul(hidden_two, grad_gate_pre)
    grad_w_up = left_matmul(hidden_two, grad_up_pre)
    ffn_out = lax.psum(matmul(activ, w_down), "tp")
    output = (resid + ffn_out).astype(halves)
    part_two = right_matmul(grad_gate_pre, w_gate) + right_matmul(grad_up_pre, w_up)
    d_hidden_two = lax.psum(part_two, "tp")
    grad_norm_two = jnp.sum(d_hidden_two * normed_two, axis=0)
    d_normed_two = d_hidden_two * gain_two
    grad_resid = grad_out + scale_two * (
        d_normed_two - normed_two * jnp.mean(d_normed_two * normed_two, axis=1, keepdims=True)
    )
    grad_resid_low = grad_resid.astype(halves)
    d_gated = right_matmul(grad_resid_low, w_out)
    grad_w_out = left_matmul(gated, grad_resid_low)
    d_conved = d_gated * proj_c
    grad_proj_c = (d_gated * conved).astype(halves)
    edge_one = d_conved * first_lag
    edge_two = d_conved * second_lag
    incoming = passed_along(jnp.stack([edge_one[:2], edge_two[:2]]), "seq", -1)
    next_one = jnp.concatenate([edge_one[1:], incoming[0, :1]], axis=0)
    next_two = jnp.concatenate([edge_two[2:], incoming[1]], axis=0)
    d_mixed = (
        kernel[2][None, :] * d_conved
        + kernel[1][None, :] * next_one
        + kernel[0][None, :] * next_two
    )
    grad_conv = jnp.stack(
        [
            jnp.sum(d_conved * lag_two, axis=0),
            jnp.sum(d_conved * lag_one, axis=0),
            jnp.sum(d_conved * current, axis=0),
        ]
    )
    grad_proj_b = (d_mixed * proj_x).astype(halves)
    grad_proj_x = (d_mixed * proj_b).astype(halves)
    grad_w_in = jnp.stack(
        [
            left_matmul(hidden_one, grad_proj_b),
            left_matmul(hidden_one, grad_proj_c),
            left_matmul(hidden_one, grad_proj_x),
        ]
    )
    part_one = (
        right_matmul(grad_proj_b, w_in[0])
        + right_matmul(grad_proj_c, w_in[1])
        + right_matmul(grad_proj_x, w_in[2])
    )
    d_hidden_one = lax.psum(part_one, "tp")
    grad_norm_one = jnp.sum(d_hidden_one * normed_one, axis=0)
    d_normed_one = d_hidden_one * gain_one
    grad_inputs = grad_resid + scale_one * (
        d_normed_one - normed_one * jnp.mean(d_normed_one * normed_one, axis=1, keepdims=True)
    )
    (
        grad_w_in,
        grad_conv,
        grad_w_out,
        grad_norm_one,
        grad_norm_two,
        grad_w_gate,
        grad_w_up,
        grad_w_down,
    ) = lax.psum(
        (
            grad_w_in,
            grad_conv,
            grad_w_out,
            grad_norm_one,
            grad_norm_two,
            grad_w_gate,
            grad_w_up,
            grad_w_down,
        ),
        "seq",
    )
    return (
        output,
        grad_inputs,
        grad_w_in,
        grad_conv,
        grad_w_out,
        grad_norm_one,
        grad_norm_two,
        grad_w_gate,
        grad_w_up,
        grad_w_down,
    )


def solution(mesh):
    return jax.shard_map(
        per_device,
        mesh=mesh,
        in_specs=(
            P("seq", None),
            P(None, None, "tp"),
            P(None, "tp"),
            P("tp", None),
            P(),
            P(),
            P(None, "tp"),
            P(None, "tp"),
            P("tp", None),
            P(),
            P("seq", None),
        ),
        out_specs=(
            P("seq", None),
            P("seq", None),
            P(None, None, "tp"),
            P(None, "tp"),
            P("tp", None),
            P(),
            P(),
            P(None, "tp"),
            P(None, "tp"),
            P("tp", None),
        ),
        check_vma=False,
    )
```

profile of v0, /device:TPU:0, one launch (start us, length us, event | category | flops | bytes accessed | tf_op | source)
XLA Modules:
  0.0 1521.4 jit_solution(15218738786776546902)
XLA Ops:
  8.1 4.4 fusion.11
  16.9 3.5 multiply_convert_fusion.8
  26.5 8.0 multiply_convert_fusion.7
  35.7 6.6 fusion.45
  42.9 243.5 %all-reduce.8.cloned.1.call-done = f32[3072,1024]{1,0:T(8,128)} async-done(((f32[3072,1024]{1,0:T(8,128)}), f32[3072,1024]{1,0:T(8,128)}) %all-reduce.8.cloned.1.call-update) | async-done | bytes 12582928 | tf_op jit(solution)/shard_map/psum | solution.py:76
  286.4 7.3 multiply_reduce_fusion.2
  293.7 4.8 copy-done.2
  300.2 10.8 fusion.47
  311.0 10.9 fusion.46
  321.9 25.7 %multiply_convert_fusion = (bf16[3072,1152]{1,0:T(8,128)(2,1)}, bf16[3072,1152]{1,0:T(8,128)(2,1)}, bf16[3072,1152]{1,0:T(8,128)(2,1)}) fusion(f32[3072,1152]{1,0:T(8,128)} %fusion.46, f32[3072,1152]{1,0:T(8,128)} %fusion.47, bf16[1152,1024]{1,0:T(8,128)(2,1)S(1)} %copy-done, bf16[3072,1024]{1,0:T(8,128)(2,1)} %param.21, f32[3072]{0:T(1024)S(1)} %get-tuple-element.46), kind=kOutput, calls=%fused_computation.7 | convolution fusion | flops 7310278656 | bytes 58208256 | tf_op jit(solution)/shard_map/dot_general | solution.py:30
  347.6 14.7 fusion.49
  362.3 13.8 convolution_add_fusion
  376.2 13.2 fusion.48
  389.4 226.5 %all-reduce.10.cloned.1.call-done = f32[3072,1024]{1,0:T(8,128)} async-done(((f32[3072,1024]{1,0:T(8,128)}), f32[3072,1024]{1,0:T(8,128)}) %all-reduce.10.cloned.1.call-update) | async-done | bytes 12582928 | tf_op jit(solution)/shard_map/psum | solution.py:97
  615.9 9.6 multiply_reduce_fusion
  625.5 11.8 multiply_add_fusion
  639.2 4.5 copy-done.3
  650.4 6.5 fusion.30
  661.4 2.9 multiply_convert_fusion.6
  664.3 6.3 fusion.26
  670.7 14.6 add_add_fusion
  685.6 14.1 fusion.51
  699.8 14.5 fusion.50
  714.3 13.1 fusion.19
  729.3 2.8 fusion.15
  737.7 392.9 %all-reduce.14.cloned.1.call-done = (f32[3072,1024]{1,0:T(8,128)}, f32[3072,1024]{1,0:T(8,128)}) async-done(((f32[3072,1024]{1,0:T(8,128)}, f32[3072,1024]{1,0:T(8,128)}), (f32[3072,1024]{1,0:T(8,128)}, f32[3072,1024]{1,0:T(8,128)})) %all-reduce.14.cloned.1.call-update) | async-done | bytes 25165840 | tf_op jit(solution)/shard_map/psum | solution.py:94
  1130.6 8.1 fusion.10
  1138.7 30.0 %all-reduce = (f32[3,256]{1,0:T(4,128)}, f32[1024]{0:T(1024)}, f32[1024]{0:T(1024)}) all-reduce(f32[3,256]{1,0:T(4,128)S(1)} %pad_maximum_fusion.2, f32[1024]{0:T(1024)S(1)} %get-tuple-element.12, f32[1024]{0:T(1024)S(1)} %get-tuple-element.10), channel_id=1, replica_groups=mesh['seq'=8,'tp'=4] {'seq'}, use_global_device_ids=true, to_apply=%region_13.14 | all-reduce | flops 2816 | bytes 22528 | tf_op jit(solution)/shard_map/psum | solution.py:154
  1168.8 12.4 add_convert_fusion
  1183.4 13.0 fusion.9
  1196.3 305.0 %all-reduce.12.cloned.1.call-done = (f32[3,1024,256]{2,1,0:T(8,128)}, f32[256,1024]{1,0:T(8,128)}, f32[1024,1152]{1,0:T(8,128)}, f32[1024,1152]{1,0:T(8,128)}, f32[1152,1024]{1,0:T(8,128)}) async-done(((f32[3,1024,256]{2,1,0:T(8,128)}, f32[256,1024]{1,0:T(8,128)}, f32[1024,1152]{1,0:T(8,128)}, f32[1024,1152]{1,0:T(8,128)}, f32[1152,1024]{1,0:T(8,128)}), (f32[3,1024,256]{2,1,0:T(8,128)}, ...) | async-done | bytes 18350096 | tf_op jit(solution)/shard_map/psum | solution.py:154
  1501.4 3.9 copy.30
  (168 shorter events, 47.0 us)
Async XLA Ops:
  7.2 314.7 %copy-start = (bf16[1152,1024]{1,0:T(8,128)(2,1)S(1)}, bf16[1152,1024]{1,0:T(8,128)(2,1)}, u32[]{:S(2)}) copy-start(bf16[1152,1024]{1,0:T(8,128)(2,1)} %param.19) | copy-start | bytes 7077892
  7.2 279.2 %all-reduce.8.cloned.1.call-start = ((), (), s32[]{:S(2)}) async-start(), calls=%async_computation | async-start | bytes 25165824 | tf_op jit(solution)/shard_map/psum | solution.py:76
  21.6 3.2 collective-permute-start
  23.9 10.5 copy-start.38
  23.9 10.5 copy-start.40
  24.0 10.5 copy-start.42
  24.1 10.3 copy-start.33
  24.2 10.3 copy-start.31
  26.4 9.2 copy-start.26
  42.3 573.6 %all-reduce.10.cloned.1.call-start = ((), (), s32[]{:S(2)}) async-start(), calls=%async_computation.1 | async-start | bytes 25165824 | tf_op jit(solution)/shard_map/psum | solution.py:97
  300.2 10.8 copy-start.19
  300.2 10.8 copy-start.46
  347.6 14.7 copy-start.48
  347.6 14.7 copy-start.49
  376.2 754.4 %all-reduce.14.cloned.1.call-start = ((), (), s32[]{:S(2)}) async-start(), calls=%async_computation.3 | async-start | bytes 50331648 | tf_op jit(solution)/shard_map/psum | solution.py:94
  625.5 11.9 copy-start.27
  637.4 8.3 copy-start.23
  637.4 8.3 copy-start.32
  637.4 8.2 copy-start.34
  648.9 8.4 collective-permute-start.1
  661.4 9.2 copy-start.14
  685.3 816.0 %all-reduce.12.cloned.1.call-start = ((), (), s32[]{:S(2)}) async-start(), calls=%async_computation.2 | async-start | bytes 36700160 | tf_op jit(solution)/shard_map/psum | solution.py:154
  685.6 28.6 %slice-start.5 = ((s8[6291456]{0:T(1024)(128)(4,1)}), s8[4194304]{0:T(1024)(128)(4,1)S(1)}, s32[]{:S(2)}) async-start(s8[6291456]{0:T(1024)(128)(4,1)} %bitcast.75), calls=%async_computation.9 | async-start | bytes 8388608
  699.8 14.5 slice-start.6
  699.8 27.6 %slice-start.3 = ((s8[6291456]{0:T(1024)(128)(4,1)}), s8[4194304]{0:T(1024)(128)(4,1)S(1)}, s32[]{:S(2)}) async-start(s8[6291456]{0:T(1024)(128)(4,1)} %bitcast.73), calls=%async_computation.7 | async-start | bytes 8388608
  699.8 29.5 %slice-start = ((s8[12582912]{0:T(1024)(128)(4,1)}), s8[4194304]{0:T(1024)(128)(4,1)S(1)}, s32[]{:S(2)}) async-start(s8[12582912]{0:T(1024)(128)(4,1)} %bitcast.71), calls=%async_computation.4 | async-start | bytes 8388608
  699.8 29.5 %slice-start.1 = ((s8[12582912]{0:T(1024)(128)(4,1)}), s8[4194304]{0:T(1024)(128)(4,1)S(1)}, s32[]{:S(2)}) async-start(s8[12582912]{0:T(1024)(128)(4,1)} %bitcast.71), calls=%async_computation.5 | async-start | bytes 8388608
  714.2 13.1 slice-start.4
  714.3 15.0 slice-start.2
  737.7 392.9 %copy-start.30 = (f32[3072]{0:T(1024)S(1)}, f32[3072]{0:T(1024)}, u32[]{:S(2)}) copy-start(f32[3072]{0:T(1024)} %copy-done.29) | copy-start | bytes 36868
  737.7 392.9 %copy-start.36 = (f32[1024]{0:T(1024)S(1)}, f32[1024]{0:T(1024)}, u32[]{:S(2)}) copy-start(f32[1024]{0:T(1024)} %copy-done.35) | copy-start | bytes 12292
  1168.8 14.6 copy-start.6
  (33 other events, 124.8 us)
Sparse Core Ops, SparseCore 0:
  42.4 243.9 all-reduce.7
  376.3 239.5 all-reduce.9
  685.5 445.0 all-reduce.13
  1134.8 366.5 all-reduce.11
where the time goes:
time: 1530 us; the launch traced here: 1520 us
  waiting for transfers between devices  1170 us (76%)
  matrix products  188 us (12%)
  other arithmetic  82.9 us (5%)
  local copies, waits for them, and re-layouts  32.5 us (2%)
  blocking collectives  30 us (2%)
    psum x1, waiting for transfers between devices, per_device(): ffn_out = lax.psum(matmul(activ, w_down), 'tp')  393 us
    psum x1, waiting for transfers between devices, per_device(): lax.psum((grad_w_in, grad_conv, grad_w_out, grad_norm_one, grad_norm_two,...  305 us
    psum x1, waiting for transfers between devices, per_device(): mixer_out = lax.psum(matmul(gated, w_out), 'tp')  243 us
    psum x1, waiting for transfers between devices, per_device(): d_hidden_two = lax.psum(part_two, 'tp')  226 us
    dot_general x7, matrix products, right_matmul(): lax.dot_general(left, right, (((1,), (1,)), ((), ())), preferred_element_...  83.5 us
    dot_general x7, matrix products, matmul(): return jnp.dot(left, right, preferred_element_type=jnp.float32)  54.7 us
    dot_general x7, matrix products, left_matmul(): lax.dot_general(left, right, (((0,), (0,)), ((), ())), preferred_element_...  50 us
    unnamed x123, local copies, waits for them, and re-layouts  32 us
  transfers between devices with their start and end apart: 6, of which 5 were waited for; matrix products, arithmetic and copies ran while one was open for 7% of the time, Pallas kernels for 0%

commit v1 on v0

v1 whole, which is shorter than its diff:
```python
import functools

import jax
import jax.numpy as jnp
from jax import lax
from jax.experimental import pallas as pl
from jax.experimental.pallas import tpu as pltpu
from jax.sharding import PartitionSpec as P

SEQS = 6
F32 = jnp.float32
BF16 = jnp.bfloat16
VMEM_LIMIT = 56 * 2**20


def params():
    return pltpu.CompilerParams(vmem_limit_bytes=VMEM_LIMIT)


def cost(flops, moved):
    return pl.CostEstimate(flops=int(flops), bytes_accessed=int(moved), transcendentals=0)


def nbytes(*arrays):
    return sum(a.size * a.dtype.itemsize for a in arrays)


def shape(dims, dtype):
    return jax.ShapeDtypeStruct(dims, dtype)


def dot(left, right):
    return jnp.dot(left, right, preferred_element_type=F32)


def dot_nt(left, right):
    return lax.dot_general(left, right, (((1,), (1,)), ((), ())), preferred_element_type=F32)


def dot_tn(left, right):
    return lax.dot_general(left, right, (((0,), (0,)), ((), ())), preferred_element_type=F32)


def rms_scale(values):
    return lax.rsqrt(jnp.mean(values * values, axis=1, keepdims=True) + 1e-05)


def resident(array):
    zeros = (0,) * array.ndim
    return pl.BlockSpec(array.shape, lambda i, *_: zeros, pipeline_mode=pl.Buffered(1))


def mixer_forward_body(slot, base, x, halo, gain_one, gain_two, taps, w_b, w_c, w_x, w_out,
                       h1, p_b, p_c, p_x, conv, gated, resid, h2, carry):
    step = pl.program_id(0)
    rows = x.shape[0]

    def hidden(values):
        wide = values.astype(F32)
        return wide, ((wide * rms_scale(wide)) * gain_one[...]).astype(BF16)

    @pl.when(step == 0)
    def _():
        _, before = hidden(halo[...])
        mixed = (dot(before, w_b[...]) * dot(before, w_x[...])).astype(BF16).astype(F32)
        carry[...] = mixed[8:16]

    wide, low = hidden(x[...])
    h1[...] = low
    b = dot(low, w_b[...])
    xx = dot(low, w_x[...])
    c = dot(low, w_c[...])
    p_b[...] = b.astype(BF16)
    p_x[...] = xx.astype(BF16)
    p_c[...] = c.astype(BF16)
    mixed = (b * xx).astype(BF16).astype(F32)
    fresh = lax.rem(base[0] + step * rows, slot) == 0
    last = jnp.where(fresh, 0.0, carry[...])
    row = lax.broadcasted_iota(jnp.int32, mixed.shape, 0)
    one = jnp.where(row == 0, last[7:8], pltpu.roll(mixed, 1, 0))
    two = jnp.where(row == 0, last[6:7], jnp.where(row == 1, last[7:8], pltpu.roll(mixed, 2, 0)))
    carry[...] = mixed[rows - 8:]
    conved = taps[2:3] * mixed + taps[1:2] * one + taps[0:1] * two
    conv[...] = conved.astype(BF16)
    gate = (c * conved).astype(BF16)
    gated[...] = gate
    res = wide + dot(gate, w_out[...])
    resid[...] = res
    h2[...] = ((res * rms_scale(res)) * gain_two[...]).astype(BF16)


def mixer_forward(slot, base, x, halo, gain_one, gain_two, taps, w_b, w_c, w_x, w_out, tile=256):
    rows, width = x.shape
    chans = w_b.shape[1]
    row = lambda n: pl.BlockSpec((tile, n), lambda i, *_: (i, 0))
    outs = [shape((rows, width), BF16)] + [shape((rows, chans), BF16)] * 5 + [
        shape((rows, width), F32), shape((rows, width), BF16)]
    return pl.pallas_call(
        functools.partial(mixer_forward_body, slot),
        grid_spec=pltpu.PrefetchScalarGridSpec(
            num_scalar_prefetch=1,
            grid=(rows // tile,),
            in_specs=[row(width)] + [resident(a) for a in (halo, gain_one, gain_two, taps, w_b, w_c, w_x, w_out)],
            out_specs=[row(s.shape[1]) for s in outs],
            scratch_shapes=[pltpu.VMEM((8, chans), F32)],
        ),
        out_shape=outs,
        compiler_params=params(),
        cost_estimate=cost(8 * rows * width * chans, nbytes(x, w_b, w_c, w_x, w_out, *outs)),
        name="mixer_forward",
    )(base, x, halo, gain_one, gain_two, taps, w_b, w_c, w_x, w_out)


def ffn_body(h2, grad, w_gu, w_down, out, back, activ, grads):
    units = w_down.shape[0]
    both = dot(h2[...], w_gu[...])
    d_activ = dot_nt(grad[...], w_down[...])
    gate = both[:, :units]
    up = both[:, units:]
    sig = 1.0 / (1.0 + jnp.exp(-gate))
    silu = gate * sig
    act = (silu * up).astype(BF16)
    g_gate = (d_activ * up * sig * (1.0 + gate * (1.0 - sig))).astype(BF16)
    g_up = (d_activ * silu).astype(BF16)
    activ[...] = act
    pair = jnp.concatenate([g_gate, g_up], axis=1)
    grads[...] = pair
    out[...] = dot(act, w_down[...]).astype(BF16)
    back[...] = dot_nt(pair, w_gu[...]).astype(BF16)


def ffn(h2, grad, w_gu, w_down, tile=256):
    rows, width = h2.shape
    units = w_down.shape[0]
    row = lambda n: pl.BlockSpec((tile, n), lambda i: (i, 0))
    outs = [shape((rows, width), BF16)] * 2 + [shape((rows, units), BF16), shape((rows, 2 * units), BF16)]
    return pl.pallas_call(
        ffn_body,
        grid=(rows // tile,),
        in_specs=[row(width), row(width), resident(w_gu), resident(w_down)],
        out_specs=[row(s.shape[1]) for s in outs],
        out_shape=outs,
        compiler_params=params(),
        cost_estimate=cost(12 * rows * width * units, nbytes(h2, grad, w_gu, w_down, *outs)),
        name="ffn",
    )(h2, grad, w_gu, w_down)


def weight_grad_body(left, right, out):
    out[...] = dot_tn(left[...], right[...])


def weight_grad(left, right):
    rows, high = left.shape
    wide = right.shape[1]
    tile = next(t for t in (768, 640, 512, 384, 256, 128) if wide % t == 0)
    return pl.pallas_call(
        weight_grad_body,
        grid=(wide // tile,),
        in_specs=[resident(left), pl.BlockSpec((rows, tile), lambda i: (0, i))],
        out_specs=pl.BlockSpec((high, tile), lambda i: (0, i)),
        out_shape=shape((high, wide), F32),
        compiler_params=params(),
        cost_estimate=cost(2 * rows * high * wide, nbytes(left, right) + 4 * high * wide),
        name="weight_grad",
    )(left, right)


def mixer_backward_body(slot, own, base, grl, x, p_b, p_c, p_x, conv, next_grl, next_c, gain_one, taps,
                        w_b, w_c, w_x, w_out, g_in, g_proj, g_conv, g_norm, carry):
    step = pl.program_id(0)
    steps = pl.num_programs(0)
    rows = x.shape[0]

    @pl.when(step == 0)
    def _():
        after = dot_nt(next_grl[...], w_out[...]) * next_c[...].astype(F32)
        carry[...] = after[0:8]
        g_conv[...] = jnp.zeros_like(g_conv)
        g_norm[...] = jnp.zeros_like(g_norm)

    d_gated = dot_nt(grl[...], w_out[...])
    d_conv = d_gated * p_c[...].astype(F32)
    g_c = (d_gated * conv[...].astype(F32)).astype(BF16)
    fresh = lax.rem(base[0] + (steps - step) * rows, slot) == 0
    first = jnp.where(fresh, 0.0, carry[...])
    row = lax.broadcasted_iota(jnp.int32, d_conv.shape, 0)
    one = jnp.where(row == rows - 1, first[0:1], pltpu.roll(d_conv, rows - 1, 0))
    two = jnp.where(row == rows - 2, first[0:1],
                    jnp.where(row == rows - 1, first[1:2], pltpu.roll(d_conv, rows - 2, 0)))
    carry[...] = d_conv[0:8]
    b = p_b[...].astype(F32)
    xx = p_x[...].astype(F32)
    mixed = (b[:, :own] * xx[:, :own]).astype(BF16).astype(F32)
    g_conv[0:1] += jnp.sum(two[:, :own] * mixed, axis=0, keepdims=True)
    g_conv[1:2] += jnp.sum(one[:, :own] * mixed, axis=0, keepdims=True)
    g_conv[2:3] += jnp.sum(d_conv[:, :own] * mixed, axis=0, keepdims=True)
    d_mixed = taps[2:3] * d_conv + taps[1:2] * one + taps[0:1] * two
    g_b = (d_mixed * xx).astype(BF16)
    g_x = (d_mixed * b).astype(BF16)
    g_proj[...] = jnp.concatenate([g_b[:, :own], g_c[:, :own], g_x[:, :own]], axis=1)
    d_hidden = dot_nt(g_b, w_b[...]) + dot_nt(g_c, w_c[...]) + dot_nt(g_x, w_x[...])
    wide = x[...].astype(F32)
    scale = rms_scale(wide)
    normed = wide * scale
    g_norm[0:1] += jnp.sum(d_hidden * normed, axis=0, keepdims=True)
    d_normed = d_hidden * gain_one[...]
    g_in[...] = grl[...].astype(F32) + scale * (
        d_normed - normed * jnp.mean(d_normed * normed, axis=1, keepdims=True))


def mixer_backward(slot, own, base, grl, x, p_b, p_c, p_x, conv, next_grl, next_c, gain_one, taps,
                   w_b, w_c, w_x, w_out, tile=256):
    rows, width = x.shape
    chans = w_b.shape[1]
    steps = rows // tile
    row = lambda n: pl.BlockSpec((tile, n), lambda i, *_: (steps - 1 - i, 0))
    whole = lambda dims: pl.BlockSpec(dims, lambda i, *_: (0, 0))
    outs = [shape((rows, width), F32), shape((rows, 3 * own), BF16), shape((8, own), F32), shape((8, width), F32)]
    return pl.pallas_call(
        functools.partial(mixer_backward_body, slot, own),
        grid_spec=pltpu.PrefetchScalarGridSpec(
            num_scalar_prefetch=1,
            grid=(steps,),
            in_specs=[row(width), row(width)] + [row(chans)] * 4
            + [resident(a) for a in (next_grl, next_c, gain_one, taps, w_b, w_c, w_x, w_out)],
            out_specs=[row(width), row(3 * own), whole((8, own)), whole((8, width))],
            scratch_shapes=[pltpu.VMEM((8, chans), F32)],
        ),
        out_shape=outs,
        compiler_params=params(),
        cost_estimate=cost(8 * rows * width * chans, nbytes(grl, x, p_b, p_c, p_x, conv, w_b, w_c, w_x, w_out, *outs)),
        name="mixer_backward",
    )(base, grl, x, p_b, p_c, p_x, conv, next_grl, next_c, gain_one, taps, w_b, w_c, w_x, w_out)


def swap(value, step):
    count = lax.axis_size("tp")
    return lax.ppermute(value, "tp", [(i, i ^ step) for i in range(count)])


def shifted(value, steps):
    count = lax.axis_size("seq")
    return lax.ppermute(value, "seq", [(i, i + steps) for i in range(count) if 0 <= i + steps < count])


def others(value):
    count = lax.axis_size("tp")
    if count == 4:
        side = swap(value, 1)
        far = swap(value, 2)
        return [value, side, far, swap(side, 2)]
    every = lax.all_gather(value, "tp")
    me = lax.axis_index("tp")
    return [lax.dynamic_index_in_dim(every, me ^ j, 0, keepdims=False) for j in range(count)]


def scatter_sum(value):
    return lax.psum_scatter(value, "tp", scatter_dimension=0, tiled=True)


def gather(value):
    return lax.all_gather(value, "tp", axis=0, tiled=True)


def per_device(inputs, w_in, conv_w, w_out, norm_one, norm_two, w_gate, w_up, w_down, lengths, cotangent):
    rows, width = inputs.shape
    own = w_in.shape[2]
    units = w_gate.shape[1]
    slot = rows * lax.axis_size("seq") // SEQS
    tp = lax.axis_index("tp")
    quarter = rows // lax.axis_size("tp")
    start = lax.axis_index("seq") * rows
    base = start[None].astype(jnp.int32)

    w_in_all = others(jnp.concatenate([w_in[0], w_in[1], w_in[2]], axis=0))
    w_out_all = others(w_out)
    taps_all = others(jnp.concatenate([conv_w, jnp.zeros((13, own), BF16)], axis=0))
    w_b, w_c, w_x = (jnp.concatenate([w[i * width:(i + 1) * width] for w in w_in_all], axis=1) for i in range(3))
    w_o = jnp.concatenate(w_out_all, axis=0)
    taps = jnp.concatenate(taps_all, axis=1)[:8].astype(F32)
    gain_one = norm_one.astype(F32)[None, :]
    gain_two = norm_two.astype(F32)[None, :]

    place = start + jnp.arange(rows, dtype=jnp.int32)
    seq_of = place // slot
    limit = jnp.sum(jnp.where(seq_of[:, None] == jnp.arange(SEQS, dtype=jnp.int32)[None, :], lengths[None, :], 0), axis=1)
    real = (place - seq_of * slot < limit)[:, None]
    grad_low = jnp.where(real, cotangent, 0).astype(BF16)

    extra = -units % 128
    columns = lambda w: jnp.pad(w, ((0, 0), (0, extra)))
    w_gu = jnp.concatenate([columns(w_gate), columns(w_up)], axis=1)
    w_dn = jnp.pad(w_down, ((0, extra), (0, 0)))

    halo = shifted(inputs[rows - 16:], 1)
    h1, p_b, p_c, p_x, conv, gated, resid, h2 = mixer_forward(
        slot, base, inputs, halo, gain_one, gain_two, taps, w_b, w_c, w_x, w_o)
    next_c = shifted(p_c[:16], -1)

    out_part, back_part, activ, grads = ffn(h2, grad_low, w_gu, w_dn)
    d_hidden = scatter_sum(back_part).astype(F32)
    mine = lambda a: lax.dynamic_slice_in_dim(a, tp * quarter, quarter, 0)
    res = mine(resid)
    scale = rms_scale(res)
    normed = res * scale
    d_normed = d_hidden * gain_two
    g_norm_two = jnp.sum(d_hidden * normed, axis=0)
    g_res = mine(grad_low).astype(F32) + scale * (
        d_normed - normed * jnp.mean(d_normed * normed, axis=1, keepdims=True))
    grl = gather(g_res.astype(BF16))
    output = gather((res + scatter_sum(out_part).astype(F32)).astype(BF16))

    g_down = weight_grad(activ, grad_low)
    g_gu = weight_grad(h2, grads)

    next_grl = shifted(grl[:16], -1)
    grad_inputs, g_proj, g_conv, g_norm_one = mixer_backward(
        slot, own, base, grl, inputs, p_b, p_c, p_x, conv, next_grl, next_c, gain_one, taps, w_b, w_c, w_x, w_o)
    g_in = weight_grad(h1, g_proj)
    g_out = weight_grad(gated[:, :own], grl)

    big = lax.psum(tuple(a.astype(BF16) for a in (g_down, g_gu, g_in, g_out)), "seq")
    g_down, g_gu, g_in, g_out = (a.astype(F32) for a in big)
    g_conv, g_norm_one = lax.psum((g_conv[:3], g_norm_one[0]), "seq")
    g_norm_two = lax.psum(g_norm_two, ("seq", "tp"))
    padded = units + extra
    return (
        output,
        grad_inputs,
        jnp.stack([g_in[:, i * own:(i + 1) * own] for i in range(3)]),
        g_conv,
        g_out,
        g_norm_one,
        g_norm_two,
        g_gu[:, :units],
        g_gu[:, padded:padded + units],
        g_down[:units],
    )


def solution(mesh):
    tokens = P("seq", None)
    columns = P(None, "tp")
    lines = P("tp", None)
    stacked = P(None, None, "tp")
    return jax.shard_map(
        per_device,
        mesh=mesh,
        in_specs=(tokens, stacked, columns, lines, P(), P(), columns, columns, lines, P(), tokens),
        out_specs=(tokens, tokens, stacked, columns, lines, P(), P(), columns, columns, lines),
        check_vma=False,
    )
```

time: 1530 us -> 727 us (0.48)
  waiting for transfers between devices: 1170 us -> 369 us
  Pallas kernels: 0 us -> 191 us
  matrix products: 188 us -> 0 us
  other arithmetic: 82.9 us -> 52.7 us
  blocking collectives: 30 us -> 59 us
    psum x4 -> x1, waiting for transfers between devices: 1170 us -> 139 us  [per_device(): lax.psum(tuple((a.astype(BF16) for a in (g_down, g_gu, g_in, g_out))), 's...]
    pallas_call x0 -> x7, Pallas kernels: none -> 191 us  [the longest x1 55.9 us: ffn(): pl.pallas_call(ffn_body, grid=(rows // tile,), in_specs=[row(width), row(...]
    dot_general x21 -> x0, matrix products: 188 us -> none  [the longest x7 83.5 us: right_matmul(): lax.dot_general(left, right, (((1,), (1,)), ((), ())), preferred_element_...]
    reduce_scatter x0 -> x2, waiting for transfers between devices: none -> 138 us  [scatter_sum(): return lax.psum_scatter(value, 'tp', scatter_dimension=0, tiled=True)]
    ppermute x2 -> x12, waiting for transfers between devices: 0.53 us -> 71.3 us  [the longest x9 71.3 us: swap(): return lax.ppermute(value, 'tp', [(i, i ^ step) for i in range(count)])]
    psum x1 -> x2, blocking collectives: 30 us -> 59 us  [the longest x1 41.3 us: per_device(): g_norm_two = lax.psum(g_norm_two, ('seq', 'tp'))]
    add x2 -> x0, other arithmetic: 24.8 us -> none  [the longest x1 13 us: per_device(): grad_resid + scale_one * (d_normed_one - normed_one * jnp.mean(d_normed_o...]
    unnamed x123 -> x40, local copies, waits for them, and re-layouts: 32 us -> 7.58 us
  transfers between devices with their start and end apart: 6 -> 17, of which waited for: 5 -> 6; matrix products, arithmetic and copies ran while one was open for 7% -> 7% of each run, Pallas kernels for 0% -> 13%
where the time goes in v1:
time: 727 us; the launch traced here: 726 us
  waiting for transfers between devices  369 us (51%)
  Pallas kernels  191 us (26%)
  blocking collectives  59 us (8%)
  other arithmetic  52.7 us (7%)
  local copies, waits for them, and re-layouts  22.4 us (3%)
  starting transfers between devices  16.8 us (2%)
  between operations  14.1 us (2%)
    psum x1, waiting for transfers between devices, per_device(): lax.psum(tuple((a.astype(BF16) for a in (g_down, g_gu, g_in, g_out))), 's...  139 us
    reduce_scatter x2, waiting for transfers between devices, scatter_sum(): return lax.psum_scatter(value, 'tp', scatter_dimension=0, tiled=True)  138 us
    ppermute x9, waiting for transfers between devices, swap(): return lax.ppermute(value, 'tp', [(i, i ^ step) for i in range(count)])  71.3 us
    pallas_call x1, Pallas kernels, ffn(): pl.pallas_call(ffn_body, grid=(rows // tile,), in_specs=[row(width), row(...  55.9 us
    pallas_call x4, Pallas kernels, weight_grad(): pl.pallas_call(weight_grad_body, grid=(wide // tile,), in_specs=[resident...  51.8 us
    pallas_call x1, Pallas kernels, mixer_backward(): pl.pallas_call(functools.partial(mixer_backward_body, slot, own), grid_sp...  45.1 us
    psum x1, blocking collectives, per_device(): g_norm_two = lax.psum(g_norm_two, ('seq', 'tp'))  41.3 us
    pallas_call x1, Pallas kernels, mixer_forward(): pl.pallas_call(functools.partial(mixer_forward_body, slot), grid_spec=plt...  38.6 us
  transfers between devices with their start and end apart: 17, of which 6 were waited for; matrix products, arithmetic and copies ran while one was open for 7% of the time, Pallas kernels for 13%

profile of v1, /device:TPU:0, one launch (start us, length us, event | category | flops | bytes accessed | tf_op | source)
XLA Modules:
  0.0 725.6 jit_solution(6472056869331690217)
XLA Ops:
  10.0 2.9 collective-permute-start.4
  17.1 7.5 %broadcast_select_fusion.grad.right = bf16[3072,1024]{1,0:T(8,128)(2,1)} fusion(bf16[3072,1024]{1,0:T(8,128)(2,1)} %param.21, pred[3072]{0:T(1024)(128)(4,1)S(1)} %subtract_compare_fusion), kind=kLoop, calls=%fused_computation | loop fusion | flops 3145728 | bytes 12585984 | tf_op jit(solution)/shard_map/jit(_where)/select_n | solution.py:289
  26.2 32.8 %collective-permute-done.7 = bf16[256,1024]{1,0:T(8,128)(2,1)} collective-permute-done((bf16[256,1024]{1,0:T(8,128)(2,1)}, bf16[256,1024]{1,0:T(8,128)(2,1)}, u32[]{:S(2)}, u32[]{:S(2)}) %collective-permute-start.7) | collective-permute-done | bytes 524320 | tf_op jit(solution)/shard_map/ppermute | solution.py:239
  61.0 2.5 pad_maximum_fusion.w_gu
  68.4 38.4 %collective-permute-done.3 = bf16[16,256]{1,0:T(8,128)(2,1)S(1)} collective-permute-done((bf16[16,256]{1,0:T(8,128)(2,1)S(1)}, bf16[16,256]{1,0:T(8,128)(2,1)S(1)}, u32[]{:S(2)}, u32[]{:S(2)}) %collective-permute-start.3) | collective-permute-done | bytes 8224 | tf_op jit(solution)/shard_map/ppermute | solution.py:239
  110.0 2.1 fusion.13
  112.3 2.3 pad_maximum_fusion.2
  116.8 38.6 %mixer_forward.1 = (bf16[3072,1024]{1,0:T(8,128)(2,1)}, bf16[3072,1024]{1,0:T(8,128)(2,1)}, bf16[3072,1024]{1,0:T(8,128)(2,1)}, bf16[3072,1024]{1,0:T(8,128)(2,1...) custom-call(s32[1]{0:T(128)} %bitcast.base, ...), custom_call_target="tpu_custom_call" | custom-call | flops 25769803776 | bytes 71303168 | tf_op jit(solution)/shard_map/mixer_forward/pallas_call | solution.py:98
  155.4 55.9 %ffn.1 = (bf16[3072,1024]{1,0:T(8,128)(2,1)}, bf16[3072,1024]{1,0:T(8,128)(2,1)}, bf16[3072,1152]{1,0:T(8,128)(2,1)}, bf16[3072,2304]{1,0:T(8,128)(2,1)}) custom-call(bf16[3072,1024]{1,0:T(8,128)(2,1)} %get-tuple-element.27.h2.left, bf16[3072,1024]{1,0:T(8,128)(2,1)} %broadcast_select_fusion.grad.right, bf16[1024,2304]{1,0:T(8,128)(2,1)} %pad_maximum_fusion.w_gu, ...), custom_call_target="tpu_custom_call" | custom-call | flops 43486543872 | bytes 53477376 | tf_op jit(solution)/shard_map/ffn/pallas_call | solution.py:137
  212.3 2.2 multiply_reduce_fusion
  214.5 68.7 %reduce-scatter.5.cloned.1.call-done = bf16[768,1024]{1,0:T(8,128)(2,1)} async-done(((bf16[3072,1024]{1,0:T(8,128)(2,1)}), bf16[768,1024]{1,0:T(8,128)(2,1)}) %reduce-scatter.5.cloned.1.call-update) | async-done | bytes 1572880 | tf_op jit(solution)/shard_map/reduce_scatter | solution.py:259
  283.2 3.5 fusion.6
  286.7 69.7 %reduce-scatter.3.cloned.1.call-done = bf16[768,1024]{1,0:T(8,128)(2,1)} async-done(((bf16[3072,1024]{1,0:T(8,128)(2,1)}), bf16[768,1024]{1,0:T(8,128)(2,1)}) %reduce-scatter.3.cloned.1.call-update) | async-done | bytes 1572880 | tf_op jit(solution)/shard_map/reduce_scatter | solution.py:259
  356.4 5.6 fusion.5
  364.8 2.7 slice.92.left
  367.4 14.3 %weight_grad.7 = f32[1152,1024]{1,0:T(8,128)} custom-call(bf16[3072,1152]{1,0:T(8,128)(2,1)} %get-tuple-element.41.left, bf16[3072,1024]{1,0:T(8,128)(2,1)} %broadcast_select_fusion.grad.right), custom_call_target="tpu_custom_call" | custom-call | flops 7247757312 | bytes 18087936 | tf_op jit(solution)/shard_map/weight_grad/pallas_call | solution.py:157
  381.7 4.1 convert_element_type.61
  385.9 21.3 %weight_grad.6 = f32[1024,2304]{1,0:T(8,128)} custom-call(bf16[3072,1024]{1,0:T(8,128)(2,1)} %get-tuple-element.27.h2.left, bf16[3072,2304]{1,0:T(8,128)(2,1)} %get-tuple-element.40.right), custom_call_target="tpu_custom_call" | custom-call | flops 14495514624 | bytes 29884416 | tf_op jit(solution)/shard_map/weight_grad/pallas_call | solution.py:157
  407.2 6.3 convert_element_type.59
  413.5 18.8 %all-gather.5.cloned.1.call-done.grl.right = bf16[3072,1024]{1,0:T(8,128)(2,1)} async-done(((bf16[768,1024]{1,0:T(8,128)(2,1)}), bf16[3072,1024]{1,0:T(8,128)(2,1)}) %all-gather.5.cloned.1.call-update) | async-done | bytes 6291472 | tf_op jit(solution)/shard_map/all_gather | solution.py:263
  434.6 5.2 weight_grad.5
  439.8 2.2 convert_element_type.57
  442.7 45.1 %mixer_backward.1 = (f32[3072,1024]{1,0:T(8,128)}, bf16[3072,768]{1,0:T(8,128)(2,1)}, f32[8,256]{1,0:T(8,128)}, f32[8,1024]{1,0:T(8,128)}) custom-call(s32[1]{0:T(128)} %bitcast.base, bf16[3072,1024]{1,0:T(8,128)(2,1)} %all-gather.5.cloned.1.call-done.grl.right, bf16[3072,1024]{1,0:T(8,128)(2,1)} %x.5, bf16[3072,1024]{1,0:T(8,128)(2,1)} %get-tuple-element.30.p_b, ...), custom_call_target="tpu_custom_call" | custom-call | flops 25769803776 | bytes 63479808 | tf_op jit(solution)/shard_map/mixer_backward/pallas_call | solution.py:220
  487.8 11.0 %weight_grad.4 = f32[1024,768]{1,0:T(8,128)} custom-call(bf16[3072,1024]{1,0:T(8,128)(2,1)} %get-tuple-element.35.left, bf16[3072,768]{1,0:T(8,128)(2,1)} %get-tuple-element.36.right), custom_call_target="tpu_custom_call" | custom-call | flops 4831838208 | bytes 14155776 | tf_op jit(solution)/shard_map/weight_grad/pallas_call | solution.py:157
  498.7 3.2 convert_element_type.55
  501.9 41.3 %psum.53 = f32[1024]{0:T(1024)} all-reduce(f32[1024]{0:T(1024)S(1)} %get-tuple-element.42), channel_id=1, replica_groups=mesh['seq'=8,'tp'=4] {'seq','tp'}, use_global_device_ids=true, to_apply=%region_10.11 | all-reduce | flops 1024 | bytes 8192 | tf_op jit(solution)/shard_map/psum | solution.py:326
  544.1 17.7 %all-reduce.1 = (f32[3,256]{1,0:T(4,128)}, f32[1024]{0:T(1024)}) all-reduce(f32[3,256]{1,0:T(4,128)S(1)} %slice.91, f32[1024]{0:T(1024)S(1)} %bitcast.21), channel_id=1, replica_groups=mesh['seq'=8,'tp'=4] {'seq'}, use_global_device_ids=true, to_apply=%region_6.7 | all-reduce | flops 1792 | bytes 14336 | tf_op jit(solution)/shard_map/psum | solution.py:325
  561.7 139.3 %all-reduce.5.cloned.1.call-done = (bf16[1024,768]{1,0:T(8,128)(2,1)}, bf16[256,1024]{1,0:T(8,128)(2,1)}, bf16[1024,2304]{1,0:T(8,128)(2,1)}, bf16[1152,1024]{1,0:T(8,128)(2,1)}) async-done(((bf16[1024,768]{1,0:T(8,128)(2,1)}, bf16[256,1024]{1,0:T(8,128)(2,1)}, bf16[1024,2304]{1,0:T(8,128)(2,1)}, bf16[1152,1024]{1,0:T(8,128)(2,1)}), (bf16[1024,768]{1,0:T(8,128)(2,1)}, bf16[256,1024]{1,0:T(8,128)(2,1)}, ...) | async-done | bytes 9175056 | tf_op jit(solution)/shard_map/psum | solution.py:323
  701.1 2.1 convert_element_type.58
  706.7 2.7 convert_element_type.62
  709.4 5.1 fusion.11
  716.4 2.7 copy.29
  (96 shorter events, 33.5 us)
Async XLA Ops:
  7.2 5.7 copy-start.9
  7.2 9.8 %copy-start.10 = (s32[6]{0:T(128)S(1)}, s32[6]{0:T(128)}, u32[]{:S(2)}) copy-start(s32[6]{0:T(128)} %param.20) | copy-start | bytes 76
  7.2 276.0 %reduce-scatter.5.cloned.1.call-start = ((), (), s32[]{:S(2)}) async-start(), calls=%async_computation.4 | async-start | bytes 7864320 | tf_op jit(solution)/shard_map/reduce_scatter | solution.py:259
  10.0 50.8 %collective-permute-start.4 = (bf16[3072,256]{1,0:T(8,128)(2,1)}, bf16[3072,256]{1,0:T(8,128)(2,1)S(1)}, u32[]{:S(2)}, u32[]{:S(2)}) collective-permute-start(bf16[3072,256]{1,0:T(8,128)(2,1)} %pad_maximum_fusion.5), channel_id=1, source_target_pairs={{0,1},{1,0},{2,3},{3,2},{4,5},{5,4},{6,7},{7,6},{8,9},{9,8},{10,11... | collective-permute-start | bytes 4718600 | tf_op jit(solution)/shard_map/ppermute | solution.py:239
  12.9 11.7 %collective-permute-start.2 = (bf16[16,256]{1,0:T(8,128)(2,1)S(1)}, bf16[16,256]{1,0:T(8,128)(2,1)S(1)}, u32[]{:S(2)}, u32[]{:S(2)}) collective-permute-start(bf16[16,256]{1,0:T(8,128)(2,1)S(1)} %concatenate.24), channel_id=1, source_target_pairs={{0,2},{1,3},{2,0},{3,1},{4,6},{5,7},{6,4},{7,5},{8,10},{9,11},{10,... | collective-permute-start | bytes 24584 | tf_op jit(solution)/shard_map/ppermute | solution.py:239
  14.4 49.1 %collective-permute-start.1 = (bf16[16,256]{1,0:T(8,128)(2,1)S(1)}, bf16[16,256]{1,0:T(8,128)(2,1)S(1)}, u32[]{:S(2)}, u32[]{:S(2)}) collective-permute-start(bf16[16,256]{1,0:T(8,128)(2,1)S(1)} %concatenate.24), channel_id=1, source_target_pairs={{0,1},{1,0},{2,3},{3,2},{4,5},{5,4},{6,7},{7,6},{8,9},{9,8},{10,11... | collective-permute-start | bytes 24584 | tf_op jit(solution)/shard_map/ppermute | solution.py:239
  15.0 95.1 %collective-permute-start.5 = (bf16[3072,256]{1,0:T(8,128)(2,1)}, bf16[3072,256]{1,0:T(8,128)(2,1)}, u32[]{:S(2)}, u32[]{:S(2)}) collective-permute-start(bf16[3072,256]{1,0:T(8,128)(2,1)} %pad_maximum_fusion.5), channel_id=1, source_target_pairs={{0,2},{1,3},{2,0},{3,1},{4,6},{5,7},{6,4},{7,5},{8,10},{9,11},{10,... | collective-permute-start | bytes 4718600 | tf_op jit(solution)/shard_map/ppermute | solution.py:239
  15.0 44.0 %collective-permute-start.7 = (bf16[256,1024]{1,0:T(8,128)(2,1)}, bf16[256,1024]{1,0:T(8,128)(2,1)}, u32[]{:S(2)}, u32[]{:S(2)}) collective-permute-start(bf16[256,1024]{1,0:T(8,128)(2,1)} %param.14), channel_id=1, source_target_pairs={{0,1},{1,0},{2,3},{3,2},{4,5},{5,4},{6,7},{7,6},{8,9},{9,8},{10,11... | collective-permute-start | bytes 1572872 | tf_op jit(solution)/shard_map/ppermute | solution.py:239
  17.1 43.9 %copy-start.2 = (bf16[1024,1152]{1,0:T(8,128)(2,1)S(1)}, bf16[1024,1152]{1,0:T(8,128)(2,1)}, u32[]{:S(2)}) copy-start(bf16[1024,1152]{1,0:T(8,128)(2,1)} %param.18) | copy-start | bytes 7077892
  17.1 43.9 %copy-start.3 = (bf16[1024,1152]{1,0:T(8,128)(2,1)S(1)}, bf16[1024,1152]{1,0:T(8,128)(2,1)}, u32[]{:S(2)}) copy-start(bf16[1024,1152]{1,0:T(8,128)(2,1)} %param.17) | copy-start | bytes 7077892
  24.6 41.8 %copy-start.6 = (bf16[1024]{0:T(1024)(128)(2,1)S(1)}, bf16[1024]{0:T(1024)(128)(2,1)}, u32[]{:S(2)}) copy-start(bf16[1024]{0:T(1024)(128)(2,1)} %param.16) | copy-start | bytes 6148
  24.6 42.4 %copy-start.7 = (bf16[1024]{0:T(1024)(128)(2,1)S(1)}, bf16[1024]{0:T(1024)(128)(2,1)}, u32[]{:S(2)}) copy-start(bf16[1024]{0:T(1024)(128)(2,1)} %param.15) | copy-start | bytes 6148
  24.6 85.2 %collective-permute-start.8 = (bf16[256,1024]{1,0:T(8,128)(2,1)}, bf16[256,1024]{1,0:T(8,128)(2,1)S(1)}, u32[]{:S(2)}, u32[]{:S(2)}) collective-permute-start(bf16[256,1024]{1,0:T(8,128)(2,1)} %param.14), channel_id=1, source_target_pairs={{0,2},{1,3},{2,0},{3,1},{4,6},{5,7},{6,4},{7,5},{8,10},{9,11},{10,... | collective-permute-start | bytes 1572872 | tf_op jit(solution)/shard_map/ppermute | solution.py:239
  59.0 50.8 %collective-permute-start.9 = (bf16[256,1024]{1,0:T(8,128)(2,1)}, bf16[256,1024]{1,0:T(8,128)(2,1)S(1)}, u32[]{:S(2)}, u32[]{:S(2)}) collective-permute-start(bf16[256,1024]{1,0:T(8,128)(2,1)} %collective-permute-done.7), channel_id=1, source_target_pairs={{0,2},{1,3},{2,0},{3,1},{4,6},{5,7},{6,4},{7,5},{8,10},{9,11},{10,... | collective-permute-start | bytes 1572872 | tf_op jit(solution)/shard_map/ppermute | solution.py:239
  60.8 51.4 %collective-permute-start.6 = (bf16[3072,256]{1,0:T(8,128)(2,1)S(1)}, bf16[3072,256]{1,0:T(8,128)(2,1)S(1)}, u32[]{:S(2)}, u32[]{:S(2)}) collective-permute-start(bf16[3072,256]{1,0:T(8,128)(2,1)S(1)} %collective-permute-done.4), channel_id=1, source_target_pairs={{0,2},{1,3},{2,0},{3,1},{4,6},{5,7},{6,4},{7,5},{8,10},{9,11},{10,... | collective-permute-start | bytes 4718600 | tf_op jit(solution)/shard_map/ppermute | solution.py:239
  63.6 43.3 %collective-permute-start.3 = (bf16[16,256]{1,0:T(8,128)(2,1)S(1)}, bf16[16,256]{1,0:T(8,128)(2,1)S(1)}, u32[]{:S(2)}, u32[]{:S(2)}) collective-permute-start(bf16[16,256]{1,0:T(8,128)(2,1)S(1)} %collective-permute-done.1), channel_id=1, source_target_pairs={{0,2},{1,3},{2,0},{3,1},{4,6},{5,7},{6,4},{7,5},{8,10},{9,11},{10,... | collective-permute-start | bytes 24584 | tf_op jit(solution)/shard_map/ppermute | solution.py:239
  106.8 9.4 %collective-permute-start = (bf16[16,1024]{1,0:T(8,128)(2,1)S(1)}, bf16[16,1024]{1,0:T(8,128)(2,1)S(1)}, u32[]{:S(2)}, u32[]{:S(2)}) collective-permute-start(bf16[16,1024]{1,0:T(8,128)(2,1)S(1)} %slice.72), channel_id=1, source_target_pairs={{0,4},{4,8},{8,12},{12,16},{16,20},{20,24},{24,28},{1,5},{5,9},{9,... | collective-permute-start | bytes 98312 | tf_op jit(solution)/shard_map/ppermute | solution.py:244
  109.9 2.2 copy-start.4
  211.3 145.1 %reduce-scatter.3.cloned.1.call-start = ((), (), s32[]{:S(2)}) async-start(), calls=%async_computation.2 | async-start | bytes 7864320 | tf_op jit(solution)/shard_map/reduce_scatter | solution.py:259
  212.1 71.2 %copy-start.5 = (f32[1024]{0:T(1024)S(1)}, f32[1024]{0:T(1024)}, u32[]{:S(2)}) copy-start(f32[1024]{0:T(1024)} %convert_element_type.48) | copy-start | bytes 12292
  212.1 220.3 %all-gather.5.cloned.1.call-start = ((), (), s32[]{:S(2)}) async-start(), calls=%async_computation.5 | async-start | bytes 7864320 | tf_op jit(solution)/shard_map/all_gather | solution.py:263
  283.2 73.2 %copy-start = (bf16[768,1024]{1,0:T(8,128)(2,1)S(1)}, bf16[768,1024]{1,0:T(8,128)(2,1)}, u32[]{:S(2)}) copy-start(bf16[768,1024]{1,0:T(8,128)(2,1)} %reduce-scatter.5.cloned.1.call-done) | copy-start | bytes 4718596
  362.1 181.2 %all-gather.3.cloned.1.call-start = ((), (), s32[]{:S(2)}) async-start(), calls=%async_computation.3 | async-start | bytes 7864320 | tf_op jit(solution)/shard_map/all_gather | solution.py:263
  362.7 338.4 %all-reduce.5.cloned.1.call-start = ((), (), s32[]{:S(2)}) async-start(), calls=%async_computation.6 | async-start | bytes 18350080 | tf_op jit(solution)/shard_map/psum | solution.py:323
  363.5 78.6 %collective-permute-start.11 = (bf16[16,1024]{1,0:T(8,128)(2,1)S(1)}, bf16[16,1024]{1,0:T(8,128)(2,1)S(1)}, u32[]{:S(2)}, u32[]{:S(2)}) collective-permute-start(bf16[16,1024]{1,0:T(8,128)(2,1)S(1)} %slice.87), channel_id=1, source_target_pairs={{4,0},{8,4},{12,8},{16,12},{20,16},{24,20},{28,24},{5,1},{9,5},{13... | collective-permute-start | bytes 98312 | tf_op jit(solution)/shard_map/ppermute | solution.py:244
  433.1 8.9 %collective-permute-start.10 = (bf16[16,1024]{1,0:T(8,128)(2,1)S(1)}, bf16[16,1024]{1,0:T(8,128)(2,1)S(1)}, u32[]{:S(2)}, u32[]{:S(2)}) collective-permute-start(bf16[16,1024]{1,0:T(8,128)(2,1)S(1)} %slice.105), channel_id=1, source_target_pairs={{4,0},{8,4},{12,8},{16,12},{20,16},{24,20},{28,24},{5,1},{9,5},{13... | collective-permute-start | bytes 98312 | tf_op jit(solution)/shard_map/ppermute | solution.py:244
  501.9 41.4 %copy-start.8 = (f32[8,256]{1,0:T(8,128)S(1)}, f32[8,256]{1,0:T(8,128)}, u32[]{:S(2)}) copy-start(f32[8,256]{1,0:T(8,128)} %get-tuple-element.37) | copy-start | bytes 24580
  703.2 6.2 slice-start
  705.0 1.7 copy-start.1
  705.0 4.4 slice-start.1
  709.4 7.0 slice-start.2
  709.4 7.0 slice-start.3
  (3 other events, 1.8 us)
Sparse Core Ops, SparseCore 0:
  211.5 71.7 reduce-scatter.4
  286.2 70.1 reduce-scatter.2
  362.2 70.1 all-gather.4
  434.1 70.1 all-gather.2
  507.9 193.1 all-reduce.4

commit v2 on v1

v2 whole, which is shorter than its diff:
```python
import functools

import jax
import jax.numpy as jnp
from jax import lax
from jax.experimental import pallas as pl
from jax.experimental.pallas import tpu as pltpu
from jax.sharding import PartitionSpec as P

SEQS = 6
F32 = jnp.float32
BF16 = jnp.bfloat16
VMEM_LIMIT = 56 * 2**20
TILE = 256
CHUNKS = 3


def params():
    return pltpu.CompilerParams(vmem_limit_bytes=VMEM_LIMIT)


def cost(flops, moved):
    return pl.CostEstimate(flops=int(flops), bytes_accessed=int(moved), transcendentals=0)


def nbytes(*arrays):
    return sum(a.size * a.dtype.itemsize for a in arrays)


def shape(dims, dtype):
    return jax.ShapeDtypeStruct(dims, dtype)


def dot(left, right):
    return jnp.dot(left, right, preferred_element_type=F32)


def dot_nt(left, right):
    return lax.dot_general(left, right, (((1,), (1,)), ((), ())), preferred_element_type=F32)


def dot_tn(left, right):
    return lax.dot_general(left, right, (((0,), (0,)), ((), ())), preferred_element_type=F32)


def rms_scale(values):
    return lax.rsqrt(jnp.mean(values * values, axis=1, keepdims=True) + 1e-05)


def resident(array):
    zeros = (0,) * array.ndim
    return pl.BlockSpec(array.shape, lambda i, *_: zeros, pipeline_mode=pl.Buffered(1))


HALF = 128


def pack_half(w_in, conv_w, w_out):
    width = w_in.shape[1]
    out = w_out.reshape(HALF, width // HALF, HALF).transpose(1, 0, 2).reshape(width, HALF)
    taps = jnp.concatenate([conv_w, jnp.zeros((13, HALF), BF16)], axis=0)
    return jnp.concatenate([w_in.reshape(3 * width, HALF), out, taps], axis=0)


def group_arrays(group):
    kind, arrays = group
    return list(arrays) if kind == "whole" else [a for half in arrays for a in half]


def channels_of(group):
    kind, arrays = group
    return arrays[1].shape[0] if kind == "whole" else 2 * HALF


def copies(layout, refs, core, w_all, w_out, taps):
    width = w_all.shape[0]
    chans = w_out.shape[0]
    pairs, at, refs = [], 0, list(refs)
    for kind, size, arrays in layout:
        if kind == "whole":
            w_in, w_o, tap = (refs.pop(0) for _ in range(3))
            for i in range(3):
                pairs.append((w_in.at[i], w_all.at[:, pl.ds(i * chans + at, size)]))
            pairs.append((w_o, w_out.at[pl.ds(at, size), :]))
            pairs.append((tap, taps.at[:, pl.ds(at, size)]))
        else:
            for which, count in enumerate(arrays):
                parts = [refs.pop(0) for _ in range(count)]
                core_of = core if which == 0 else 1 - core
                place = at + core_of * HALF

                def rows(first, length):
                    if len(parts) == 1 or first < 2 * width:
                        return parts[0].at[pl.ds(first, length), :]
                    return parts[1].at[pl.ds(first - 2 * width, length), :]

                for i in range(3):
                    spot = pl.multiple_of(i * chans + place, HALF)
                    pairs.append((rows(i * width, width), w_all.at[:, pl.ds(spot, HALF)]))
                spot = pl.multiple_of(place, HALF)
                for j in range(width // HALF):
                    pairs.append((rows(3 * width + j * HALF, HALF), w_out.at[pl.ds(spot, HALF), pl.ds(j * HALF, HALF)]))
                pairs.append((rows(4 * width, 16), taps.at[:, pl.ds(spot, HALF)]))
        at += size
    return pairs


def layout_of(groups):
    return [(kind, channels_of((kind, arrays)), None if kind == "whole" else [len(h) for h in arrays])
            for kind, arrays in groups]


def copy_count(layout, width):
    per_half = 4 + width // HALF
    return sum(5 if kind == "whole" else 2 * per_half for kind, _, _ in layout)


def bring(pairs, sems):
    handles = [pltpu.make_async_copy(a, b, sems.at[k]) for k, (a, b) in enumerate(pairs)]
    for h in handles:
        h.start()
    for h in handles:
        h.wait()


def weight_scratch(width, chans, layout):
    return [
        pltpu.VMEM((width, 3 * chans), BF16),
        pltpu.VMEM((chans, width), BF16),
        pltpu.VMEM((16, chans), BF16),
        pltpu.SemaphoreType.DMA((copy_count(layout, width),)),
    ]


def layer_body(slot, own, layout, chunk_start, split, counts, info, lens, *refs):
    refs = list(refs)
    x, cot, halo, gain_one, gain_two = (refs.pop(0) for _ in range(5))
    weights = [refs.pop(0) for _ in range(counts[0])]
    w_gate, w_up, w_down = (refs.pop(0) for _ in range(3))
    del refs[:counts[1]]
    proj, gated, h1, h2, grad, activ, grads, resid = (refs.pop(0) for _ in range(8))
    forward = [refs.pop(0) for _ in range(4 if split else 1)]
    backward = [refs.pop(0) for _ in range(4 if split else 1)]
    w_all, w_out, taps, sems, w_gu, w_dn, more, carry = refs
    step = pl.program_id(0)
    rows, width = x.shape
    chans = w_out.shape[0]
    units = w_dn.shape[0]
    place = info[0] + chunk_start + step * rows

    def late():
        pairs = [(w_gate, w_gu.at[:, pl.ds(0, units)]), (w_up, w_gu.at[:, pl.ds(units, units)]), (w_down, w_dn)]
        return [pltpu.make_async_copy(a, b, more.at[k]) for k, (a, b) in enumerate(pairs)]

    def hidden(wide):
        return ((wide * rms_scale(wide)) * gain_one[...]).astype(BF16)

    @pl.when(step == 0)
    def _():
        early = [pltpu.make_async_copy(a, b, sems.at[k])
                 for k, (a, b) in enumerate(copies(layout, weights, info[1], w_all, w_out, taps))]
        for h in early:
            h.start()
        for h in late():
            h.start()
        for h in early:
            h.wait()
        for h in late():
            h.wait()
        before = dot(hidden(halo[...].astype(F32)), w_all[...])
        mixed = (before[:, :chans] * before[:, 2 * chans:]).astype(BF16).astype(F32)
        carry[...] = mixed[8:16]

    wide = x[...].astype(F32)
    low = hidden(wide)
    h1[...] = low
    every = dot(low, w_all[...])
    b, c, xx = (every[:, i * chans:(i + 1) * chans] for i in range(3))
    mixed = (b * xx).astype(BF16).astype(F32)
    before = jnp.where(lax.rem(place, slot) == 0, 0.0, carry[...])
    row = lax.broadcasted_iota(jnp.int32, mixed.shape, 0)
    one = jnp.where(row == 0, before[7:8], pltpu.roll(mixed, 1, 0))
    two = jnp.where(row == 0, before[6:7], jnp.where(row == 1, before[7:8], pltpu.roll(mixed, 2, 0)))
    carry[...] = mixed[rows - 8:]
    tap = taps[...].astype(F32)
    conved = tap[2:3] * mixed + tap[1:2] * one + tap[0:1] * two
    gate = (c * conved).astype(BF16)
    for i, part in enumerate((b, c, xx, conved)):
        proj[:, i * chans:(i + 1) * chans] = part.astype(BF16)
    gated[...] = gate[:, :own]
    res = wide + dot(gate, w_out[...])
    post = ((res * rms_scale(res)) * gain_two[...]).astype(BF16)
    h2[...] = post
    limit = lens[lax.div(place, slot)] - lax.rem(place, slot)
    line = lax.broadcasted_iota(jnp.int32, (rows, width), 0)
    low_grad = jnp.where(line < limit, cot[...].astype(F32), 0.0).astype(BF16)
    grad[...] = low_grad

    both = dot(post, w_gu[...])
    d_activ = dot_nt(low_grad, w_dn[...])
    pre = both[:, :units]
    up = both[:, units:]
    sig = 1.0 / (1.0 + jnp.exp(-pre))
    silu = pre * sig
    act = (silu * up).astype(BF16)
    g_gate = (d_activ * up * sig * (1.0 + pre * (1.0 - sig))).astype(BF16)
    g_up = (d_activ * silu).astype(BF16)
    activ[...] = act
    grads[:, :units] = g_gate
    grads[:, units:] = g_up
    back = dot_nt(grads[...], w_gu[...]).astype(BF16)
    out = dot(act, w_dn[...]).astype(BF16)
    if not split:
        forward[0][...] = out
        resid[...] = res
        backward[0][...] = back
        return
    far = lax.bitwise_xor(step, info[2])
    for j in range(4):
        @pl.when(far == j)
        def _():
            backward[j][...] = back
            forward[j][...] = out
            if j == 0:
                resid[...] = res


def layer(chunk, chunks, slot, own, info, lens, x, cot, halo, gain_one, gain_two, groups, w_gate, w_up, w_down, kept, after, tile, split):
    rows, width = x.shape
    layout = layout_of(groups)
    chans = sum(size for _, size, _ in layout)
    units = w_down.shape[0]
    weights = [a for g in groups for a in group_arrays(g)]
    steps = rows // chunks // tile
    row = lambda n: pl.BlockSpec((tile, n), lambda i, *_: (chunk * steps + i, 0))
    once = lambda n, at: pl.BlockSpec((tile, n), lambda i, *_: (at, 0))
    anywhere = pl.BlockSpec(memory_space=pl.ANY)
    outs = [shape((rows, 4 * chans), BF16), shape((rows, own), BF16), shape((rows, width), BF16),
            shape((rows, width), BF16), shape((rows, width), BF16), shape((rows, units), BF16), shape((rows, 2 * units), BF16)]
    specs = [row(s.shape[1]) for s in outs]
    part = pl.BlockSpec((tile, width), lambda i, *_: (i, 0))
    sums = shape((rows // chunks, width), BF16)
    if split:
        outs += [shape((chunks * tile, width), F32)] + [shape((chunks * tile, width), BF16)] * 4
        outs += [shape((tile, width), BF16)] * 4
        specs += [once(width, chunk)] * 5 + [once(width, 0)] * 4
    else:
        outs += [shape((rows, width), F32), sums, sums]
        specs += [row(width), part, part]
    ins = [x, cot, halo, gain_one, gain_two, *weights, w_gate, w_up, w_down, *kept, *after]
    result = pl.pallas_call(
        functools.partial(layer_body, slot, own, layout, chunk * steps * tile, split, (len(weights), len(kept) + len(after))),
        grid_spec=pltpu.PrefetchScalarGridSpec(
            num_scalar_prefetch=2,
            grid=(steps,),
            in_specs=[row(width), row(width)] + [resident(a) for a in (halo, gain_one, gain_two)]
            + [anywhere] * (len(weights) + 3 + len(kept) + len(after)),
            out_specs=specs,
            scratch_shapes=weight_scratch(width, chans, layout) + [
                pltpu.VMEM((width, 2 * units), BF16), pltpu.VMEM((units, width), BF16),
                pltpu.SemaphoreType.DMA((3,)), pltpu.VMEM((8, chans), F32)],
        ),
        out_shape=outs,
        input_output_aliases={2 + len(ins) - len(kept) - len(after) + k: k for k in range(len(kept))},
        compiler_params=params(),
        cost_estimate=cost(steps * tile * width * (8 * chans + 12 * units),
                           nbytes(x, cot, *outs[:7]) // chunks + nbytes(*weights, w_gate, w_up, w_down)),
        name="layer",
    )(info, lens, *ins)
    shared = 12 if split else 8
    return result[:shared], result[shared:]


def second_norm_body(info, d_own, d_side, d_far, d_corner, resid, grad, gain, out, g_norm):
    d_hidden = (d_own[...].astype(F32) + d_side[...].astype(F32)) + (d_far[...].astype(F32) + d_corner[...].astype(F32))
    res = resid[...]
    scale = rms_scale(res)
    normed = res * scale
    g_norm[...] = jnp.sum(d_hidden * normed, axis=0, keepdims=True)
    d_normed = d_hidden * gain[...]
    out[...] = (grad[...].astype(F32) + scale * (
        d_normed - normed * jnp.mean(d_normed * normed, axis=1, keepdims=True))).astype(BF16)


def second_norm(chunk, info, pieces, resid, grad, gain):
    block, width = pieces[0].shape
    same = pl.BlockSpec((block, width), lambda i, *_: (0, 0))
    return pl.pallas_call(
        second_norm_body,
        grid_spec=pltpu.PrefetchScalarGridSpec(
            num_scalar_prefetch=1,
            grid=(1,),
            in_specs=[same, same, same, same,
                      pl.BlockSpec((block, width), lambda i, info: (chunk, 0)),
                      pl.BlockSpec((block, width), lambda i, info: (4 * chunk + info[2], 0)),
                      resident(gain)],
            out_specs=[same, pl.BlockSpec((1, width), lambda i, *_: (0, 0))],
        ),
        out_shape=[shape((block, width), BF16), shape((1, width), F32)],
        compiler_params=params(),
        cost_estimate=cost(0, 14 * block * width),
        name="second_norm",
    )(info, *pieces, resid, grad, gain)


def place_body(info, own, side, far, left, right, *refs):
    target = refs[-1]
    j = pl.program_id(0) % 4
    for k, source in enumerate((own, side, far)):
        @pl.when(j == k)
        def _():
            target[...] = source[...]

    @pl.when(j == 3)
    def _():
        target[:, :left.shape[1]] = left[...]
        target[:, left.shape[1]:] = right[...]


def place(first, chunks, info, pieces, rows, into, corner=0):
    width = pieces[0].shape[1]
    block = pieces[0].shape[0] // chunks
    kept = [] if into is None else [into]
    at = [0, 0, 0, corner, corner]
    return pl.pallas_call(
        place_body,
        grid_spec=pltpu.PrefetchScalarGridSpec(
            num_scalar_prefetch=1,
            grid=(4 * chunks,),
            in_specs=[pl.BlockSpec((block, p.shape[1]), lambda i, *_, k=k: (k + i // 4, 0)) for p, k in zip(pieces, at)]
            + [pl.BlockSpec(memory_space=pl.ANY)] * len(kept),
            out_specs=pl.BlockSpec((block, width), lambda i, info: (4 * (first + i // 4) + lax.bitwise_xor(i % 4, info[2]), 0)),
        ),
        out_shape=shape((rows, width), BF16),
        input_output_aliases={6: 0} if kept else {},
        compiler_params=params(),
        cost_estimate=cost(0, 2 * nbytes(*pieces)),
        name="place",
    )(info, *pieces, *kept)


def weight_grad_body(left, right, *refs):
    out = refs[-1]
    out[...] = dot_tn(left[...], right[...]).astype(out.dtype)


def weight_grad(left, right, after=(), first=0, wide=None, dtype=F32):
    rows, high = left.shape
    wide = wide or right.shape[1]
    tile = next(t for t in (768, 640, 512, 384, 256, 128) if wide % t == 0)
    return pl.pallas_call(
        weight_grad_body,
        grid=(wide // tile,),
        in_specs=[resident(left), pl.BlockSpec((rows, tile), lambda i: (0, first // tile + i))]
        + [pl.BlockSpec(memory_space=pl.ANY)] * len(after),
        out_specs=pl.BlockSpec((high, tile), lambda i: (0, i)),
        out_shape=shape((high, wide), dtype),
        compiler_params=params(),
        cost_estimate=cost(2 * rows * high * wide, nbytes(left) + 2 * rows * wide + 4 * high * wide),
        name="weight_grad",
    )(left, right, *after)


def conv_backward(slot, info, total, d_gated, c, conved, taps, carry):
    step = pl.program_id(0)
    rows = d_gated.shape[0]
    d_conv = d_gated * c[...].astype(F32)
    g_c = (d_gated * conved[...].astype(F32)).astype(BF16)
    fresh = lax.rem(info[0] + (total - step) * rows, slot) == 0
    after = jnp.where(fresh, 0.0, carry[...])
    row = lax.broadcasted_iota(jnp.int32, d_conv.shape, 0)
    one = jnp.where(row == rows - 1, after[0:1], pltpu.roll(d_conv, rows - 1, 0))
    two = jnp.where(row == rows - 2, after[0:1], jnp.where(row == rows - 1, after[1:2], pltpu.roll(d_conv, rows - 2, 0)))
    carry[...] = d_conv[0:8]
    tap = taps[...].astype(F32)
    return d_conv, one, two, g_c, tap[2:3] * d_conv + tap[1:2] * one + tap[0:1] * two


def own_backward_body(slot, info, grl, p_b, p_c, p_x, conved, next_grl, next_c, w_out, taps, *refs):
    g_proj, g_conv, carry = refs[-3:]

    @pl.when(pl.program_id(0) == 0)
    def _():
        carry[...] = (dot_nt(next_grl[...], w_out[...]) * next_c[...].astype(F32))[0:8]
        g_conv[...] = jnp.zeros_like(g_conv)

    own = w_out.shape[0]
    d_conv, one, two, g_c, d_mixed = conv_backward(slot, info, pl.num_programs(0), dot_nt(grl[...], w_out[...]), p_c, conved, taps, carry)
    b = p_b[...].astype(F32)
    xx = p_x[...].astype(F32)
    mixed = (b * xx).astype(BF16).astype(F32)
    g_proj[:, :own] = (d_mixed * xx).astype(BF16)
    g_proj[:, own:2 * own] = g_c
    g_proj[:, 2 * own:] = (d_mixed * b).astype(BF16)
    for k, values in enumerate((two, one, d_conv)):
        g_conv[k:k + 1] += jnp.sum(values * mixed, axis=0, keepdims=True)


def own_backward(slot, info, grl, proj, next_grl, next_c, w_out, taps, after=(), tile=512):
    rows, width = grl.shape
    own = w_out.shape[0]
    groups = proj.shape[1] // 4 // own
    steps = rows // tile
    row = lambda n, at=0: pl.BlockSpec((tile, n), lambda i, *_: (steps - 1 - i, at))
    outs = [shape((rows, 3 * own), BF16), shape((8, own), F32)]
    ins = [grl, proj, proj, proj, proj, next_grl, next_c, w_out, taps]
    return pl.pallas_call(
        functools.partial(own_backward_body, slot),
        grid_spec=pltpu.PrefetchScalarGridSpec(
            num_scalar_prefetch=1,
            grid=(steps,),
            in_specs=[row(width)] + [row(own, k * groups) for k in range(4)] + [resident(a) for a in ins[5:]]
            + [pl.BlockSpec(memory_space=pl.ANY)] * len(after),
            out_specs=[row(3 * own), pl.BlockSpec((8, own), lambda i, *_: (0, 0))],
            scratch_shapes=[pltpu.VMEM((8, own), F32)],
        ),
        out_shape=outs,
        compiler_params=params(),
        cost_estimate=cost(2 * rows * width * own, nbytes(grl, *outs) + nbytes(proj) // groups),
        name="own_backward",
    )(info, *ins, *after)


def mixer_backward_body(slot, layout, count, total, begun, info, grl, x, p_b, p_c, p_x, conved, next_grl, next_c, gain_one, *refs):
    weights = refs[:count]
    g_in, g_norm, rest, w_all, w_out, taps, sems, carry, held = refs[-9:]
    step = pl.program_id(0)
    chans = w_out.shape[0]

    @pl.when(step == 0)
    def _():
        bring(copies(layout, weights, info[1], w_all, w_out, taps), sems)
        if begun:
            carry[...] = refs[count][...]
        else:
            carry[...] = (dot_nt(next_grl[...], w_out[...]) * next_c[...].astype(F32))[0:8]
        g_norm[...] = jnp.zeros_like(g_norm)

    _, _, _, g_c, d_mixed = conv_backward(slot, info, total, dot_nt(grl[...], w_out[...]), p_c, conved, taps, carry)
    rest[...] = carry[...]
    held[:, :chans] = (d_mixed * p_x[...].astype(F32)).astype(BF16)
    held[:, chans:2 * chans] = g_c
    held[:, 2 * chans:] = (d_mixed * p_b[...].astype(F32)).astype(BF16)
    d_hidden = dot_nt(held[...], w_all[...])
    wide = x[...].astype(F32)
    scale = rms_scale(wide)
    normed = wide * scale
    g_norm[0:1] += jnp.sum(d_hidden * normed, axis=0, keepdims=True)
    d_normed = d_hidden * gain_one[...]
    g_in[...] = grl[...].astype(F32) + scale * (
        d_normed - normed * jnp.mean(d_normed * normed, axis=1, keepdims=True))


def mixer_backward(slot, info, grl, x, proj, next_grl, next_c, gain_one, groups, after=(), part=0, parts=1, kept=(), tile=512):
    rows, width = x.shape
    layout = layout_of(groups)
    chans = sum(size for _, size, _ in layout)
    weights = [a for g in groups for a in group_arrays(g)]
    steps = rows // tile // parts
    total = rows // tile - part * steps
    row = lambda n, at=0: pl.BlockSpec((tile, n), lambda i, *_: (total - 1 - i, at))
    outs = [shape((rows, width), F32), shape((8, width), F32), shape((8, chans), F32)]
    fixed = lambda n: pl.BlockSpec((8, n), lambda i, *_: (0, 0))
    ins = [grl, x, proj, proj, proj, proj, next_grl, next_c, gain_one, *weights, *kept]
    anywhere = pl.BlockSpec(memory_space=pl.ANY)
    return pl.pallas_call(
        functools.partial(mixer_backward_body, slot, layout, len(weights), total, bool(kept)),
        grid_spec=pltpu.PrefetchScalarGridSpec(
            num_scalar_prefetch=1,
            grid=(steps,),
            in_specs=[row(width), row(width)] + [row(chans, k) for k in range(4)]
            + [resident(a) for a in (next_grl, next_c, gain_one)] + [anywhere] * len(weights)
            + ([resident(kept[0]), anywhere] if kept else []) + [anywhere] * len(after),
            out_specs=[row(width), fixed(width), fixed(chans)],
            scratch_shapes=weight_scratch(width, chans, layout)
            + [pltpu.VMEM((8, chans), F32), pltpu.VMEM((tile, 3 * chans), BF16)],
        ),
        out_shape=outs,
        input_output_aliases={len(ins): 0} if kept else {},
        compiler_params=params(),
        cost_estimate=cost(8 * rows * width * chans // parts, nbytes(grl, x, proj, *outs) // parts + nbytes(*weights)),
        name="mixer_backward",
    )(info, *ins, *after)


def swap(value, step):
    count = lax.axis_size("tp")
    return lax.ppermute(value, "tp", [(i, i ^ step) for i in range(count)])


def swap_seq(value, step):
    count = lax.axis_size("seq")
    return lax.ppermute(value, "seq", [(i, i ^ step) for i in range(count)])


def shifted(value, steps):
    count = lax.axis_size("seq")
    return lax.ppermute(value, "seq", [(i, i + steps) for i in range(count) if 0 <= i + steps < count])


def weight_groups(w_in, conv_w, w_out, core, tp):
    own_taps = jnp.concatenate([conv_w, jnp.zeros((13, conv_w.shape[1]), BF16)], axis=0)
    own = ("whole", [w_in, w_out, own_taps])
    width = w_in.shape[1]
    if lax.axis_size("tp") == 4 and w_out.shape[0] == 2 * HALF:
        cut = lambda a, dim: lax.dynamic_slice_in_dim(a, core * HALF, HALF, dim)
        half = pack_half(cut(w_in, 2), cut(conv_w, 1), cut(w_out, 0))
        side, far = swap(half, 1), swap(half, 2)
        low, high = swap(side[:2 * width], 2), swap(far[2 * width:], 1)
        pairs = [("halves", [[side], [swap_seq(side, 1)]]), ("halves", [[far], [swap_seq(far, 1)]])]
        corner = ("halves", [[low, high], [swap_seq(low, 1), swap_seq(high, 1)]])
        return [own, *pairs, corner]
    every = [lax.all_gather(a, "tp") for a in own[1]]
    take = lambda a, j: lax.dynamic_index_in_dim(a, tp ^ j, 0, keepdims=False)
    return [own] + [("whole", [take(a, j) for a in every]) for j in range(1, lax.axis_size("tp"))]


def exchange(blocks):
    return [blocks[0]] + [swap(blocks[j], j) for j in (3, 1, 2)]


def to_sides(own):
    return [swap(own, 1), swap(own, 2)]


def corners(sides):
    half = sides[0][0].shape[1] // 2
    low = [far[:, :half] for _, far in sides]
    high = [side[:, half:] for side, _ in sides]
    join = lambda parts: parts[0] if len(parts) == 1 else jnp.concatenate(parts, axis=0)
    return [swap(join(low), 1), swap(join(high), 2)]


class SeqSum:
    def __init__(self, value):
        seq = lax.axis_index("seq")
        self.core = seq & 1
        line = seq >> 1
        self.keep = (line & 1) ^ (line >> 1)
        self.rows = value.shape[0]
        self.value = value

    def cut(self, array, which, count):
        size = self.rows // count
        return lax.dynamic_slice_in_dim(array, which * size, size, 0)

    def pair(self):
        self.sent = swap_seq(self.cut(self.value, 1 - self.core, 2).astype(BF16), 1)

    def near(self):
        self.value = self.cut(self.value, self.core, 2) + self.sent.astype(F32)
        self.sent = swap_seq(self.cut(self.value, 1 - self.keep, 4).astype(BF16), 2)

    def cross(self):
        self.value = (self.cut(self.value, self.keep, 4) + self.sent.astype(F32)).astype(BF16)
        self.sent = swap_seq(self.value, 6)

    def back(self):
        self.value = (self.value.astype(F32) + self.sent.astype(F32)).astype(BF16)
        self.sent = swap_seq(self.value, 2)

    def share(self):
        first = self.keep == 0
        self.value = jnp.concatenate([jnp.where(first, self.value, self.sent), jnp.where(first, self.sent, self.value)], axis=0)
        self.sent = swap_seq(self.value, 1)

    def result(self):
        first = self.core == 0
        return jnp.concatenate(
            [jnp.where(first, self.value, self.sent), jnp.where(first, self.sent, self.value)], axis=0).astype(F32)

    def state(self):
        return self.value, self.sent

    def put(self, state):
        self.value, self.sent = state


def seq_sum(value):
    return lax.psum(value.astype(BF16), "seq").astype(F32)


def small_sum(value):
    if lax.axis_size("seq") != 8:
        return lax.psum(value, "seq")
    for step in (1, 2, 6):
        value = value + swap_seq(value, step)
    return value


def per_device(inputs, w_in, conv_w, w_out, norm_one, norm_two, w_gate, w_up, w_down, lengths, cotangent):
    rows, width = inputs.shape
    own = w_in.shape[2]
    units = w_gate.shape[1]
    slot = rows * lax.axis_size("seq") // SEQS
    group = lax.axis_size("tp")
    tp = lax.axis_index("tp")
    seq = lax.axis_index("seq")
    core = seq & 1
    info = jnp.stack([seq * rows, core, tp]).astype(jnp.int32)
    chunk = rows // CHUNKS
    block = chunk // group
    split = group == 4

    halo = shifted(inputs[rows - 16:], 1)
    groups = weight_groups(w_in, conv_w, w_out, core, tp)
    gain_one = norm_one.astype(F32)[None, :]
    gain_two = norm_two.astype(F32)[None, :]
    extra = -units % 128
    columns = lambda w: jnp.pad(w, ((0, 0), (0, extra)))
    w_gate, w_up, w_down = columns(w_gate), columns(w_up), jnp.pad(w_down, ((0, extra), (0, 0)))
    padded = units + extra

    scatter = lambda a: lax.psum_scatter(a, "tp", scatter_dimension=0, tiled=True)
    gather = lambda a: lax.all_gather(a.astype(BF16), "tp", axis=0, tiled=True)
    tie = lax.optimization_barrier

    def chunk_layer(k, kept, after=()):
        before = halo if k == 0 else inputs[k * chunk - 16:k * chunk]
        return layer(k, CHUNKS, slot, own, info, lengths, inputs, cotangent, before, gain_one, gain_two, groups,
                     w_gate, w_up, w_down, kept, after, block if split else TILE, split)

    if split and lax.axis_size("seq") == 8:
        kept, blocks0 = chunk_layer(0, [])
        terms0 = exchange(blocks0)
        kept, blocks1 = chunk_layer(1, kept)
        kept, blocks1, terms0 = tie((kept, blocks1, terms0))

        share0, norm0 = second_norm(0, info, terms0, kept[7], kept[4], gain_two)
        terms1 = exchange(blocks1)
        sides0 = to_sides(share0)
        kept, blocks2 = chunk_layer(2, kept, [share0])
        kept, blocks2, sides0, terms1 = tie((kept, blocks2, sides0, terms1))

        proj, gated, h1, h2, grad_low, activ, grads, resid = kept[:8]
        terms2 = exchange(blocks2)
        share1, norm1 = second_norm(1, info, terms1, resid, grad_low, gain_two)
        sides1 = to_sides(share1)
        split_at = 2 * padded * 2 // 3
        g_first = weight_grad(h2, grads, [share1], 0, split_at)
        g_first, terms2, activ, share1, grads = tie((g_first, terms2, activ, share1, grads))

        first = SeqSum(g_first)
        first.pair()
        share2, norm2 = second_norm(2, info, terms2, resid, grad_low, gain_two)
        sides2 = to_sides(share2)
        g_down = weight_grad(activ, grad_low, [share2], dtype=BF16)
        g_down, grads, sides1, state = tie((g_down, grads, sides1, first.state()))

        first.put(state)
        first.near()
        corner01 = corners([sides0, sides1])
        next_c = shifted(proj[:16, width:2 * width], -1)
        g_second = weight_grad(h2, grads, [first.value], split_at, 2 * padded - split_at, BF16)
        g_second, corner01, sides2, next_c, state, forward = tie(
            (g_second, corner01, sides2, next_c, first.state(), kept[8:12]))

        first.put(state)
        first.cross()
        g_down, g_second = lax.psum((g_down, g_second), "seq")
        corner2 = corners([sides2])
        grl = place(0, 1, info, [share0, *sides0, *corner01], rows, None)
        next_grl = shifted(grl[:16], -1)
        grl = place(1, 1, info, [share1, *sides1, *corner01], rows, grl, 1)
        grl, next_grl, corner2, forward = tie((grl, next_grl, corner2, forward))

        terms = exchange(forward)
        grl = place(2, 1, info, [share2, *sides2, *corner2], rows, grl)
        g_proj, g_conv = own_backward(slot, info, grl, proj, next_grl, next_c[:, :own], w_out, groups[0][1][2])
        g_in = weight_grad(h1, g_proj)
        g_in, terms[1], state = tie((g_in, terms[1], first.state()))

        first.put(state)
        first.back()
        tail_in = SeqSum(jnp.concatenate([g_in, jnp.pad(g_conv[:3].reshape(1, -1), ((0, 15), (0, 0)))], axis=0))
        tail_in.pair()
        g_out = weight_grad(gated, grl, [tail_in.value])
        g_out, state = tie((g_out, tail_in.state()))

        tail_in.put(state)
        tail_in.near()
        tail_out = SeqSum(g_out)
        tail_out.pair()
        g_norm_two = norm0 + norm1 + norm2
        g_norm_two = g_norm_two + swap(g_norm_two, 1)
        back = lambda k, kept, after: mixer_backward(
            slot, info, grl, inputs, proj, next_grl, next_c, gain_one, groups, after, k, 2, kept)
        grad_inputs, norm_late, rest = back(0, (), [tail_in.value])
        grad_inputs, norm_late, rest, terms, g_norm_two, state, state2, state3 = tie((
            grad_inputs, norm_late, rest, terms, g_norm_two, tail_in.state(), tail_out.state(), first.state()))

        tail_in.put(state)
        tail_out.put(state2)
        first.put(state3)
        final = (resid + sum(t.astype(F32) for t in terms)).astype(BF16)
        sides = to_sides(final)
        tail_in.cross()
        tail_out.near()
        grad_inputs, norm_early, _ = back(1, (rest, grad_inputs), [tail_in.value, tail_out.value, final])
        grad_inputs, norm_early, sides, g_down, g_second, state, state2, state3 = tie((
            grad_inputs, norm_early, sides, g_down, g_second, tail_in.state(), tail_out.state(), first.state()))

        tail_in.put(state)
        tail_out.put(state2)
        first.put(state3)
        corner = corners([sides])
        first.share()
        tail_in.back()
        tail_out.cross()
        g_norm_two = g_norm_two + swap(g_norm_two, 2)
        norms = small_sum(jnp.concatenate([norm_early[:1] + norm_late[:1], g_norm_two], axis=0))
        g_norm_one, g_norm_two = norms[0], norms[1]
        output = place(0, CHUNKS, info, [final, *sides, *corner], rows, None)
        tail_in.share()
        tail_out.back()
        tail_out.share()
        g_first = first.result()
        g_gu = jnp.concatenate([g_first, g_second.astype(F32)], axis=1)
        g_down = g_down.astype(F32)
        g_out = tail_out.result()
        g_in = tail_in.result()
        g_conv = g_in[width].reshape(3, own)
    else:
        kept, finals, shares, g_norm_two = [], [], [], 0.0
        cut = lambda a, k: lax.dynamic_slice_in_dim(a, k * chunk + tp * block, block, 0)
        whole = lambda blocks: blocks[0] if not split else jnp.concatenate(
            [lax.dynamic_index_in_dim(jnp.stack(blocks), tp ^ j, 0, keepdims=False) for j in range(4)], axis=0)
        for k in range(CHUNKS):
            kept, blocks = chunk_layer(k, kept)
            terms = kept[8:12] if split else blocks[:1]
            terms = [t[k * block:(k + 1) * block] for t in terms] if split else terms
            d_hidden = scatter(whole(blocks if split else blocks[1:])).astype(F32)
            res = kept[7][k * block:(k + 1) * block] if split else cut(kept[7], k)
            finals.append(gather(res + scatter(whole(terms)).astype(F32)))
            scale = rms_scale(res)
            normed = res * scale
            d_normed = d_hidden * gain_two
            g_norm_two += jnp.sum(d_hidden * normed, axis=0)
            shares.append(gather(cut(kept[4], k).astype(F32) + scale * (
                d_normed - normed * jnp.mean(d_normed * normed, axis=1, keepdims=True))))
        proj, gated, h1, h2, grad_low, activ, grads, resid = kept[:8]
        grl = jnp.concatenate(shares, axis=0)
        output = jnp.concatenate(finals, axis=0)
        g_norm_two = lax.psum(g_norm_two, "tp")
        next_c = shifted(proj[:16, width:2 * width], -1)
        next_grl = shifted(grl[:16], -1)
        g_proj, g_conv = own_backward(slot, info, grl, proj, next_grl, next_c[:, :own], w_out, groups[0][1][2])
        grad_inputs, g_norm_one, _ = mixer_backward(slot, info, grl, inputs, proj, next_grl, next_c, gain_one, groups)
        g_norm_one = small_sum(g_norm_one[0])
        g_down = seq_sum(weight_grad(activ, grad_low))
        g_gu = seq_sum(weight_grad(h2, grads))
        g_out = seq_sum(weight_grad(gated, grl))
        g_in = seq_sum(weight_grad(h1, g_proj))
        g_conv = lax.psum(g_conv[:3], "seq")
        g_norm_two = lax.psum(g_norm_two, "seq")
    g_in = g_in[:width]
    return (
        output,
        grad_inputs,
        jnp.stack([g_in[:, i * own:(i + 1) * own] for i in range(3)]),
        g_conv,
        g_out,
        g_norm_one,
        g_norm_two,
        g_gu[:, :units],
        g_gu[:, padded:padded + units],
        g_down[:units],
    )


def solution(mesh):
    tokens = P("seq", None)
    columns = P(None, "tp")
    lines = P("tp", None)
    stacked = P(None, None, "tp")
    return jax.shard_map(
        per_device,
        mesh=mesh,
        in_specs=(tokens, stacked, columns, lines, P(), P(), columns, columns, lines, P(), tokens),
        out_specs=(tokens, tokens, stacked, columns, lines, P(), P(), columns, columns, lines),
        check_vma=False,
    )
```

time: 727 us -> 532 us (0.73)
  waiting for transfers between devices: 369 us -> 99.9 us
  Pallas kernels: 191 us -> 281 us
  blocking collectives: 59 us -> 0 us
  starting transfers between devices: 16.8 us -> 64.4 us
  other arithmetic: 52.7 us -> 42 us
    reduce_scatter x2 -> x0, waiting for transfers between devices: 138 us -> none  [scatter_sum(): return lax.psum_scatter(value, 'tp', scatter_dimension=0, tiled=True)]
    psum x1, waiting for transfers between devices: 139 us -> 24 us  [per_device(): g_down, g_second = lax.psum((g_down, g_second), 'seq')]
    pallas_call x3 -> x13, Pallas kernels: 140 us -> 225 us  [the longest x3 124 us: layer(): pl.pallas_call(functools.partial(layer_body, slot, own, layout, chunk * s...]
    psum x2 -> x0, blocking collectives: 59 us -> none  [the longest x1 41.3 us: per_device(): g_norm_two = lax.psum(g_norm_two, ('seq', 'tp'))]
    ppermute x9 -> x32, starting transfers between devices: 12.4 us -> 36.9 us  [swap(): return lax.ppermute(value, 'tp', [(i, i ^ step) for i in range(count)])]
    ppermute x0 -> x22, waiting for transfers between devices: none -> 22.2 us  [swap_seq(): return lax.ppermute(value, 'seq', [(i, i ^ step) for i in range(count)])]
    ppermute x0 -> x22, starting transfers between devices: none -> 22.2 us  [swap_seq(): return lax.ppermute(value, 'seq', [(i, i ^ step) for i in range(count)])]
    all_gather x2 -> x0, waiting for transfers between devices: 18.8 us -> none  [gather(): return lax.all_gather(value, 'tp', axis=0, tiled=True)]
  transfers between devices with their start and end apart: 17 -> 58, of which waited for: 6 -> 12; matrix products, arithmetic and copies ran while one was open for 7% -> 8% of each run, Pallas kernels for 13% -> 45%
where the time goes in v2:
time: 532 us; the launch traced here: 524 us
  Pallas kernels  281 us (53%)
  waiting for transfers between devices  99.9 us (19%)
  starting transfers between devices  64.4 us (12%)
  other arithmetic  42 us (8%)
  local copies, waits for them, and re-layouts  21.2 us (4%)
  between operations  15.4 us (3%)
    pallas_call x3, Pallas kernels, layer(): pl.pallas_call(functools.partial(layer_body, slot, own, layout, chunk * s...  124 us
    pallas_call x5, Pallas kernels, weight_grad(): pl.pallas_call(weight_grad_body, grid=(wide // tile,), in_specs=[resident...  56.2 us
    pallas_call x2, Pallas kernels, mixer_backward(): pl.pallas_call(functools.partial(mixer_backward_body, slot, layout, len(w...  54.5 us
    ppermute x32, waiting for transfers between devices, swap(): return lax.ppermute(value, 'tp', [(i, i ^ step) for i in range(count)])  53.6 us
    ppermute x32, starting transfers between devices, swap(): return lax.ppermute(value, 'tp', [(i, i ^ step) for i in range(count)])  36.9 us
    psum x1, waiting for transfers between devices, per_device(): g_down, g_second = lax.psum((g_down, g_second), 'seq')  24 us
    ppermute x22, waiting for transfers between devices, swap_seq(): return lax.ppermute(value, 'seq', [(i, i ^ step) for i in range(count)])  22.2 us
    ppermute x22, starting transfers between devices, swap_seq(): return lax.ppermute(value, 'seq', [(i, i ^ step) for i in range(count)])  22.2 us
  transfers between devices with their start and end apart: 58, of which 12 were waited for; matrix products, arithmetic and copies ran while one was open for 8% of the time, Pallas kernels for 45%

profile of v2, /device:TPU:0, one launch (start us, length us, event | category | flops | bytes accessed | tf_op | source)
XLA Modules:
  0.0 524.0 jit_solution(624387757130581232)
XLA Ops:
  10.4 3.0 collective-permute-start.2
  14.9 21.8 %collective-permute-done.2.refs_10_.refs_5_ = bf16[4112,128]{1,0:T(8,128)(2,1)S(1)} collective-permute-done((bf16[4112,128]{1,0:T(8,128)(2,1)S(1)}, bf16[4112,128]{1,0:T(8,128)(2,1)S(1)}, u32[]{:S(2)}, u32[]{:S(2)}) %collective-permute-start.2) | collective-permute-done | bytes 1052704 | tf_op jit(solution)/shard_map/ppermute | solution.py:488
  40.6 9.5 %collective-permute-done.5.refs_13_.refs_8_ = bf16[2064,128]{1,0:T(8,128)(2,1)} collective-permute-done((bf16[2064,128]{1,0:T(8,128)(2,1)S(1)}, bf16[2064,128]{1,0:T(8,128)(2,1)}, u32[]{:S(2)}, u32[]{:S(2)}) %collective-permute-start.5) | collective-permute-done | bytes 528416 | tf_op jit(solution)/shard_map/ppermute | solution.py:488
  50.1 3.0 collective-permute-done.4.refs_12_.refs_7_
  60.3 41.3 %layer.3 = (bf16[3072,4096]{1,0:T(8,128)(2,1)}, bf16[3072,256]{1,0:T(8,128)(2,1)}, bf16[3072,1024]{1,0:T(8,128)(2,1)}, bf16[3072,1024]{1,0:T(8,128)(2,1)}, bf16[...) custom-call(s32[3]{0:T(128)} %pad_add_fusion.info, ...), custom_call_target="tpu_custom_call" | custom-call | flops 23085449216 | bytes 41975808 | tf_op jit(solution)/shard_map/layer/pallas_call | solution.py:251
  105.2 41.5 %layer.4 = (bf16[3072,4096]{1,0:T(8,128)(2,1)}, bf16[3072,256]{1,0:T(8,128)(2,1)}, bf16[3072,1024]{1,0:T(8,128)(2,1)}, bf16[3072,1024]{1,0:T(8,128)(2,1)}, bf16[...) custom-call(s32[3]{0:T(128)} %pad_add_fusion.info, ...), custom_call_target="tpu_custom_call", output_to_operand_aliasing={{0}: (21, {}), {1}: (22, {}), {2}: (23, {}), {3}: (24, {}),... | custom-call | flops 23085449216 | bytes 41975808 | tf_op jit(solution)/shard_map/layer/pallas_call | solution.py:251
  147.8 4.4 second_norm.3
  157.8 41.5 %layer.5 = (bf16[3072,4096]{1,0:T(8,128)(2,1)}, bf16[3072,256]{1,0:T(8,128)(2,1)}, bf16[3072,1024]{1,0:T(8,128)(2,1)}, bf16[3072,1024]{1,0:T(8,128)(2,1)}, bf16[...) custom-call(s32[3]{0:T(128)} %pad_add_fusion.info, ...), custom_call_target="tpu_custom_call", output_to_operand_aliasing={{0}: (21, {}), {1}: (22, {}), {2}: (23, {}), {3}: (24, {}),... | custom-call | flops 23085449216 | bytes 41975808 | tf_op jit(solution)/shard_map/layer/pallas_call | solution.py:251
  203.0 4.2 second_norm.4
  207.2 16.7 %weight_grad.5 = f32[1024,1536]{1,0:T(8,128)} custom-call(bf16[3072,1024]{1,0:T(8,128)(2,1)} %get-tuple-element.250.left, bf16[3072,2304]{1,0:T(8,128)(2,1)} %get-tuple-element.271.right, bf16[256,1024]{1,0:T(8,128)(2,1)} %get-tuple-element.285.refs_0_.own), custom_call_target="tpu_custom_call" | custom-call | flops 9663676416 | bytes 22020096 | tf_op jit(solution)/shard_map/weight_grad/pallas_call | solution.py:351
  229.3 4.2 second_norm.5
  233.6 12.7 %weight_grad.6 = bf16[1152,1024]{1,0:T(8,128)(2,1)} custom-call(bf16[3072,1152]{1,0:T(8,128)(2,1)} %get-tuple-element.268.left, bf16[3072,1024]{1,0:T(8,128)(2,1)} %get-tuple-element.256.grad.right, bf16[256,1024]{1,0:T(8,128)(2,1)} %get-tuple-element.267.refs_0_.own), custom_call_target="tpu_custom_call" | custom-call | flops 7247757312 | bytes 18087936 | tf_op jit(solution)/shard_map/weight_grad/pallas_call | solution.py:351
  259.2 10.4 %weight_grad.7 = bf16[1024,768]{1,0:T(8,128)(2,1)} custom-call(bf16[3072,1024]{1,0:T(8,128)(2,1)} %get-tuple-element.250.left, bf16[3072,2304]{1,0:T(8,128)(2,1)} %get-tuple-element.271.right, f32[512,1536]{1,0:T(8,128)} %copy-done.3), custom_call_target="tpu_custom_call" | custom-call | flops 4831838208 | bytes 14155776 | tf_op jit(solution)/shard_map/weight_grad/pallas_call | solution.py:351
  269.6 10.9 %collective-permute-done.24.right = bf16[512,512]{1,0:T(8,128)(2,1)S(1)} collective-permute-done((bf16[512,512]{1,0:T(8,128)(2,1)}, bf16[512,512]{1,0:T(8,128)(2,1)S(1)}, u32[]{:S(2)}, u32[]{:S(2)}) %collective-permute-start.24) | collective-permute-done | bytes 524320 | tf_op jit(solution)/shard_map/ppermute | solution.py:488
  283.2 4.1 place.4.refs_0_
  289.6 4.1 place.5.refs_0_
  296.2 3.8 collective-permute-start.33
  300.6 4.1 place.6.grl.right
  304.7 11.2 %own_backward.1 = (bf16[3072,768]{1,0:T(8,128)(2,1)}, f32[8,256]{1,0:T(8,128)}) custom-call(s32[3]{0:T(128)} %pad_add_fusion.info, bf16[3072,1024]{1,0:T(8,128)(2,1)} %place.6.grl.right, bf16[3072,4096]{1,0:T(8,128)(2,1)} %get-tuple-element.278.p_b.p_c.p_x.conved, bf16[3072,4096]{1,0:T(8,128)(2,1)} %get-tuple-element.278.p_b.p_c.p_x.conved, ...), custom_call_target="tpu_custom_call" | custom-call | flops 1610612736 | bytes 17309696 | tf_op jit(solution)/shard_map/own_backward/pallas_call | solution.py:407
  316.6 10.9 %weight_grad.8 = f32[1024,768]{1,0:T(8,128)} custom-call(bf16[3072,1024]{1,0:T(8,128)(2,1)} %get-tuple-element.298.left, bf16[3072,768]{1,0:T(8,128)(2,1)} %get-tuple-element.299.right), custom_call_target="tpu_custom_call" | custom-call | flops 4831838208 | bytes 14155776 | tf_op jit(solution)/shard_map/weight_grad/pallas_call | solution.py:351
  327.5 4.7 collective-permute-done.32
  336.1 3.1 collective-permute-done.37
  343.3 3.8 collective-permute-start.40
  347.1 5.3 %weight_grad.9 = f32[256,1024]{1,0:T(8,128)} custom-call(bf16[3072,256]{1,0:T(8,128)(2,1)} %get-tuple-element.297.left, bf16[3072,1024]{1,0:T(8,128)(2,1)} %place.6.grl.right, f32[1040,768]{1,0:T(8,128)} %copy-done.1), custom_call_target="tpu_custom_call" | custom-call | flops 1610612736 | bytes 8912896 | tf_op jit(solution)/shard_map/weight_grad/pallas_call | solution.py:351
  355.1 27.7 %mixer_backward.2 = (f32[3072,1024]{1,0:T(8,128)}, f32[8,1024]{1,0:T(8,128)}, f32[8,1024]{1,0:T(8,128)}) custom-call(s32[3]{0:T(128)} %pad_add_fusion.info, bf16[3072,1024]{1,0:T(8,128)(2,1)} %place.6.grl.right, bf16[3072,1024]{1,0:T(8,128)(2,1)} %x.7, bf16[3072,4096]{1,0:T(8,128)(2,1)} %get-tuple-element.278.p_b.p_c.p_x.conved, ...), custom_call_target="tpu_custom_call" | custom-call | flops 12884901888 | bytes 33619968 | tf_op jit(solution)/shard_map/mixer_backward/pallas_call | solution.py:466
  382.8 15.8 %collective-permute-done.38 = bf16[260,768]{1,0:T(8,128)(2,1)S(1)} collective-permute-done((bf16[260,768]{1,0:T(8,128)(2,1)S(1)}, bf16[260,768]{1,0:T(8,128)(2,1)S(1)}, u32[]{:S(2)}, u32[]{:S(2)}) %collective-permute-start.38) | collective-permute-done | bytes 399392 | tf_op jit(solution)/shard_map/ppermute | solution.py:493
  398.6 4.1 add_convert_fusion.refs_15_.own
  411.7 26.8 %mixer_backward.3 = (f32[3072,1024]{1,0:T(8,128)}, f32[8,1024]{1,0:T(8,128)}, f32[8,1024]{1,0:T(8,128)}) custom-call(s32[3]{0:T(128)} %pad_add_fusion.info, bf16[3072,1024]{1,0:T(8,128)(2,1)} %place.6.grl.right, bf16[3072,1024]{1,0:T(8,128)(2,1)} %x.7, bf16[3072,4096]{1,0:T(8,128)(2,1)} %get-tuple-element.278.p_b.p_c.p_x.conved, ...), custom_call_target="tpu_custom_call", output_to_operand_aliasing={{0}: (22, {})} | custom-call | flops 12884901888 | bytes 33619968 | tf_op jit(solution)/shard_map/mixer_backward/pallas_call | solution.py:466
  438.6 24.0 %all-reduce.5.cloned.1.call-done = (bf16[1152,1024]{1,0:T(8,128)(2,1)}, bf16[1024,768]{1,0:T(8,128)(2,1)}) async-done(((bf16[1152,1024]{1,0:T(8,128)(2,1)}, bf16[1024,768]{1,0:T(8,128)(2,1)}), (bf16[1152,1024]{1,0:T(8,128)(2,1)}, bf16[1024,768]{1,0:T(8,128)(2,1)})) %all-reduce.5.cloned.1.call-update) | async-done | bytes 3932176 | tf_op jit(solution)/shard_map/psum | solution.py:660
  476.6 4.6 collective-permute-done.54
  492.6 9.6 %place.7 = bf16[3072,1024]{1,0:T(8,128)(2,1)} custom-call(s32[3]{0:T(128)} %pad_add_fusion.info, bf16[768,1024]{1,0:T(8,128)(2,1)} %copy-done.8, bf16[768,1024]{1,0:T(8,128)(2,1)} %collective-permute-done.41.side, bf16[768,1024]{1,0:T(8,128)(2,1)} %collective-permute-done.42.far, bf16[768,512]{1,0:T(8,128)(2,1)} %collective-permute-done.45.left, ...), custom_call_target="tpu_custom_call" | custom-call | bytes 12582912 | tf_op jit(solution)/shard_map/place/pallas_call | solution.py:325
  512.1 4.6 pad_maximum_fusion
  (289 shorter events, 111.0 us)
Async XLA Ops:
  7.2 455.4 %all-reduce.5.cloned.1.call-start = ((), (), s32[]{:S(2)}) async-start(), calls=%async_computation | async-start | bytes 7864320 | tf_op jit(solution)/shard_map/psum | solution.py:660
  10.4 26.3 %collective-permute-start.2 = (bf16[4112,128]{1,0:T(8,128)(2,1)S(1)}, bf16[4112,128]{1,0:T(8,128)(2,1)S(1)}, u32[]{:S(2)}, u32[]{:S(2)}) collective-permute-start(bf16[4112,128]{1,0:T(8,128)(2,1)S(1)} %concatenate.40), channel_id=1, source_target_pairs={{0,2},{1,3},{2,0},{3,1},{4,6},{5,7},{6,4},{7,5},{8,10},{9,11},{10,... | collective-permute-start | bytes 3158024 | tf_op jit(solution)/shard_map/ppermute | solution.py:488
  13.4 25.1 %collective-permute-start = (bf16[4112,128]{1,0:T(8,128)(2,1)S(1)}, bf16[4112,128]{1,0:T(8,128)(2,1)S(1)}, u32[]{:S(2)}, u32[]{:S(2)}) collective-permute-start(bf16[4112,128]{1,0:T(8,128)(2,1)S(1)} %concatenate.40), channel_id=1, source_target_pairs={{0,1},{1,0},{2,3},{3,2},{4,5},{5,4},{6,7},{7,6},{8,9},{9,8},{10,11... | collective-permute-start | bytes 3158024 | tf_op jit(solution)/shard_map/ppermute | solution.py:488
  38.5 20.9 %collective-permute-start.3 = (bf16[4112,128]{1,0:T(8,128)(2,1)S(1)}, bf16[4112,128]{1,0:T(8,128)(2,1)}, u32[]{:S(2)}, u32[]{:S(2)}) collective-permute-start(bf16[4112,128]{1,0:T(8,128)(2,1)S(1)} %collective-permute-done.2.refs_10_.refs_5_), channel_id=1, source_target_pairs={{0,4},{4,0},{8,12},{12,8},{16,20},{20,16},{24,28},{28,24},{1,5},{5... | collective-permute-start | bytes 3158024 | tf_op jit(solution)/shard_map/ppermute | solution.py:493
  101.6 45.1 %collective-permute-start.10 = (bf16[256,1024]{1,0:T(8,128)(2,1)}, bf16[256,1024]{1,0:T(8,128)(2,1)S(1)}, u32[]{:S(2)}, u32[]{:S(2)}) collective-permute-start(bf16[256,1024]{1,0:T(8,128)(2,1)} %get-tuple-element.210), channel_id=1, source_target_pairs={{0,1},{1,0},{2,3},{3,2},{4,5},{5,4},{6,7},{7,6},{8,9},{9,8},{10,11... | collective-permute-start | bytes 1572872 | tf_op jit(solution)/shard_map/ppermute | solution.py:488
  102.7 44.0 %collective-permute-start.11 = (bf16[256,1024]{1,0:T(8,128)(2,1)}, bf16[256,1024]{1,0:T(8,128)(2,1)S(1)}, u32[]{:S(2)}, u32[]{:S(2)}) collective-permute-start(bf16[256,1024]{1,0:T(8,128)(2,1)} %get-tuple-element.211), channel_id=1, source_target_pairs={{0,2},{1,3},{2,0},{3,1},{4,6},{5,7},{6,4},{7,5},{8,10},{9,11},{10,... | collective-permute-start | bytes 1572872 | tf_op jit(solution)/shard_map/ppermute | solution.py:488
  103.7 43.0 %collective-permute-start.9 = (bf16[256,1024]{1,0:T(8,128)(2,1)}, bf16[256,1024]{1,0:T(8,128)(2,1)S(1)}, u32[]{:S(2)}, u32[]{:S(2)}) collective-permute-start(bf16[256,1024]{1,0:T(8,128)(2,1)} %get-tuple-element.209), channel_id=1, source_target_pairs={{0,3},{1,2},{2,1},{3,0},{4,7},{5,6},{6,5},{7,4},{8,11},{9,10},{10,... | collective-permute-start | bytes 1572872 | tf_op jit(solution)/shard_map/ppermute | solution.py:488
  152.2 47.1 %collective-permute-start.12 = (bf16[256,1024]{1,0:T(8,128)(2,1)}, bf16[256,1024]{1,0:T(8,128)(2,1)S(1)}, u32[]{:S(2)}, u32[]{:S(2)}) collective-permute-start(bf16[256,1024]{1,0:T(8,128)(2,1)} %get-tuple-element.228.refs_31_.own), channel_id=1, source_target_pairs={{0,1},{1,0},{2,3},{3,2},{4,5},{5,4},{6,7},{7,6},{8,9},{9,8},{10,11... | collective-permute-start | bytes 1572872 | tf_op jit(solution)/shard_map/ppermute | solution.py:488
  153.3 46.1 %collective-permute-start.13 = (bf16[256,1024]{1,0:T(8,128)(2,1)}, bf16[256,1024]{1,0:T(8,128)(2,1)S(1)}, u32[]{:S(2)}, u32[]{:S(2)}) collective-permute-start(bf16[256,1024]{1,0:T(8,128)(2,1)} %get-tuple-element.228.refs_31_.own), channel_id=1, source_target_pairs={{0,2},{1,3},{2,0},{3,1},{4,6},{5,7},{6,4},{7,5},{8,10},{9,11},{10,... | collective-permute-start | bytes 1572872 | tf_op jit(solution)/shard_map/ppermute | solution.py:488
  154.3 45.1 %collective-permute-start.14 = (bf16[256,1024]{1,0:T(8,128)(2,1)S(1)}, bf16[256,1024]{1,0:T(8,128)(2,1)S(1)}, u32[]{:S(2)}, u32[]{:S(2)}) collective-permute-start(bf16[256,1024]{1,0:T(8,128)(2,1)S(1)} %copy-done.53), channel_id=1, source_target_pairs={{0,3},{1,2},{2,1},{3,0},{4,7},{5,6},{6,5},{7,4},{8,11},{9,10},{10,... | collective-permute-start | bytes 1572872 | tf_op jit(solution)/shard_map/ppermute | solution.py:488
  155.7 43.7 %collective-permute-start.15 = (bf16[256,1024]{1,0:T(8,128)(2,1)S(1)}, bf16[256,1024]{1,0:T(8,128)(2,1)S(1)}, u32[]{:S(2)}, u32[]{:S(2)}) collective-permute-start(bf16[256,1024]{1,0:T(8,128)(2,1)S(1)} %copy-done.52), channel_id=1, source_target_pairs={{0,1},{1,0},{2,3},{3,2},{4,5},{5,4},{6,7},{7,6},{8,9},{9,8},{10,11... | collective-permute-start | bytes 1572872 | tf_op jit(solution)/shard_map/ppermute | solution.py:488
  156.8 42.6 %collective-permute-start.16 = (bf16[256,1024]{1,0:T(8,128)(2,1)S(1)}, bf16[256,1024]{1,0:T(8,128)(2,1)S(1)}, u32[]{:S(2)}, u32[]{:S(2)}) collective-permute-start(bf16[256,1024]{1,0:T(8,128)(2,1)S(1)} %copy-done.51), channel_id=1, source_target_pairs={{0,2},{1,3},{2,0},{3,1},{4,6},{5,7},{6,4},{7,5},{8,10},{9,11},{10,... | collective-permute-start | bytes 1572872 | tf_op jit(solution)/shard_map/ppermute | solution.py:488
  199.4 24.5 %collective-permute-start.17 = (bf16[256,1024]{1,0:T(8,128)(2,1)}, bf16[256,1024]{1,0:T(8,128)(2,1)S(1)}, u32[]{:S(2)}, u32[]{:S(2)}) collective-permute-start(bf16[256,1024]{1,0:T(8,128)(2,1)} %get-tuple-element.259), channel_id=1, source_target_pairs={{0,3},{1,2},{2,1},{3,0},{4,7},{5,6},{6,5},{7,4},{8,11},{9,10},{10,... | collective-permute-start | bytes 1572872 | tf_op jit(solution)/shard_map/ppermute | solution.py:488
  200.9 23.3 %collective-permute-start.18 = (bf16[256,1024]{1,0:T(8,128)(2,1)}, bf16[256,1024]{1,0:T(8,128)(2,1)S(1)}, u32[]{:S(2)}, u32[]{:S(2)}) collective-permute-start(bf16[256,1024]{1,0:T(8,128)(2,1)} %get-tuple-element.260), channel_id=1, source_target_pairs={{0,1},{1,0},{2,3},{3,2},{4,5},{5,4},{6,7},{7,6},{8,9},{9,8},{10,11... | collective-permute-start | bytes 1572872 | tf_op jit(solution)/shard_map/ppermute | solution.py:488
  202.0 22.6 %collective-permute-start.19 = (bf16[256,1024]{1,0:T(8,128)(2,1)}, bf16[256,1024]{1,0:T(8,128)(2,1)S(1)}, u32[]{:S(2)}, u32[]{:S(2)}) collective-permute-start(bf16[256,1024]{1,0:T(8,128)(2,1)} %get-tuple-element.261), channel_id=1, source_target_pairs={{0,2},{1,3},{2,0},{3,1},{4,6},{5,7},{6,4},{7,5},{8,10},{9,11},{10,... | collective-permute-start | bytes 1572872 | tf_op jit(solution)/shard_map/ppermute | solution.py:488
  249.2 31.4 %collective-permute-start.28 = (bf16[256,1536]{1,0:T(8,128)(2,1)S(1)}, bf16[256,1536]{1,0:T(8,128)(2,1)}, u32[]{:S(2)}, u32[]{:S(2)}) collective-permute-start(bf16[256,1536]{1,0:T(8,128)(2,1)S(1)} %dynamic-slice_convert_fusion.2), channel_id=1, source_target_pairs={{0,8},{4,12},{8,0},{12,4},{16,24},{20,28},{24,16},{28,20},{1,9},{5... | collective-permute-start | bytes 2359304 | tf_op jit(solution)/shard_map/ppermute | solution.py:493
  256.3 24.2 %collective-permute-start.24 = (bf16[512,512]{1,0:T(8,128)(2,1)}, bf16[512,512]{1,0:T(8,128)(2,1)S(1)}, u32[]{:S(2)}, u32[]{:S(2)}) collective-permute-start(bf16[512,512]{1,0:T(8,128)(2,1)} %pad_maximum_fusion.5), channel_id=1, source_target_pairs={{0,2},{1,3},{2,0},{3,1},{4,6},{5,7},{6,4},{7,5},{8,10},{9,11},{10,... | collective-permute-start | bytes 1572872 | tf_op jit(solution)/shard_map/ppermute | solution.py:488
  258.2 22.3 %collective-permute-start.23 = (bf16[512,512]{1,0:T(8,128)(2,1)}, bf16[512,512]{1,0:T(8,128)(2,1)S(1)}, u32[]{:S(2)}, u32[]{:S(2)}) collective-permute-start(bf16[512,512]{1,0:T(8,128)(2,1)} %pad_maximum_fusion.4), channel_id=1, source_target_pairs={{0,1},{1,0},{2,3},{3,2},{4,5},{5,4},{6,7},{7,6},{8,9},{9,8},{10,11... | collective-permute-start | bytes 1572872 | tf_op jit(solution)/shard_map/ppermute | solution.py:488
  293.8 38.4 %collective-permute-start.32 = (bf16[768,1024]{1,0:T(8,128)(2,1)}, bf16[768,1024]{1,0:T(8,128)(2,1)}, u32[]{:S(2)}, u32[]{:S(2)}) collective-permute-start(bf16[768,1024]{1,0:T(8,128)(2,1)} %get-tuple-element.300), channel_id=1, source_target_pairs={{0,3},{1,2},{2,1},{3,0},{4,7},{5,6},{6,5},{7,4},{8,11},{9,10},{10,... | collective-permute-start | bytes 4718600 | tf_op jit(solution)/shard_map/ppermute | solution.py:488
  296.2 31.3 %collective-permute-start.33 = (bf16[256,1536]{1,0:T(8,128)(2,1)S(1)}, bf16[256,1536]{1,0:T(8,128)(2,1)S(1)}, u32[]{:S(2)}, u32[]{:S(2)}) collective-permute-start(bf16[256,1536]{1,0:T(8,128)(2,1)S(1)} %add_convert_fusion.2), channel_id=1, source_target_pairs={{0,24},{4,28},{8,16},{12,20},{16,8},{20,12},{24,0},{28,4},{1,25},{... | collective-permute-start | bytes 2359304 | tf_op jit(solution)/shard_map/ppermute | solution.py:493
  339.3 43.5 %collective-permute-start.35 = (bf16[768,1024]{1,0:T(8,128)(2,1)}, bf16[768,1024]{1,0:T(8,128)(2,1)}, u32[]{:S(2)}, u32[]{:S(2)}) collective-permute-start(bf16[768,1024]{1,0:T(8,128)(2,1)} %get-tuple-element.312), channel_id=1, source_target_pairs={{0,1},{1,0},{2,3},{3,2},{4,5},{5,4},{6,7},{7,6},{8,9},{9,8},{10,11... | collective-permute-start | bytes 4718600 | tf_op jit(solution)/shard_map/ppermute | solution.py:488
  339.8 43.0 %collective-permute-start.36 = (bf16[768,1024]{1,0:T(8,128)(2,1)}, bf16[768,1024]{1,0:T(8,128)(2,1)}, u32[]{:S(2)}, u32[]{:S(2)}) collective-permute-start(bf16[768,1024]{1,0:T(8,128)(2,1)} %get-tuple-element.313), channel_id=1, source_target_pairs={{0,2},{1,3},{2,0},{3,1},{4,6},{5,7},{6,4},{7,5},{8,10},{9,11},{10,... | collective-permute-start | bytes 4718600 | tf_op jit(solution)/shard_map/ppermute | solution.py:488
  343.3 39.5 %collective-permute-start.40 = (bf16[256,1536]{1,0:T(8,128)(2,1)}, bf16[256,1536]{1,0:T(8,128)(2,1)}, u32[]{:S(2)}, u32[]{:S(2)}) collective-permute-start(bf16[256,1536]{1,0:T(8,128)(2,1)} %add_convert_fusion.1), channel_id=1, source_target_pairs={{0,8},{4,12},{8,0},{12,4},{16,24},{20,28},{24,16},{28,20},{1,9},{5... | collective-permute-start | bytes 2359304 | tf_op jit(solution)/shard_map/ppermute | solution.py:493
  353.9 44.7 %collective-permute-start.38 = (bf16[260,768]{1,0:T(8,128)(2,1)S(1)}, bf16[260,768]{1,0:T(8,128)(2,1)S(1)}, u32[]{:S(2)}, u32[]{:S(2)}) collective-permute-start(bf16[260,768]{1,0:T(8,128)(2,1)S(1)} %dynamic-slice_convert_fusion.3), channel_id=1, source_target_pairs={{0,8},{4,12},{8,0},{12,4},{16,24},{20,28},{24,16},{28,20},{1,9},{5... | collective-permute-start | bytes 1198088 | tf_op jit(solution)/shard_map/ppermute | solution.py:493
  355.0 27.7 %collective-permute-start.39 = (bf16[128,1024]{1,0:T(8,128)(2,1)}, bf16[128,1024]{1,0:T(8,128)(2,1)}, u32[]{:S(2)}, u32[]{:S(2)}) collective-permute-start(bf16[128,1024]{1,0:T(8,128)(2,1)} %dynamic-slice_convert_fusion.4), channel_id=1, source_target_pairs={{0,4},{4,0},{8,12},{12,8},{16,20},{20,16},{24,28},{28,24},{1,5},{5... | collective-permute-start | bytes 786440 | tf_op jit(solution)/shard_map/ppermute | solution.py:493
  402.7 59.9 %collective-permute-start.41 = (bf16[768,1024]{1,0:T(8,128)(2,1)S(1)}, bf16[768,1024]{1,0:T(8,128)(2,1)}, u32[]{:S(2)}, u32[]{:S(2)}) collective-permute-start(bf16[768,1024]{1,0:T(8,128)(2,1)S(1)} %add_convert_fusion.refs_15_.own), channel_id=1, source_target_pairs={{0,1},{1,0},{2,3},{3,2},{4,5},{5,4},{6,7},{7,6},{8,9},{9,8},{10,11... | collective-permute-start | bytes 4718600 | tf_op jit(solution)/shard_map/ppermute | solution.py:488
  402.8 59.8 %collective-permute-start.42 = (bf16[768,1024]{1,0:T(8,128)(2,1)S(1)}, bf16[768,1024]{1,0:T(8,128)(2,1)}, u32[]{:S(2)}, u32[]{:S(2)}) collective-permute-start(bf16[768,1024]{1,0:T(8,128)(2,1)S(1)} %add_convert_fusion.refs_15_.own), channel_id=1, source_target_pairs={{0,2},{1,3},{2,0},{3,1},{4,6},{5,7},{6,4},{7,5},{8,10},{9,11},{10,... | collective-permute-start | bytes 4718600 | tf_op jit(solution)/shard_map/ppermute | solution.py:488
  405.0 57.6 %collective-permute-start.44 = (bf16[64,1024]{1,0:T(8,128)(2,1)}, bf16[64,1024]{1,0:T(8,128)(2,1)S(1)}, u32[]{:S(2)}, u32[]{:S(2)}) collective-permute-start(bf16[64,1024]{1,0:T(8,128)(2,1)} %dynamic-slice_convert_fusion.5), channel_id=1, source_target_pairs={{0,8},{4,12},{8,0},{12,4},{16,24},{20,28},{24,16},{28,20},{1,9},{5... | collective-permute-start | bytes 393224 | tf_op jit(solution)/shard_map/ppermute | solution.py:493
  407.7 54.9 %collective-permute-start.43 = (bf16[260,768]{1,0:T(8,128)(2,1)S(1)}, bf16[260,768]{1,0:T(8,128)(2,1)S(1)}, u32[]{:S(2)}, u32[]{:S(2)}) collective-permute-start(bf16[260,768]{1,0:T(8,128)(2,1)S(1)} %add_convert_fusion.4.refs_13_), channel_id=1, source_target_pairs={{0,24},{4,28},{8,16},{12,20},{16,8},{20,12},{24,0},{28,4},{1,25},{... | collective-permute-start | bytes 1198088 | tf_op jit(solution)/shard_map/ppermute | solution.py:493
  410.1 28.5 %collective-permute-start.52 = (f32[1,1024]{1,0:T(1,128)S(1)}, f32[1,1024]{1,0:T(1,128)S(1)}, u32[]{:S(2)}, u32[]{:S(2)}) collective-permute-start(f32[1,1024]{1,0:T(1,128)S(1)} %add.122), channel_id=1, source_target_pairs={{0,2},{1,3},{2,0},{3,1},{4,6},{5,7},{6,4},{7,5},{8,10},{9,11},{10,... | collective-permute-start | bytes 12296 | tf_op jit(solution)/shard_map/ppermute | solution.py:488
  469.6 23.0 %collective-permute-start.45 = (bf16[768,512]{1,0:T(8,128)(2,1)S(1)}, bf16[768,512]{1,0:T(8,128)(2,1)}, u32[]{:S(2)}, u32[]{:S(2)}) collective-permute-start(bf16[768,512]{1,0:T(8,128)(2,1)S(1)} %slice.100), channel_id=1, source_target_pairs={{0,1},{1,0},{2,3},{3,2},{4,5},{5,4},{6,7},{7,6},{8,9},{9,8},{10,11... | collective-permute-start | bytes 2359304 | tf_op jit(solution)/shard_map/ppermute | solution.py:488
  471.5 21.1 %collective-permute-start.46 = (bf16[768,512]{1,0:T(8,128)(2,1)S(1)}, bf16[768,512]{1,0:T(8,128)(2,1)}, u32[]{:S(2)}, u32[]{:S(2)}) collective-permute-start(bf16[768,512]{1,0:T(8,128)(2,1)S(1)} %slice.101), channel_id=1, source_target_pairs={{0,2},{1,3},{2,0},{3,1},{4,6},{5,7},{6,4},{7,5},{8,10},{9,11},{10,... | collective-permute-start | bytes 2359304 | tf_op jit(solution)/shard_map/ppermute | solution.py:488
  (83 other events, 875.3 us)
Sparse Core Ops, SparseCore 0:
  339.4 123.1 all-reduce.4

commit v3 on v2

--- a/solution.py
+++ b/solution.py
@@ -376,14 +376,16 @@
     return d_conv, one, two, g_c, tap[2:3] * d_conv + tap[1:2] * one + tap[0:1] * two
 
 
-def own_backward_body(slot, info, grl, p_b, p_c, p_x, conved, next_grl, next_c, w_out, taps, *refs):
-    g_proj, g_conv, carry = refs[-3:]
+def own_backward_body(slot, info, grl, p_b, p_c, p_x, conved, h1, gated, next_grl, next_c, w_out, taps, *refs):
+    g_in, g_out, g_conv, carry, g_proj = refs[-5:]
 
     @pl.when(pl.program_id(0) == 0)
     def _():
         carry[...] = (dot_nt(next_grl[...], w_out[...]) * next_c[...].astype(F32))[0:8]
-        g_conv[...] = jnp.zeros_like(g_conv)
-
+        for total in (g_in, g_out, g_conv):
+            total[...] = jnp.zeros_like(total)
+
+    g_out[...] += dot_tn(gated[...], grl[...])
     own = w_out.shape[0]
     d_conv, one, two, g_c, d_mixed = conv_backward(slot, info, pl.num_programs(0), dot_nt(grl[...], w_out[...]), p_c, conved, taps, carry)
     b = p_b[...].astype(F32)
@@ -394,29 +396,31 @@
     g_proj[:, 2 * own:] = (d_mixed * b).astype(BF16)
     for k, values in enumerate((two, one, d_conv)):
         g_conv[k:k + 1] += jnp.sum(values * mixed, axis=0, keepdims=True)
-
-
-def own_backward(slot, info, grl, proj, next_grl, next_c, w_out, taps, after=(), tile=512):
+    g_in[...] += dot_tn(h1[...], g_proj[...])
+
+
+def own_backward(slot, info, grl, proj, h1, gated, next_grl, next_c, w_out, taps, after=(), tile=512):
     rows, width = grl.shape
     own = w_out.shape[0]
     groups = proj.shape[1] // 4 // own
     steps = rows // tile
     row = lambda n, at=0: pl.BlockSpec((tile, n), lambda i, *_: (steps - 1 - i, at))
-    outs = [shape((rows, 3 * own), BF16), shape((8, own), F32)]
-    ins = [grl, proj, proj, proj, proj, next_grl, next_c, w_out, taps]
+    outs = [shape((width, 3 * own), F32), shape((own, width), F32), shape((8, own), F32)]
+    ins = [grl, proj, proj, proj, proj, h1, gated, next_grl, next_c, w_out, taps]
     return pl.pallas_call(
         functools.partial(own_backward_body, slot),
         grid_spec=pltpu.PrefetchScalarGridSpec(
             num_scalar_prefetch=1,
             grid=(steps,),
-            in_specs=[row(width)] + [row(own, k * groups) for k in range(4)] + [resident(a) for a in ins[5:]]
+            in_specs=[row(width)] + [row(own, k * groups) for k in range(4)] + [row(width), row(own)]
+            + [resident(a) for a in ins[7:]]
             + [pl.BlockSpec(memory_space=pl.ANY)] * len(after),
-            out_specs=[row(3 * own), pl.BlockSpec((8, own), lambda i, *_: (0, 0))],
-            scratch_shapes=[pltpu.VMEM((8, own), F32)],
+            out_specs=[pl.BlockSpec(s.shape, lambda i, *_: (0, 0)) for s in outs],
+            scratch_shapes=[pltpu.VMEM((8, own), F32), pltpu.VMEM((tile, 3 * own), BF16)],
         ),
         out_shape=outs,
         compiler_params=params(),
-        cost_estimate=cost(2 * rows * width * own, nbytes(grl, *outs) + nbytes(proj) // groups),
+        cost_estimate=cost(10 * rows * width * own, nbytes(grl, h1, gated, *outs) + nbytes(proj) // groups),
         name="own_backward",
     )(info, *ins, *after)
 
@@ -657,37 +661,42 @@
 
         first.put(state)
         first.cross()
-        g_down, g_second = lax.psum((g_down, g_second), "seq")
         corner2 = corners([sides2])
         grl = place(0, 1, info, [share0, *sides0, *corner01], rows, None)
         next_grl = shifted(grl[:16], -1)
         grl = place(1, 1, info, [share1, *sides1, *corner01], rows, grl, 1)
         grl, next_grl, corner2, forward = tie((grl, next_grl, corner2, forward))
 
-        terms = exchange(forward)
+        half = width // 2
+        moved = [swap(forward[3][:, :half], 1), swap(forward[3][:, half:], 2)]
         grl = place(2, 1, info, [share2, *sides2, *corner2], rows, grl)
-        g_proj, g_conv = own_backward(slot, info, grl, proj, next_grl, next_c[:, :own], w_out, groups[0][1][2])
-        g_in = weight_grad(h1, g_proj)
-        g_in, terms[1], state = tie((g_in, terms[1], first.state()))
+        g_in, g_out, g_conv = own_backward(
+            slot, info, grl, proj, h1, gated, next_grl, next_c[:, :own], w_out, groups[0][1][2])
+        g_in, g_out, g_conv, moved, state = tie((g_in, g_out, g_conv, moved, first.state()))
 
         first.put(state)
-        first.back()
+        add = lambda a, b: (a.astype(F32) + b.astype(F32)).astype(BF16)
+        from_side, from_far = moved
+        far = jnp.concatenate([add(forward[2][:, :half], from_side), forward[2][:, half:]], axis=1)
+        side = jnp.concatenate([forward[1][:, :half], add(forward[1][:, half:], from_far)], axis=1)
+        terms = [forward[0], swap(side, 1), swap(far, 2)]
         tail_in = SeqSum(jnp.concatenate([g_in, jnp.pad(g_conv[:3].reshape(1, -1), ((0, 15), (0, 0)))], axis=0))
         tail_in.pair()
-        g_out = weight_grad(gated, grl, [tail_in.value])
-        g_out, state = tie((g_out, tail_in.state()))
-
-        tail_in.put(state)
-        tail_in.near()
         tail_out = SeqSum(g_out)
         tail_out.pair()
-        g_norm_two = norm0 + norm1 + norm2
-        g_norm_two = g_norm_two + swap(g_norm_two, 1)
+        first.back()
+        g_down, g_second, state, state2 = tie((g_down, g_second, tail_in.state(), tail_out.state()))
+
+        g_down, g_second = lax.psum((g_down, g_second), "seq")
+        tail_in.put(state)
+        tail_out.put(state2)
+        tail_in.near()
+        tail_out.near()
         back = lambda k, kept, after: mixer_backward(
             slot, info, grl, inputs, proj, next_grl, next_c, gain_one, groups, after, k, 2, kept)
-        grad_inputs, norm_late, rest = back(0, (), [tail_in.value])
-        grad_inputs, norm_late, rest, terms, g_norm_two, state, state2, state3 = tie((
-            grad_inputs, norm_late, rest, terms, g_norm_two, tail_in.state(), tail_out.state(), first.state()))
+        grad_inputs, norm_late, rest = back(0, (), [tail_in.value, tail_out.value])
+        grad_inputs, norm_late, rest, terms, norm0, norm1, norm2, state, state2, state3 = tie((
+            grad_inputs, norm_late, rest, terms, norm0, norm1, norm2, tail_in.state(), tail_out.state(), first.state()))
 
         tail_in.put(state)
         tail_out.put(state2)
@@ -695,31 +704,45 @@
         final = (resid + sum(t.astype(F32) for t in terms)).astype(BF16)
         sides = to_sides(final)
         tail_in.cross()
-        tail_out.near()
+        tail_out.cross()
+        g_norm_two = norm0 + norm1 + norm2
+        g_norm_two = g_norm_two + swap(g_norm_two, 1)
         grad_inputs, norm_early, _ = back(1, (rest, grad_inputs), [tail_in.value, tail_out.value, final])
-        grad_inputs, norm_early, sides, g_down, g_second, state, state2, state3 = tie((
-            grad_inputs, norm_early, sides, g_down, g_second, tail_in.state(), tail_out.state(), first.state()))
+        grad_inputs, norm_early, sides, state, state2, g_norm_two = tie((
+            grad_inputs, norm_early, sides, tail_in.state(), tail_out.state(), g_norm_two))
+
+        tail_in.put(state)
+        tail_out.put(state2)
+        corner = corners([sides])
+        tail_in.back()
+        tail_out.back()
+        g_norm_two = g_norm_two + swap(g_norm_two, 2)
+        corner, g_norm_two, state, state2 = tie((corner, g_norm_two, tail_in.state(), tail_out.state()))
+
+        tail_in.put(state)
+        tail_out.put(state2)
+        norms = jnp.concatenate([norm_early[:1] + norm_late[:1], g_norm_two], axis=0)
+        norms = norms + swap_seq(norms, 1)
+        tail_in.share()
+        tail_out.share()
+        first.share()
+        output = place(0, CHUNKS, info, [final, *sides, *corner], rows, None)
+        output, norms, state, state2, state3 = tie((output, norms, tail_in.state(), tail_out.state(), first.state()))
+        g_down, g_second, _ = tie((g_down, g_second, output))
 
         tail_in.put(state)
         tail_out.put(state2)
         first.put(state3)
-        corner = corners([sides])
-        first.share()
-        tail_in.back()
-        tail_out.cross()
-        g_norm_two = g_norm_two + swap(g_norm_two, 2)
-        norms = small_sum(jnp.concatenate([norm_early[:1] + norm_late[:1], g_norm_two], axis=0))
+        norms = norms + swap_seq(norms, 2)
+        g_out = tail_out.result()
+        g_in = tail_in.result()
+        g_conv = g_in[width].reshape(3, own)
+        norms, g_out, g_in, g_conv = tie((norms, g_out, g_in, g_conv))
+        norms = norms + swap_seq(norms, 6)
         g_norm_one, g_norm_two = norms[0], norms[1]
-        output = place(0, CHUNKS, info, [final, *sides, *corner], rows, None)
-        tail_in.share()
-        tail_out.back()
-        tail_out.share()
         g_first = first.result()
         g_gu = jnp.concatenate([g_first, g_second.astype(F32)], axis=1)
         g_down = g_down.astype(F32)
-        g_out = tail_out.result()
-        g_in = tail_in.result()
-        g_conv = g_in[width].reshape(3, own)
     else:
         kept, finals, shares, g_norm_two = [], [], [], 0.0
         cut = lambda a, k: lax.dynamic_slice_in_dim(a, k * chunk + tp * block, block, 0)
@@ -744,13 +767,14 @@
         g_norm_two = lax.psum(g_norm_two, "tp")
         next_c = shifted(proj[:16, width:2 * width], -1)
         next_grl = shifted(grl[:16], -1)
-        g_proj, g_conv = own_backward(slot, info, grl, proj, next_grl, next_c[:, :own], w_out, groups[0][1][2])
+        g_in, g_out, g_conv = own_backward(
+            slot, info, grl, proj, h1, gated, next_grl, next_c[:, :own], w_out, groups[0][1][2])
         grad_inputs, g_norm_one, _ = mixer_backward(slot, info, grl, inputs, proj, next_grl, next_c, gain_one, groups)
         g_norm_one = small_sum(g_norm_one[0])
         g_down = seq_sum(weight_grad(activ, grad_low))
         g_gu = seq_sum(weight_grad(h2, grads))
-        g_out = seq_sum(weight_grad(gated, grl))
-        g_in = seq_sum(weight_grad(h1, g_proj))
+        g_out = seq_sum(g_out)
+        g_in = seq_sum(g_in)
         g_conv = lax.psum(g_conv[:3], "seq")
         g_norm_two = lax.psum(g_norm_two, "seq")
     g_in = g_in[:width]

time: 532 us -> 516 us (0.970)
  waiting for transfers between devices: 99.9 us -> 86.9 us
  Pallas kernels: 281 us -> 274 us
  starting transfers between devices: 64.4 us -> 69.8 us
    pallas_call x5 -> x3, Pallas kernels: 56.2 us -> 39.6 us  [weight_grad(): pl.pallas_call(weight_grad_body, grid=(wide // tile,), in_specs=[resident...]
    ppermute x22, waiting for transfers between devices: 22.2 us -> 9.13 us  [swap_seq(): return lax.ppermute(value, 'seq', [(i, i ^ step) for i in range(count)])]
    ppermute x32 -> x33, waiting for transfers between devices: 53.6 us -> 64.3 us  [swap(): return lax.ppermute(value, 'tp', [(i, i ^ step) for i in range(count)])]
    psum x1, waiting for transfers between devices: 24 us -> 13.5 us  [per_device(): g_down, g_second = lax.psum((g_down, g_second), 'seq')]
    pallas_call x1, Pallas kernels: 11.2 us -> 19.9 us  [own_backward(): pl.pallas_call(functools.partial(own_backward_body, slot), grid_spec=pltp...]
    ppermute x32 -> x33, starting transfers between devices: 36.9 us -> 39.8 us  [swap(): return lax.ppermute(value, 'tp', [(i, i ^ step) for i in range(count)])]
  transfers between devices with their start and end apart: 58 -> 59, of which waited for: 12 -> 14; matrix products, arithmetic and copies ran while one was open for 8% -> 9% of each run, Pallas kernels for 45% -> 44%
where the time goes in v3:
time: 516 us; the launch traced here: 508 us
  Pallas kernels  274 us (53%)
  waiting for transfers between devices  86.9 us (17%)
  starting transfers between devices  69.8 us (14%)
  other arithmetic  42.7 us (8%)
  local copies, waits for them, and re-layouts  19.4 us (4%)
  between operations  15.4 us (3%)
    pallas_call x3, Pallas kernels, layer(): pl.pallas_call(functools.partial(layer_body, slot, own, layout, chunk * s...  125 us
    ppermute x33, waiting for transfers between devices, swap(): return lax.ppermute(value, 'tp', [(i, i ^ step) for i in range(count)])  64.3 us
    pallas_call x2, Pallas kernels, mixer_backward(): pl.pallas_call(functools.partial(mixer_backward_body, slot, layout, len(w...  54.5 us
    ppermute x33, starting transfers between devices, swap(): return lax.ppermute(value, 'tp', [(i, i ^ step) for i in range(count)])  39.8 us
    pallas_call x3, Pallas kernels, weight_grad(): pl.pallas_call(weight_grad_body, grid=(wide // tile,), in_specs=[resident...  39.6 us
    ppermute x22, starting transfers between devices, swap_seq(): return lax.ppermute(value, 'seq', [(i, i ^ step) for i in range(count)])  24.8 us
    pallas_call x4, Pallas kernels, place(): pl.pallas_call(place_body, grid_spec=pltpu.PrefetchScalarGridSpec(num_sca...  22.2 us
    pallas_call x1, Pallas kernels, own_backward(): pl.pallas_call(functools.partial(own_backward_body, slot), grid_spec=pltp...  19.9 us
  transfers between devices with their start and end apart: 59, of which 14 were waited for; matrix products, arithmetic and copies ran while one was open for 9% of the time, Pallas kernels for 44%

profile of v3, /device:TPU:0, one launch (start us, length us, event | category | flops | bytes accessed | tf_op | source)
XLA Modules:
  0.0 508.1 jit_solution(15866239209328796453)
XLA Ops:
  10.4 3.0 collective-permute-start.2
  14.9 21.8 %collective-permute-done.2.refs_10_.refs_5_ = bf16[4112,128]{1,0:T(8,128)(2,1)S(1)} collective-permute-done((bf16[4112,128]{1,0:T(8,128)(2,1)S(1)}, bf16[4112,128]{1,0:T(8,128)(2,1)S(1)}, u32[]{:S(2)}, u32[]{:S(2)}) %collective-permute-start.2) | collective-permute-done | bytes 1052704 | tf_op jit(solution)/shard_map/ppermute | solution.py:492
  40.6 9.5 %collective-permute-done.5.refs_13_.refs_8_ = bf16[2064,128]{1,0:T(8,128)(2,1)} collective-permute-done((bf16[2064,128]{1,0:T(8,128)(2,1)S(1)}, bf16[2064,128]{1,0:T(8,128)(2,1)}, u32[]{:S(2)}, u32[]{:S(2)}) %collective-permute-start.5) | collective-permute-done | bytes 528416 | tf_op jit(solution)/shard_map/ppermute | solution.py:492
  50.1 3.0 collective-permute-done.4.refs_12_.refs_7_
  60.4 41.3 %layer.3 = (bf16[3072,4096]{1,0:T(8,128)(2,1)}, bf16[3072,256]{1,0:T(8,128)(2,1)}, bf16[3072,1024]{1,0:T(8,128)(2,1)}, bf16[3072,1024]{1,0:T(8,128)(2,1)}, bf16[...) custom-call(s32[3]{0:T(128)} %pad_add_fusion.info, ...), custom_call_target="tpu_custom_call" | custom-call | flops 23085449216 | bytes 41975808 | tf_op jit(solution)/shard_map/layer/pallas_call | solution.py:251
  105.3 41.6 %layer.4 = (bf16[3072,4096]{1,0:T(8,128)(2,1)}, bf16[3072,256]{1,0:T(8,128)(2,1)}, bf16[3072,1024]{1,0:T(8,128)(2,1)}, bf16[3072,1024]{1,0:T(8,128)(2,1)}, bf16[...) custom-call(s32[3]{0:T(128)} %pad_add_fusion.info, ...), custom_call_target="tpu_custom_call", output_to_operand_aliasing={{0}: (21, {}), {1}: (22, {}), {2}: (23, {}), {3}: (24, {}),... | custom-call | flops 23085449216 | bytes 41975808 | tf_op jit(solution)/shard_map/layer/pallas_call | solution.py:251
  148.0 4.3 second_norm.3
  157.9 41.9 %layer.5 = (bf16[3072,4096]{1,0:T(8,128)(2,1)}, bf16[3072,256]{1,0:T(8,128)(2,1)}, bf16[3072,1024]{1,0:T(8,128)(2,1)}, bf16[3072,1024]{1,0:T(8,128)(2,1)}, bf16[...) custom-call(s32[3]{0:T(128)} %pad_add_fusion.info, ...), custom_call_target="tpu_custom_call", output_to_operand_aliasing={{0}: (21, {}), {1}: (22, {}), {2}: (23, {}), {3}: (24, {}),... | custom-call | flops 23085449216 | bytes 41975808 | tf_op jit(solution)/shard_map/layer/pallas_call | solution.py:251
  203.4 4.3 second_norm.4
  207.7 16.5 %weight_grad.3 = f32[1024,1536]{1,0:T(8,128)} custom-call(bf16[3072,1024]{1,0:T(8,128)(2,1)} %get-tuple-element.276.left, bf16[3072,2304]{1,0:T(8,128)(2,1)} %get-tuple-element.297.right, bf16[256,1024]{1,0:T(8,128)(2,1)} %get-tuple-element.311.refs_0_.own), custom_call_target="tpu_custom_call" | custom-call | flops 9663676416 | bytes 22020096 | tf_op jit(solution)/shard_map/weight_grad/pallas_call | solution.py:351
  230.2 4.3 second_norm.5
  234.5 12.7 %weight_grad.4 = bf16[1152,1024]{1,0:T(8,128)(2,1)} custom-call(bf16[3072,1152]{1,0:T(8,128)(2,1)} %get-tuple-element.294.left, bf16[3072,1024]{1,0:T(8,128)(2,1)} %get-tuple-element.282.grad.right, bf16[256,1024]{1,0:T(8,128)(2,1)} %get-tuple-element.293.refs_0_.own), custom_call_target="tpu_custom_call" | custom-call | flops 7247757312 | bytes 18087936 | tf_op jit(solution)/shard_map/weight_grad/pallas_call | solution.py:351
  247.3 3.2 convert_add_fusion.refs_0_
  261.0 10.4 %weight_grad.5 = bf16[1024,768]{1,0:T(8,128)(2,1)} custom-call(bf16[3072,1024]{1,0:T(8,128)(2,1)} %get-tuple-element.276.left, bf16[3072,2304]{1,0:T(8,128)(2,1)} %get-tuple-element.297.right, f32[512,1536]{1,0:T(8,128)} %copy-done.1), custom_call_target="tpu_custom_call" | custom-call | flops 4831838208 | bytes 14155776 | tf_op jit(solution)/shard_map/weight_grad/pallas_call | solution.py:351
  271.4 10.9 %collective-permute-done.24.right = bf16[512,512]{1,0:T(8,128)(2,1)} collective-permute-done((bf16[512,512]{1,0:T(8,128)(2,1)}, bf16[512,512]{1,0:T(8,128)(2,1)}, u32[]{:S(2)}, u32[]{:S(2)}) %collective-permute-start.24) | collective-permute-done | bytes 524320 | tf_op jit(solution)/shard_map/ppermute | solution.py:492
  282.3 4.1 place.4.refs_0_
  295.4 4.9 collective-permute-start.34
  300.3 4.1 place.5.refs_0_
  308.1 4.1 place.6.grl
  312.2 19.9 %own_backward.1 = (f32[1024,768]{1,0:T(8,128)}, f32[256,1024]{1,0:T(8,128)}, f32[8,256]{1,0:T(8,128)}) custom-call(s32[3]{0:T(128)} %pad_add_fusion.info, bf16[3072,1024]{1,0:T(8,128)(2,1)} %place.6.grl, bf16[3072,4096]{1,0:T(8,128)(2,1)} %get-tuple-element.304.p_b.p_c.p_x.conved, bf16[3072,4096]{1,0:T(8,128)(2,1)} %get-tuple-element.304.p_b.p_c.p_x.conved, ...), custom_call_target="tpu_custom_call" | custom-call | flops 8053063680 | bytes 24649728 | tf_op jit(solution)/shard_map/own_backward/pallas_call | solution.py:410
  349.6 28.2 %mixer_backward.2 = (f32[3072,1024]{1,0:T(8,128)}, f32[8,1024]{1,0:T(8,128)}, f32[8,1024]{1,0:T(8,128)}) custom-call(s32[3]{0:T(128)} %pad_add_fusion.info, bf16[3072,1024]{1,0:T(8,128)(2,1)} %place.6.grl, bf16[3072,1024]{1,0:T(8,128)(2,1)} %x.7, bf16[3072,4096]{1,0:T(8,128)(2,1)} %get-tuple-element.304.p_b.p_c.p_x.conved, ...), custom_call_target="tpu_custom_call" | custom-call | flops 12884901888 | bytes 33619968 | tf_op jit(solution)/shard_map/mixer_backward/pallas_call | solution.py:470
  379.4 3.6 collective-permute-done.37
  383.1 3.2 add_convert_fusion.refs_15_.own
  394.1 26.3 %mixer_backward.3 = (f32[3072,1024]{1,0:T(8,128)}, f32[8,1024]{1,0:T(8,128)}, f32[8,1024]{1,0:T(8,128)}) custom-call(s32[3]{0:T(128)} %pad_add_fusion.info, bf16[3072,1024]{1,0:T(8,128)(2,1)} %place.6.grl, bf16[3072,1024]{1,0:T(8,128)(2,1)} %x.7, bf16[3072,4096]{1,0:T(8,128)(2,1)} %get-tuple-element.304.p_b.p_c.p_x.conved, ...), custom_call_target="tpu_custom_call", output_to_operand_aliasing={{0}: (22, {})} | custom-call | flops 12884901888 | bytes 33619968 | tf_op jit(solution)/shard_map/mixer_backward/pallas_call | solution.py:470
  429.8 12.2 %collective-permute-done.49 = f32[1,1024]{1,0:T(1,128)S(1)} collective-permute-done((f32[1,1024]{1,0:T(1,128)S(1)}, f32[1,1024]{1,0:T(1,128)S(1)}, u32[]{:S(2)}, u32[]{:S(2)}) %collective-permute-start.49) | collective-permute-done | bytes 4128 | tf_op jit(solution)/shard_map/ppermute | solution.py:492
  441.9 3.7 collective-permute-start.51
  445.7 6.2 %collective-permute-done.51 = bf16[64,1024]{1,0:T(8,128)(2,1)S(1)} collective-permute-done((bf16[64,1024]{1,0:T(8,128)(2,1)S(1)}, bf16[64,1024]{1,0:T(8,128)(2,1)S(1)}, u32[]{:S(2)}, u32[]{:S(2)}) %collective-permute-start.51) | collective-permute-done | bytes 131104 | tf_op jit(solution)/shard_map/ppermute | solution.py:497
  453.8 9.8 %place.7 = bf16[3072,1024]{1,0:T(8,128)(2,1)} custom-call(s32[3]{0:T(128)} %pad_add_fusion.info, bf16[768,1024]{1,0:T(8,128)(2,1)} %copy-done.6, bf16[768,1024]{1,0:T(8,128)(2,1)} %copy-done.19, bf16[768,1024]{1,0:T(8,128)(2,1)} %copy-done.20, bf16[768,512]{1,0:T(8,128)(2,1)} %copy-done.30, bf16[768,512]{1,0:T(8,128)(2,1)} %copy-done.31), custom_call_target="tpu_custom_call" | custom-call | bytes 12582912 | tf_op jit(solution)/shard_map/place/pallas_call | solution.py:325
  463.8 13.5 %all-reduce.5.cloned.1.call-done = (bf16[1152,1024]{1,0:T(8,128)(2,1)}, bf16[1024,768]{1,0:T(8,128)(2,1)}) async-done(((bf16[1152,1024]{1,0:T(8,128)(2,1)}, bf16[1024,768]{1,0:T(8,128)(2,1)}), (bf16[1152,1024]{1,0:T(8,128)(2,1)}, bf16[1024,768]{1,0:T(8,128)(2,1)})) %all-reduce.5.cloned.1.call-update) | async-done | bytes 3932176 | tf_op jit(solution)/shard_map/psum | solution.py:690
  483.3 4.4 pad_maximum_fusion
  491.7 2.7 convert_element_type.159
  497.7 2.8 collective-permute-done.57
  (304 shorter events, 110.3 us)
Async XLA Ops:
  7.2 470.1 %all-reduce.5.cloned.1.call-start = ((), (), s32[]{:S(2)}) async-start(), calls=%async_computation | async-start | bytes 7864320 | tf_op jit(solution)/shard_map/psum | solution.py:690
  10.4 26.3 %collective-permute-start.2 = (bf16[4112,128]{1,0:T(8,128)(2,1)S(1)}, bf16[4112,128]{1,0:T(8,128)(2,1)S(1)}, u32[]{:S(2)}, u32[]{:S(2)}) collective-permute-start(bf16[4112,128]{1,0:T(8,128)(2,1)S(1)} %concatenate.46), channel_id=1, source_target_pairs={{0,2},{1,3},{2,0},{3,1},{4,6},{5,7},{6,4},{7,5},{8,10},{9,11},{10,... | collective-permute-start | bytes 3158024 | tf_op jit(solution)/shard_map/ppermute | solution.py:492
  13.4 25.1 %collective-permute-start = (bf16[4112,128]{1,0:T(8,128)(2,1)S(1)}, bf16[4112,128]{1,0:T(8,128)(2,1)S(1)}, u32[]{:S(2)}, u32[]{:S(2)}) collective-permute-start(bf16[4112,128]{1,0:T(8,128)(2,1)S(1)} %concatenate.46), channel_id=1, source_target_pairs={{0,1},{1,0},{2,3},{3,2},{4,5},{5,4},{6,7},{7,6},{8,9},{9,8},{10,11... | collective-permute-start | bytes 3158024 | tf_op jit(solution)/shard_map/ppermute | solution.py:492
  101.7 45.2 %collective-permute-start.10 = (bf16[256,1024]{1,0:T(8,128)(2,1)}, bf16[256,1024]{1,0:T(8,128)(2,1)S(1)}, u32[]{:S(2)}, u32[]{:S(2)}) collective-permute-start(bf16[256,1024]{1,0:T(8,128)(2,1)} %get-tuple-element.236), channel_id=1, source_target_pairs={{0,1},{1,0},{2,3},{3,2},{4,5},{5,4},{6,7},{7,6},{8,9},{9,8},{10,11... | collective-permute-start | bytes 1572872 | tf_op jit(solution)/shard_map/ppermute | solution.py:492
  102.8 44.1 %collective-permute-start.11 = (bf16[256,1024]{1,0:T(8,128)(2,1)}, bf16[256,1024]{1,0:T(8,128)(2,1)S(1)}, u32[]{:S(2)}, u32[]{:S(2)}) collective-permute-start(bf16[256,1024]{1,0:T(8,128)(2,1)} %get-tuple-element.237), channel_id=1, source_target_pairs={{0,2},{1,3},{2,0},{3,1},{4,6},{5,7},{6,4},{7,5},{8,10},{9,11},{10,... | collective-permute-start | bytes 1572872 | tf_op jit(solution)/shard_map/ppermute | solution.py:492
  103.8 43.1 %collective-permute-start.9 = (bf16[256,1024]{1,0:T(8,128)(2,1)}, bf16[256,1024]{1,0:T(8,128)(2,1)S(1)}, u32[]{:S(2)}, u32[]{:S(2)}) collective-permute-start(bf16[256,1024]{1,0:T(8,128)(2,1)} %get-tuple-element.235), channel_id=1, source_target_pairs={{0,3},{1,2},{2,1},{3,0},{4,7},{5,6},{6,5},{7,4},{8,11},{9,10},{10,... | collective-permute-start | bytes 1572872 | tf_op jit(solution)/shard_map/ppermute | solution.py:492
  152.3 47.4 %collective-permute-start.12 = (bf16[256,1024]{1,0:T(8,128)(2,1)}, bf16[256,1024]{1,0:T(8,128)(2,1)S(1)}, u32[]{:S(2)}, u32[]{:S(2)}) collective-permute-start(bf16[256,1024]{1,0:T(8,128)(2,1)} %get-tuple-element.254.refs_31_.own), channel_id=1, source_target_pairs={{0,1},{1,0},{2,3},{3,2},{4,5},{5,4},{6,7},{7,6},{8,9},{9,8},{10,11... | collective-permute-start | bytes 1572872 | tf_op jit(solution)/shard_map/ppermute | solution.py:492
  153.4 46.4 %collective-permute-start.13 = (bf16[256,1024]{1,0:T(8,128)(2,1)}, bf16[256,1024]{1,0:T(8,128)(2,1)S(1)}, u32[]{:S(2)}, u32[]{:S(2)}) collective-permute-start(bf16[256,1024]{1,0:T(8,128)(2,1)} %get-tuple-element.254.refs_31_.own), channel_id=1, source_target_pairs={{0,2},{1,3},{2,0},{3,1},{4,6},{5,7},{6,4},{7,5},{8,10},{9,11},{10,... | collective-permute-start | bytes 1572872 | tf_op jit(solution)/shard_map/ppermute | solution.py:492
  154.4 45.4 %collective-permute-start.14 = (bf16[256,1024]{1,0:T(8,128)(2,1)S(1)}, bf16[256,1024]{1,0:T(8,128)(2,1)S(1)}, u32[]{:S(2)}, u32[]{:S(2)}) collective-permute-start(bf16[256,1024]{1,0:T(8,128)(2,1)S(1)} %copy-done.57), channel_id=1, source_target_pairs={{0,3},{1,2},{2,1},{3,0},{4,7},{5,6},{6,5},{7,4},{8,11},{9,10},{10,... | collective-permute-start | bytes 1572872 | tf_op jit(solution)/shard_map/ppermute | solution.py:492
  155.8 44.0 %collective-permute-start.15 = (bf16[256,1024]{1,0:T(8,128)(2,1)S(1)}, bf16[256,1024]{1,0:T(8,128)(2,1)S(1)}, u32[]{:S(2)}, u32[]{:S(2)}) collective-permute-start(bf16[256,1024]{1,0:T(8,128)(2,1)S(1)} %copy-done.56), channel_id=1, source_target_pairs={{0,1},{1,0},{2,3},{3,2},{4,5},{5,4},{6,7},{7,6},{8,9},{9,8},{10,11... | collective-permute-start | bytes 1572872 | tf_op jit(solution)/shard_map/ppermute | solution.py:492
  156.9 43.0 %collective-permute-start.16 = (bf16[256,1024]{1,0:T(8,128)(2,1)S(1)}, bf16[256,1024]{1,0:T(8,128)(2,1)S(1)}, u32[]{:S(2)}, u32[]{:S(2)}) collective-permute-start(bf16[256,1024]{1,0:T(8,128)(2,1)S(1)} %copy-done.55), channel_id=1, source_target_pairs={{0,2},{1,3},{2,0},{3,1},{4,6},{5,7},{6,4},{7,5},{8,10},{9,11},{10,... | collective-permute-start | bytes 1572872 | tf_op jit(solution)/shard_map/ppermute | solution.py:492
  199.9 24.3 %collective-permute-start.17 = (bf16[256,1024]{1,0:T(8,128)(2,1)}, bf16[256,1024]{1,0:T(8,128)(2,1)S(1)}, u32[]{:S(2)}, u32[]{:S(2)}) collective-permute-start(bf16[256,1024]{1,0:T(8,128)(2,1)} %get-tuple-element.285), channel_id=1, source_target_pairs={{0,3},{1,2},{2,1},{3,0},{4,7},{5,6},{6,5},{7,4},{8,11},{9,10},{10,... | collective-permute-start | bytes 1572872 | tf_op jit(solution)/shard_map/ppermute | solution.py:492
  201.4 23.3 %collective-permute-start.18 = (bf16[256,1024]{1,0:T(8,128)(2,1)}, bf16[256,1024]{1,0:T(8,128)(2,1)S(1)}, u32[]{:S(2)}, u32[]{:S(2)}) collective-permute-start(bf16[256,1024]{1,0:T(8,128)(2,1)} %get-tuple-element.286), channel_id=1, source_target_pairs={{0,1},{1,0},{2,3},{3,2},{4,5},{5,4},{6,7},{7,6},{8,9},{9,8},{10,11... | collective-permute-start | bytes 1572872 | tf_op jit(solution)/shard_map/ppermute | solution.py:492
  251.5 30.8 %collective-permute-start.28 = (bf16[256,1536]{1,0:T(8,128)(2,1)}, bf16[256,1536]{1,0:T(8,128)(2,1)}, u32[]{:S(2)}, u32[]{:S(2)}) collective-permute-start(bf16[256,1536]{1,0:T(8,128)(2,1)} %dynamic-slice_convert_fusion.2), channel_id=1, source_target_pairs={{0,8},{4,12},{8,0},{12,4},{16,24},{20,28},{24,16},{28,20},{1,9},{5... | collective-permute-start | bytes 2359304 | tf_op jit(solution)/shard_map/ppermute | solution.py:497
  258.0 24.3 %collective-permute-start.24 = (bf16[512,512]{1,0:T(8,128)(2,1)}, bf16[512,512]{1,0:T(8,128)(2,1)}, u32[]{:S(2)}, u32[]{:S(2)}) collective-permute-start(bf16[512,512]{1,0:T(8,128)(2,1)} %pad_maximum_fusion.7), channel_id=1, source_target_pairs={{0,2},{1,3},{2,0},{3,1},{4,6},{5,7},{6,4},{7,5},{8,10},{9,11},{10,... | collective-permute-start | bytes 1572872 | tf_op jit(solution)/shard_map/ppermute | solution.py:492
  295.4 36.7 %collective-permute-start.34 = (bf16[256,1536]{1,0:T(8,128)(2,1)}, bf16[256,1536]{1,0:T(8,128)(2,1)}, u32[]{:S(2)}, u32[]{:S(2)}) collective-permute-start(bf16[256,1536]{1,0:T(8,128)(2,1)} %add_convert_fusion.4), channel_id=1, source_target_pairs={{0,24},{4,28},{8,16},{12,20},{16,8},{20,12},{24,0},{28,4},{1,25},{... | collective-permute-start | bytes 2359304 | tf_op jit(solution)/shard_map/ppermute | solution.py:497
  305.8 26.4 %collective-permute-start.32 = (bf16[768,512]{1,0:T(8,128)(2,1)}, bf16[768,512]{1,0:T(8,128)(2,1)}, u32[]{:S(2)}, u32[]{:S(2)}) collective-permute-start(bf16[768,512]{1,0:T(8,128)(2,1)} %get-tuple-element.419), channel_id=1, source_target_pairs={{0,1},{1,0},{2,3},{3,2},{4,5},{5,4},{6,7},{7,6},{8,9},{9,8},{10,11... | collective-permute-start | bytes 2359304 | tf_op jit(solution)/shard_map/ppermute | solution.py:492
  306.3 25.9 %collective-permute-start.33 = (bf16[768,512]{1,0:T(8,128)(2,1)}, bf16[768,512]{1,0:T(8,128)(2,1)}, u32[]{:S(2)}, u32[]{:S(2)}) collective-permute-start(bf16[768,512]{1,0:T(8,128)(2,1)} %get-tuple-element.418), channel_id=1, source_target_pairs={{0,2},{1,3},{2,0},{3,1},{4,6},{5,7},{6,4},{7,5},{8,10},{9,11},{10,... | collective-permute-start | bytes 2359304 | tf_op jit(solution)/shard_map/ppermute | solution.py:492
  334.6 43.2 %collective-permute-start.41 = (bf16[256,1536]{1,0:T(8,128)(2,1)}, bf16[256,1536]{1,0:T(8,128)(2,1)}, u32[]{:S(2)}, u32[]{:S(2)}) collective-permute-start(bf16[256,1536]{1,0:T(8,128)(2,1)} %add_convert_fusion.1), channel_id=1, source_target_pairs={{0,8},{4,12},{8,0},{12,4},{16,24},{20,28},{24,16},{28,20},{1,9},{5... | collective-permute-start | bytes 2359304 | tf_op jit(solution)/shard_map/ppermute | solution.py:497
  342.4 37.1 %collective-permute-start.38 = (bf16[768,1024]{1,0:T(8,128)(2,1)}, bf16[768,1024]{1,0:T(8,128)(2,1)}, u32[]{:S(2)}, u32[]{:S(2)}) collective-permute-start(bf16[768,1024]{1,0:T(8,128)(2,1)} %pad_maximum_fusion.3), channel_id=1, source_target_pairs={{0,2},{1,3},{2,0},{3,1},{4,6},{5,7},{6,4},{7,5},{8,10},{9,11},{10,... | collective-permute-start | bytes 4718600 | tf_op jit(solution)/shard_map/ppermute | solution.py:492
  346.0 37.0 %collective-permute-start.37 = (bf16[768,1024]{1,0:T(8,128)(2,1)}, bf16[768,1024]{1,0:T(8,128)(2,1)}, u32[]{:S(2)}, u32[]{:S(2)}) collective-permute-start(bf16[768,1024]{1,0:T(8,128)(2,1)} %pad_maximum_fusion.2), channel_id=1, source_target_pairs={{0,1},{1,0},{2,3},{3,2},{4,5},{5,4},{6,7},{7,6},{8,9},{9,8},{10,11... | collective-permute-start | bytes 4718600 | tf_op jit(solution)/shard_map/ppermute | solution.py:492
  347.2 30.6 %collective-permute-start.39 = (bf16[260,768]{1,0:T(8,128)(2,1)S(1)}, bf16[260,768]{1,0:T(8,128)(2,1)S(1)}, u32[]{:S(2)}, u32[]{:S(2)}) collective-permute-start(bf16[260,768]{1,0:T(8,128)(2,1)S(1)} %dynamic-slice_convert_fusion.3), channel_id=1, source_target_pairs={{0,8},{4,12},{8,0},{12,4},{16,24},{20,28},{24,16},{28,20},{1,9},{5... | collective-permute-start | bytes 1198088 | tf_op jit(solution)/shard_map/ppermute | solution.py:497
  348.5 29.3 %collective-permute-start.40 = (bf16[64,1024]{1,0:T(8,128)(2,1)S(1)}, bf16[64,1024]{1,0:T(8,128)(2,1)S(1)}, u32[]{:S(2)}, u32[]{:S(2)}) collective-permute-start(bf16[64,1024]{1,0:T(8,128)(2,1)S(1)} %dynamic-slice_convert_fusion.5), channel_id=1, source_target_pairs={{0,8},{4,12},{8,0},{12,4},{16,24},{20,28},{24,16},{28,20},{1,9},{5... | collective-permute-start | bytes 393224 | tf_op jit(solution)/shard_map/ppermute | solution.py:497
  386.4 36.0 %collective-permute-start.42 = (bf16[768,1024]{1,0:T(8,128)(2,1)S(1)}, bf16[768,1024]{1,0:T(8,128)(2,1)S(1)}, u32[]{:S(2)}, u32[]{:S(2)}) collective-permute-start(bf16[768,1024]{1,0:T(8,128)(2,1)S(1)} %add_convert_fusion.refs_15_.own), channel_id=1, source_target_pairs={{0,1},{1,0},{2,3},{3,2},{4,5},{5,4},{6,7},{7,6},{8,9},{9,8},{10,11... | collective-permute-start | bytes 4718600 | tf_op jit(solution)/shard_map/ppermute | solution.py:492
  387.4 35.6 %collective-permute-start.43 = (bf16[768,1024]{1,0:T(8,128)(2,1)S(1)}, bf16[768,1024]{1,0:T(8,128)(2,1)S(1)}, u32[]{:S(2)}, u32[]{:S(2)}) collective-permute-start(bf16[768,1024]{1,0:T(8,128)(2,1)S(1)} %add_convert_fusion.refs_15_.own), channel_id=1, source_target_pairs={{0,2},{1,3},{2,0},{3,1},{4,6},{5,7},{6,4},{7,5},{8,10},{9,11},{10,... | collective-permute-start | bytes 4718600 | tf_op jit(solution)/shard_map/ppermute | solution.py:492
  388.4 34.0 %collective-permute-start.46 = (f32[1,1024]{1,0:T(1,128)S(1)}, f32[1,1024]{1,0:T(1,128)S(1)}, u32[]{:S(2)}, u32[]{:S(2)}) collective-permute-start(f32[1,1024]{1,0:T(1,128)S(1)} %add_add_fusion), channel_id=1, source_target_pairs={{0,1},{1,0},{2,3},{3,2},{4,5},{5,4},{6,7},{7,6},{8,9},{9,8},{10,11... | collective-permute-start | bytes 12296 | tf_op jit(solution)/shard_map/ppermute | solution.py:492
  390.1 32.3 %collective-permute-start.44 = (bf16[260,768]{1,0:T(8,128)(2,1)S(1)}, bf16[260,768]{1,0:T(8,128)(2,1)S(1)}, u32[]{:S(2)}, u32[]{:S(2)}) collective-permute-start(bf16[260,768]{1,0:T(8,128)(2,1)S(1)} %add_convert_fusion.6.refs_13_), channel_id=1, source_target_pairs={{0,24},{4,28},{8,16},{12,20},{16,8},{20,12},{24,0},{28,4},{1,25},{... | collective-permute-start | bytes 1198088 | tf_op jit(solution)/shard_map/ppermute | solution.py:497
  392.8 29.5 %collective-permute-start.45 = (bf16[64,1024]{1,0:T(8,128)(2,1)S(1)}, bf16[64,1024]{1,0:T(8,128)(2,1)S(1)}, u32[]{:S(2)}, u32[]{:S(2)}) collective-permute-start(bf16[64,1024]{1,0:T(8,128)(2,1)S(1)} %add_convert_fusion.8.refs_14_), channel_id=1, source_target_pairs={{0,24},{4,28},{8,16},{12,20},{16,8},{20,12},{24,0},{28,4},{1,25},{... | collective-permute-start | bytes 393224 | tf_op jit(solution)/shard_map/ppermute | solution.py:497
  423.0 28.9 %collective-permute-start.47 = (bf16[768,512]{1,0:T(8,128)(2,1)S(1)}, bf16[768,512]{1,0:T(8,128)(2,1)S(1)}, u32[]{:S(2)}, u32[]{:S(2)}) collective-permute-start(bf16[768,512]{1,0:T(8,128)(2,1)S(1)} %slice.124), channel_id=1, source_target_pairs={{0,1},{1,0},{2,3},{3,2},{4,5},{5,4},{6,7},{7,6},{8,9},{9,8},{10,11... | collective-permute-start | bytes 2359304 | tf_op jit(solution)/shard_map/ppermute | solution.py:492
  424.3 27.7 %collective-permute-start.48 = (bf16[768,512]{1,0:T(8,128)(2,1)S(1)}, bf16[768,512]{1,0:T(8,128)(2,1)S(1)}, u32[]{:S(2)}, u32[]{:S(2)}) collective-permute-start(bf16[768,512]{1,0:T(8,128)(2,1)S(1)} %slice.125), channel_id=1, source_target_pairs={{0,2},{1,3},{2,0},{3,1},{4,6},{5,7},{6,4},{7,5},{8,10},{9,11},{10,... | collective-permute-start | bytes 2359304 | tf_op jit(solution)/shard_map/ppermute | solution.py:492
  425.8 26.1 %collective-permute-start.50 = (bf16[260,768]{1,0:T(8,128)(2,1)S(1)}, bf16[260,768]{1,0:T(8,128)(2,1)S(1)}, u32[]{:S(2)}, u32[]{:S(2)}) collective-permute-start(bf16[260,768]{1,0:T(8,128)(2,1)S(1)} %add_convert_fusion.5), channel_id=1, source_target_pairs={{0,8},{4,12},{8,0},{12,4},{16,24},{20,28},{24,16},{28,20},{1,9},{5... | collective-permute-start | bytes 1198088 | tf_op jit(solution)/shard_map/ppermute | solution.py:497
  428.6 35.1 %collective-permute-start.55 = (bf16[512,1536]{1,0:T(8,128)(2,1)S(1)}, bf16[512,1536]{1,0:T(8,128)(2,1)}, u32[]{:S(2)}, u32[]{:S(2)}) collective-permute-start(bf16[512,1536]{1,0:T(8,128)(2,1)S(1)} %pad_maximum_fusion.4), channel_id=1, source_target_pairs={{0,4},{4,0},{8,12},{12,8},{16,20},{20,16},{24,28},{28,24},{1,5},{5... | collective-permute-start | bytes 4718600 | tf_op jit(solution)/shard_map/ppermute | solution.py:497
  (88 other events, 944.5 us)
Sparse Core Ops, SparseCore 0:
  349.7 127.5 all-reduce.4

commit v4 on v3

--- a/solution.py
+++ b/solution.py
@@ -640,8 +640,7 @@
         terms2 = exchange(blocks2)
         share1, norm1 = second_norm(1, info, terms1, resid, grad_low, gain_two)
         sides1 = to_sides(share1)
-        split_at = 2 * padded * 2 // 3
-        g_first = weight_grad(h2, grads, [share1], 0, split_at)
+        g_first = weight_grad(h2, grads, [share1])
         g_first, terms2, activ, share1, grads = tie((g_first, terms2, activ, share1, grads))
 
         first = SeqSum(g_first)
@@ -655,9 +654,7 @@
         first.near()
         corner01 = corners([sides0, sides1])
         next_c = shifted(proj[:16, width:2 * width], -1)
-        g_second = weight_grad(h2, grads, [first.value], split_at, 2 * padded - split_at, BF16)
-        g_second, corner01, sides2, next_c, state, forward = tie(
-            (g_second, corner01, sides2, next_c, first.state(), kept[8:12]))
+        corner01, sides2, next_c, state, forward = tie((corner01, sides2, next_c, first.state(), kept[8:12]))
 
         first.put(state)
         first.cross()
@@ -685,9 +682,9 @@
         tail_out = SeqSum(g_out)
         tail_out.pair()
         first.back()
-        g_down, g_second, state, state2 = tie((g_down, g_second, tail_in.state(), tail_out.state()))
-
-        g_down, g_second = lax.psum((g_down, g_second), "seq")
+        g_down, state, state2 = tie((g_down, tail_in.state(), tail_out.state()))
+
+        g_down = lax.psum(g_down, "seq")
         tail_in.put(state)
         tail_out.put(state2)
         tail_in.near()
@@ -708,8 +705,8 @@
         g_norm_two = norm0 + norm1 + norm2
         g_norm_two = g_norm_two + swap(g_norm_two, 1)
         grad_inputs, norm_early, _ = back(1, (rest, grad_inputs), [tail_in.value, tail_out.value, final])
-        grad_inputs, norm_early, sides, state, state2, g_norm_two = tie((
-            grad_inputs, norm_early, sides, tail_in.state(), tail_out.state(), g_norm_two))
+        grad_inputs, norm_early, sides, state, state2, g_norm_two, g_down = tie((
+            grad_inputs, norm_early, sides, tail_in.state(), tail_out.state(), g_norm_two, g_down))
 
         tail_in.put(state)
         tail_out.put(state2)
@@ -728,7 +725,7 @@
         first.share()
         output = place(0, CHUNKS, info, [final, *sides, *corner], rows, None)
         output, norms, state, state2, state3 = tie((output, norms, tail_in.state(), tail_out.state(), first.state()))
-        g_down, g_second, _ = tie((g_down, g_second, output))
+        g_down, _ = tie((g_down, output))
 
         tail_in.put(state)
         tail_out.put(state2)
@@ -741,7 +738,7 @@
         norms = norms + swap_seq(norms, 6)
         g_norm_one, g_norm_two = norms[0], norms[1]
         g_first = first.result()
-        g_gu = jnp.concatenate([g_first, g_second.astype(F32)], axis=1)
+        g_gu = g_first
         g_down = g_down.astype(F32)
     else:
         kept, finals, shares, g_norm_two = [], [], [], 0.0

time: 516 us -> 572 us (1.11)
  starting transfers between devices: 69.8 us -> 106 us
  waiting for transfers between devices: 86.9 us -> 106 us
  local copies, waits for them, and re-layouts: 19.4 us -> 28.2 us
  Pallas kernels: 274 us -> 268 us
    ppermute x22, starting transfers between devices: 24.8 us -> 62.6 us  [swap_seq(): return lax.ppermute(value, 'seq', [(i, i ^ step) for i in range(count)])]
    ppermute x33, waiting for transfers between devices: 64.3 us -> 101 us  [swap(): return lax.ppermute(value, 'tp', [(i, i ^ step) for i in range(count)])]
    psum x1, waiting for transfers between devices: 13.5 us -> 0.02 us  [per_device(): g_down = lax.psum(g_down, 'seq')]
    pallas_call x3 -> x2, Pallas kernels: 39.6 us -> 34.2 us  [weight_grad(): pl.pallas_call(weight_grad_body, grid=(wide // tile,), in_specs=[resident...]
  transfers between devices with their start and end apart: 59 -> 59, of which waited for: 14 -> 12; matrix products, arithmetic and copies ran while one was open for 9% -> 7% of each run, Pallas kernels for 44% -> 39%
where the time goes in v4:
time: 572 us; the launch traced here: 564 us
  Pallas kernels  268 us (47%)
  starting transfers between devices  106 us (19%)
  waiting for transfers between devices  106 us (19%)
  other arithmetic  39.7 us (7%)
  local copies, waits for them, and re-layouts  28.2 us (5%)
  between operations  15.8 us (3%)
    pallas_call x3, Pallas kernels, layer(): pl.pallas_call(functools.partial(layer_body, slot, own, layout, chunk * s...  125 us
    ppermute x33, waiting for transfers between devices, swap(): return lax.ppermute(value, 'tp', [(i, i ^ step) for i in range(count)])  101 us
    ppermute x22, starting transfers between devices, swap_seq(): return lax.ppermute(value, 'seq', [(i, i ^ step) for i in range(count)])  62.6 us
    pallas_call x2, Pallas kernels, mixer_backward(): pl.pallas_call(functools.partial(mixer_backward_body, slot, layout, len(w...  54.3 us
    ppermute x33, starting transfers between devices, swap(): return lax.ppermute(value, 'tp', [(i, i ^ step) for i in range(count)])  38.2 us
    pallas_call x2, Pallas kernels, weight_grad(): pl.pallas_call(weight_grad_body, grid=(wide // tile,), in_specs=[resident...  34.2 us
    pallas_call x4, Pallas kernels, place(): pl.pallas_call(place_body, grid_spec=pltpu.PrefetchScalarGridSpec(num_sca...  22.4 us
    pallas_call x1, Pallas kernels, own_backward(): pl.pallas_call(functools.partial(own_backward_body, slot), grid_spec=pltp...  19.9 us
  transfers between devices with their start and end apart: 59, of which 12 were waited for; matrix products, arithmetic and copies ran while one was open for 7% of the time, Pallas kernels for 39%

profile of v4, /device:TPU:0, one launch (start us, length us, event | category | flops | bytes accessed | tf_op | source)
XLA Modules:
  0.0 564.2 jit_solution(2773557659936223246)
XLA Ops:
  10.4 3.0 collective-permute-start.2
  14.9 21.8 %collective-permute-done.2.refs_10_.refs_5_ = bf16[4112,128]{1,0:T(8,128)(2,1)S(1)} collective-permute-done((bf16[4112,128]{1,0:T(8,128)(2,1)S(1)}, bf16[4112,128]{1,0:T(8,128)(2,1)S(1)}, u32[]{:S(2)}, u32[]{:S(2)}) %collective-permute-start.2) | collective-permute-done | bytes 1052704 | tf_op jit(solution)/shard_map/ppermute | solution.py:492
  40.6 9.5 %collective-permute-done.5.refs_13_.refs_8_ = bf16[2064,128]{1,0:T(8,128)(2,1)} collective-permute-done((bf16[2064,128]{1,0:T(8,128)(2,1)S(1)}, bf16[2064,128]{1,0:T(8,128)(2,1)}, u32[]{:S(2)}, u32[]{:S(2)}) %collective-permute-start.5) | collective-permute-done | bytes 528416 | tf_op jit(solution)/shard_map/ppermute | solution.py:492
  60.4 41.3 %layer.3 = (bf16[3072,4096]{1,0:T(8,128)(2,1)}, bf16[3072,256]{1,0:T(8,128)(2,1)}, bf16[3072,1024]{1,0:T(8,128)(2,1)}, bf16[3072,1024]{1,0:T(8,128)(2,1)}, bf16[...) custom-call(s32[3]{0:T(128)} %pad_add_fusion.info, ...), custom_call_target="tpu_custom_call" | custom-call | flops 23085449216 | bytes 41975808 | tf_op jit(solution)/shard_map/layer/pallas_call | solution.py:251
  105.2 41.6 %layer.4 = (bf16[3072,4096]{1,0:T(8,128)(2,1)}, bf16[3072,256]{1,0:T(8,128)(2,1)}, bf16[3072,1024]{1,0:T(8,128)(2,1)}, bf16[3072,1024]{1,0:T(8,128)(2,1)}, bf16[...) custom-call(s32[3]{0:T(128)} %pad_add_fusion.info, ...), custom_call_target="tpu_custom_call", output_to_operand_aliasing={{0}: (21, {}), {1}: (22, {}), {2}: (23, {}), {3}: (24, {}),... | custom-call | flops 23085449216 | bytes 41975808 | tf_op jit(solution)/shard_map/layer/pallas_call | solution.py:251
  147.9 4.3 second_norm.3
  157.8 41.7 %layer.5 = (bf16[3072,4096]{1,0:T(8,128)(2,1)}, bf16[3072,256]{1,0:T(8,128)(2,1)}, bf16[3072,1024]{1,0:T(8,128)(2,1)}, bf16[3072,1024]{1,0:T(8,128)(2,1)}, bf16[...) custom-call(s32[3]{0:T(128)} %pad_add_fusion.info, ...), custom_call_target="tpu_custom_call", output_to_operand_aliasing={{0}: (21, {}), {1}: (22, {}), {2}: (23, {}), {3}: (24, {}),... | custom-call | flops 23085449216 | bytes 41975808 | tf_op jit(solution)/shard_map/layer/pallas_call | solution.py:251
  203.2 4.3 second_norm.4
  207.4 21.5 %weight_grad.2 = f32[1024,2304]{1,0:T(8,128)} custom-call(bf16[3072,1024]{1,0:T(8,128)(2,1)} %get-tuple-element.272.left, bf16[3072,2304]{1,0:T(8,128)(2,1)} %get-tuple-element.273.right, bf16[256,1024]{1,0:T(8,128)(2,1)} %get-tuple-element.305.refs_0_.own), custom_call_target="tpu_custom_call" | custom-call | flops 14495514624 | bytes 29884416 | tf_op jit(solution)/shard_map/weight_grad/pallas_call | solution.py:351
  229.0 3.1 dynamic-slice_convert_fusion
  234.3 4.2 second_norm.5
  238.5 12.7 %weight_grad.3 = bf16[1152,1024]{1,0:T(8,128)(2,1)} custom-call(bf16[3072,1152]{1,0:T(8,128)(2,1)} %get-tuple-element.291.left, bf16[3072,1024]{1,0:T(8,128)(2,1)} %get-tuple-element.278.grad.right, bf16[256,1024]{1,0:T(8,128)(2,1)} %get-tuple-element.289.refs_0_.own), custom_call_target="tpu_custom_call" | custom-call | flops 7247757312 | bytes 18087936 | tf_op jit(solution)/shard_map/weight_grad/pallas_call | solution.py:351
  251.3 3.5 convert_add_fusion
  267.8 7.2 %collective-permute-done.25.side = bf16[256,1024]{1,0:T(8,128)(2,1)S(1)} collective-permute-done((bf16[256,1024]{1,0:T(8,128)(2,1)}, bf16[256,1024]{1,0:T(8,128)(2,1)S(1)}, u32[]{:S(2)}, u32[]{:S(2)}) %collective-permute-start.25) | collective-permute-done | bytes 524320 | tf_op jit(solution)/shard_map/ppermute | solution.py:492
  276.2 11.1 %collective-permute-done.24.right = bf16[512,512]{1,0:T(8,128)(2,1)S(1)} collective-permute-done((bf16[512,512]{1,0:T(8,128)(2,1)}, bf16[512,512]{1,0:T(8,128)(2,1)S(1)}, u32[]{:S(2)}, u32[]{:S(2)}) %collective-permute-start.24) | collective-permute-done | bytes 524320 | tf_op jit(solution)/shard_map/ppermute | solution.py:492
  292.9 10.8 %collective-permute-start.34 = (bf16[256,2304]{1,0:T(8,128)(2,1)}, bf16[256,2304]{1,0:T(8,128)(2,1)}, u32[]{:S(2)}, u32[]{:S(2)}) collective-permute-start(bf16[256,2304]{1,0:T(8,128)(2,1)} %add_convert_fusion.2), channel_id=1, source_target_pairs={{0,24},{4,28},{8,16},{12,20},{16,8},{20,12},{24,0},{28,4},{1,25},{... | collective-permute-start | bytes 3538952 | tf_op jit(solution)/shard_map/ppermute | solution.py:497
  303.7 4.1 place.4.refs_0_
  309.9 4.3 place.5.refs_0_
  319.1 4.1 place.6.grl
  323.2 19.9 %own_backward.1 = (f32[1024,768]{1,0:T(8,128)}, f32[256,1024]{1,0:T(8,128)}, f32[8,256]{1,0:T(8,128)}) custom-call(s32[3]{0:T(128)} %pad_add_fusion.info, bf16[3072,1024]{1,0:T(8,128)(2,1)} %place.6.grl, bf16[3072,4096]{1,0:T(8,128)(2,1)} %get-tuple-element.296.p_b.p_c.p_x.conved, bf16[3072,4096]{1,0:T(8,128)(2,1)} %get-tuple-element.296.p_b.p_c.p_x.conved, ...), custom_call_target="tpu_custom_call" | custom-call | flops 8053063680 | bytes 24649728 | tf_op jit(solution)/shard_map/own_backward/pallas_call | solution.py:410
  343.2 3.1 add_convert_fusion.1
  346.3 15.8 %collective-permute-start.41 = (bf16[256,2304]{1,0:T(8,128)(2,1)}, bf16[256,2304]{1,0:T(8,128)(2,1)}, u32[]{:S(2)}, u32[]{:S(2)}) collective-permute-start(bf16[256,2304]{1,0:T(8,128)(2,1)} %add_convert_fusion.1), channel_id=1, source_target_pairs={{0,8},{4,12},{8,0},{12,4},{16,24},{20,28},{24,16},{28,20},{1,9},{5... | collective-permute-start | bytes 3538952 | tf_op jit(solution)/shard_map/ppermute | solution.py:497
  362.5 24.7 %collective-permute-start.35 = (bf16[520,768]{1,0:T(8,128)(2,1)S(1)}, bf16[520,768]{1,0:T(8,128)(2,1)S(1)}, u32[]{:S(2)}, u32[]{:S(2)}) collective-permute-start(bf16[520,768]{1,0:T(8,128)(2,1)S(1)} %dynamic-slice_convert_fusion.2), channel_id=1, source_target_pairs={{0,4},{4,0},{8,12},{12,8},{16,20},{20,16},{24,28},{28,24},{1,5},{5... | collective-permute-start | bytes 2396168 | tf_op jit(solution)/shard_map/ppermute | solution.py:497
  397.4 28.0 %mixer_backward.2 = (f32[3072,1024]{1,0:T(8,128)}, f32[8,1024]{1,0:T(8,128)}, f32[8,1024]{1,0:T(8,128)}) custom-call(s32[3]{0:T(128)} %pad_add_fusion.info, bf16[3072,1024]{1,0:T(8,128)(2,1)} %place.6.grl, bf16[3072,1024]{1,0:T(8,128)(2,1)} %x.7, bf16[3072,4096]{1,0:T(8,128)(2,1)} %get-tuple-element.296.p_b.p_c.p_x.conved, ...), custom_call_target="tpu_custom_call" | custom-call | flops 12884901888 | bytes 33619968 | tf_op jit(solution)/shard_map/mixer_backward/pallas_call | solution.py:470
  426.6 5.1 collective-permute-done.37
  431.7 3.1 add_convert_fusion.refs_15_.own
  444.0 27.0 %collective-permute-done.46 = f32[1,1024]{1,0:T(1,128)S(1)} collective-permute-done((f32[1,1024]{1,0:T(1,128)S(1)}, f32[1,1024]{1,0:T(1,128)S(1)}, u32[]{:S(2)}, u32[]{:S(2)}) %collective-permute-start.46) | collective-permute-done | bytes 4128 | tf_op jit(solution)/shard_map/ppermute | solution.py:492
  472.3 26.4 %mixer_backward.3 = (f32[3072,1024]{1,0:T(8,128)}, f32[8,1024]{1,0:T(8,128)}, f32[8,1024]{1,0:T(8,128)}) custom-call(s32[3]{0:T(128)} %pad_add_fusion.info, bf16[3072,1024]{1,0:T(8,128)(2,1)} %place.6.grl, bf16[3072,1024]{1,0:T(8,128)(2,1)} %x.7, bf16[3072,4096]{1,0:T(8,128)(2,1)} %get-tuple-element.296.p_b.p_c.p_x.conved, ...), custom_call_target="tpu_custom_call", output_to_operand_aliasing={{0}: (22, {})} | custom-call | flops 12884901888 | bytes 33619968 | tf_op jit(solution)/shard_map/mixer_backward/pallas_call | solution.py:470
  505.4 13.6 %collective-permute-done.49 = f32[1,1024]{1,0:T(1,128)S(1)} collective-permute-done((f32[1,1024]{1,0:T(1,128)S(1)}, f32[1,1024]{1,0:T(1,128)S(1)}, u32[]{:S(2)}, u32[]{:S(2)}) %collective-permute-start.49) | collective-permute-done | bytes 4128 | tf_op jit(solution)/shard_map/ppermute | solution.py:492
  519.0 5.0 collective-permute-done.51
  526.5 9.9 %place.7 = bf16[3072,1024]{1,0:T(8,128)(2,1)} custom-call(s32[3]{0:T(128)} %pad_add_fusion.info, bf16[768,1024]{1,0:T(8,128)(2,1)} %copy-done.5, bf16[768,1024]{1,0:T(8,128)(2,1)} %copy-done.14, bf16[768,1024]{1,0:T(8,128)(2,1)} %collective-permute-done.43.far, bf16[768,512]{1,0:T(8,128)(2,1)} %copy-done.23, bf16[768,512]{1,0:T(8,128)(2,1)} %collective-permute-done.48.right), custom_call_target="tpu_custom_call" | custom-call | bytes 12582912 | tf_op jit(solution)/shard_map/place/pallas_call | solution.py:325
  539.9 4.3 fusion.1
  (290 shorter events, 108.7 us)
Async XLA Ops:
  7.2 491.6 %all-reduce.4.cloned.1.call-start = ((), (), s32[]{:S(2)}) async-start(), calls=%async_computation | async-start | bytes 4718592 | tf_op jit(solution)/shard_map/psum | solution.py:687
  10.4 26.3 %collective-permute-start.2 = (bf16[4112,128]{1,0:T(8,128)(2,1)S(1)}, bf16[4112,128]{1,0:T(8,128)(2,1)S(1)}, u32[]{:S(2)}, u32[]{:S(2)}) collective-permute-start(bf16[4112,128]{1,0:T(8,128)(2,1)S(1)} %concatenate.43), channel_id=1, source_target_pairs={{0,2},{1,3},{2,0},{3,1},{4,6},{5,7},{6,4},{7,5},{8,10},{9,11},{10,... | collective-permute-start | bytes 3158024 | tf_op jit(solution)/shard_map/ppermute | solution.py:492
  13.4 25.1 %collective-permute-start = (bf16[4112,128]{1,0:T(8,128)(2,1)S(1)}, bf16[4112,128]{1,0:T(8,128)(2,1)S(1)}, u32[]{:S(2)}, u32[]{:S(2)}) collective-permute-start(bf16[4112,128]{1,0:T(8,128)(2,1)S(1)} %concatenate.43), channel_id=1, source_target_pairs={{0,1},{1,0},{2,3},{3,2},{4,5},{5,4},{6,7},{7,6},{8,9},{9,8},{10,11... | collective-permute-start | bytes 3158024 | tf_op jit(solution)/shard_map/ppermute | solution.py:492
  101.7 45.1 %collective-permute-start.10 = (bf16[256,1024]{1,0:T(8,128)(2,1)}, bf16[256,1024]{1,0:T(8,128)(2,1)S(1)}, u32[]{:S(2)}, u32[]{:S(2)}) collective-permute-start(bf16[256,1024]{1,0:T(8,128)(2,1)} %get-tuple-element.232), channel_id=1, source_target_pairs={{0,1},{1,0},{2,3},{3,2},{4,5},{5,4},{6,7},{7,6},{8,9},{9,8},{10,11... | collective-permute-start | bytes 1572872 | tf_op jit(solution)/shard_map/ppermute | solution.py:492
  102.8 44.0 %collective-permute-start.11 = (bf16[256,1024]{1,0:T(8,128)(2,1)}, bf16[256,1024]{1,0:T(8,128)(2,1)S(1)}, u32[]{:S(2)}, u32[]{:S(2)}) collective-permute-start(bf16[256,1024]{1,0:T(8,128)(2,1)} %get-tuple-element.233), channel_id=1, source_target_pairs={{0,2},{1,3},{2,0},{3,1},{4,6},{5,7},{6,4},{7,5},{8,10},{9,11},{10,... | collective-permute-start | bytes 1572872 | tf_op jit(solution)/shard_map/ppermute | solution.py:492
  103.8 43.1 %collective-permute-start.9 = (bf16[256,1024]{1,0:T(8,128)(2,1)}, bf16[256,1024]{1,0:T(8,128)(2,1)S(1)}, u32[]{:S(2)}, u32[]{:S(2)}) collective-permute-start(bf16[256,1024]{1,0:T(8,128)(2,1)} %get-tuple-element.231), channel_id=1, source_target_pairs={{0,3},{1,2},{2,1},{3,0},{4,7},{5,6},{6,5},{7,4},{8,11},{9,10},{10,... | collective-permute-start | bytes 1572872 | tf_op jit(solution)/shard_map/ppermute | solution.py:492
  152.3 47.3 %collective-permute-start.12 = (bf16[256,1024]{1,0:T(8,128)(2,1)}, bf16[256,1024]{1,0:T(8,128)(2,1)S(1)}, u32[]{:S(2)}, u32[]{:S(2)}) collective-permute-start(bf16[256,1024]{1,0:T(8,128)(2,1)} %get-tuple-element.250.refs_31_.own), channel_id=1, source_target_pairs={{0,1},{1,0},{2,3},{3,2},{4,5},{5,4},{6,7},{7,6},{8,9},{9,8},{10,11... | collective-permute-start | bytes 1572872 | tf_op jit(solution)/shard_map/ppermute | solution.py:492
  153.3 46.2 %collective-permute-start.13 = (bf16[256,1024]{1,0:T(8,128)(2,1)}, bf16[256,1024]{1,0:T(8,128)(2,1)S(1)}, u32[]{:S(2)}, u32[]{:S(2)}) collective-permute-start(bf16[256,1024]{1,0:T(8,128)(2,1)} %get-tuple-element.250.refs_31_.own), channel_id=1, source_target_pairs={{0,2},{1,3},{2,0},{3,1},{4,6},{5,7},{6,4},{7,5},{8,10},{9,11},{10,... | collective-permute-start | bytes 1572872 | tf_op jit(solution)/shard_map/ppermute | solution.py:492
  154.3 45.2 %collective-permute-start.14 = (bf16[256,1024]{1,0:T(8,128)(2,1)S(1)}, bf16[256,1024]{1,0:T(8,128)(2,1)S(1)}, u32[]{:S(2)}, u32[]{:S(2)}) collective-permute-start(bf16[256,1024]{1,0:T(8,128)(2,1)S(1)} %copy-done.52), channel_id=1, source_target_pairs={{0,3},{1,2},{2,1},{3,0},{4,7},{5,6},{6,5},{7,4},{8,11},{9,10},{10,... | collective-permute-start | bytes 1572872 | tf_op jit(solution)/shard_map/ppermute | solution.py:492
  155.8 43.8 %collective-permute-start.15 = (bf16[256,1024]{1,0:T(8,128)(2,1)S(1)}, bf16[256,1024]{1,0:T(8,128)(2,1)S(1)}, u32[]{:S(2)}, u32[]{:S(2)}) collective-permute-start(bf16[256,1024]{1,0:T(8,128)(2,1)S(1)} %copy-done.51), channel_id=1, source_target_pairs={{0,1},{1,0},{2,3},{3,2},{4,5},{5,4},{6,7},{7,6},{8,9},{9,8},{10,11... | collective-permute-start | bytes 1572872 | tf_op jit(solution)/shard_map/ppermute | solution.py:492
  156.8 42.8 %collective-permute-start.16 = (bf16[256,1024]{1,0:T(8,128)(2,1)S(1)}, bf16[256,1024]{1,0:T(8,128)(2,1)S(1)}, u32[]{:S(2)}, u32[]{:S(2)}) collective-permute-start(bf16[256,1024]{1,0:T(8,128)(2,1)S(1)} %copy-done.50), channel_id=1, source_target_pairs={{0,2},{1,3},{2,0},{3,1},{4,6},{5,7},{6,4},{7,5},{8,10},{9,11},{10,... | collective-permute-start | bytes 1572872 | tf_op jit(solution)/shard_map/ppermute | solution.py:492
  199.6 29.3 %collective-permute-start.17 = (bf16[256,1024]{1,0:T(8,128)(2,1)}, bf16[256,1024]{1,0:T(8,128)(2,1)S(1)}, u32[]{:S(2)}, u32[]{:S(2)}) collective-permute-start(bf16[256,1024]{1,0:T(8,128)(2,1)} %get-tuple-element.281), channel_id=1, source_target_pairs={{0,3},{1,2},{2,1},{3,0},{4,7},{5,6},{6,5},{7,4},{8,11},{9,10},{10,... | collective-permute-start | bytes 1572872 | tf_op jit(solution)/shard_map/ppermute | solution.py:492
  201.1 27.9 %collective-permute-start.18 = (bf16[256,1024]{1,0:T(8,128)(2,1)}, bf16[256,1024]{1,0:T(8,128)(2,1)S(1)}, u32[]{:S(2)}, u32[]{:S(2)}) collective-permute-start(bf16[256,1024]{1,0:T(8,128)(2,1)} %get-tuple-element.282), channel_id=1, source_target_pairs={{0,1},{1,0},{2,3},{3,2},{4,5},{5,4},{6,7},{7,6},{8,9},{9,8},{10,11... | collective-permute-start | bytes 1572872 | tf_op jit(solution)/shard_map/ppermute | solution.py:492
  202.2 26.8 %collective-permute-start.19 = (bf16[256,1024]{1,0:T(8,128)(2,1)}, bf16[256,1024]{1,0:T(8,128)(2,1)S(1)}, u32[]{:S(2)}, u32[]{:S(2)}) collective-permute-start(bf16[256,1024]{1,0:T(8,128)(2,1)} %get-tuple-element.283), channel_id=1, source_target_pairs={{0,2},{1,3},{2,0},{3,1},{4,6},{5,7},{6,4},{7,5},{8,10},{9,11},{10,... | collective-permute-start | bytes 1572872 | tf_op jit(solution)/shard_map/ppermute | solution.py:492
  256.0 31.3 %collective-permute-start.28 = (bf16[256,2304]{1,0:T(8,128)(2,1)}, bf16[256,2304]{1,0:T(8,128)(2,1)S(1)}, u32[]{:S(2)}, u32[]{:S(2)}) collective-permute-start(bf16[256,2304]{1,0:T(8,128)(2,1)} %dynamic-slice_convert_fusion.1), channel_id=1, source_target_pairs={{0,8},{4,12},{8,0},{12,4},{16,24},{20,28},{24,16},{28,20},{1,9},{5... | collective-permute-start | bytes 3538952 | tf_op jit(solution)/shard_map/ppermute | solution.py:497
  287.4 26.9 %collective-permute-start.30 = (bf16[256,512]{1,0:T(8,128)(2,1)S(1)}, bf16[256,512]{1,0:T(8,128)(2,1)S(1)}, u32[]{:S(2)}, u32[]{:S(2)}) collective-permute-start(bf16[256,512]{1,0:T(8,128)(2,1)S(1)} %slice.114), channel_id=1, source_target_pairs={{0,1},{1,0},{2,3},{3,2},{4,5},{5,4},{6,7},{7,6},{8,9},{9,8},{10,11... | collective-permute-start | bytes 786440 | tf_op jit(solution)/shard_map/ppermute | solution.py:492
  288.4 25.9 %collective-permute-start.31 = (bf16[256,512]{1,0:T(8,128)(2,1)S(1)}, bf16[256,512]{1,0:T(8,128)(2,1)S(1)}, u32[]{:S(2)}, u32[]{:S(2)}) collective-permute-start(bf16[256,512]{1,0:T(8,128)(2,1)S(1)} %slice.115), channel_id=1, source_target_pairs={{0,2},{1,3},{2,0},{3,1},{4,6},{5,7},{6,4},{7,5},{8,10},{9,11},{10,... | collective-permute-start | bytes 786440 | tf_op jit(solution)/shard_map/ppermute | solution.py:492
  292.9 50.3 %collective-permute-start.34 = (bf16[256,2304]{1,0:T(8,128)(2,1)}, bf16[256,2304]{1,0:T(8,128)(2,1)}, u32[]{:S(2)}, u32[]{:S(2)}) collective-permute-start(bf16[256,2304]{1,0:T(8,128)(2,1)} %add_convert_fusion.2), channel_id=1, source_target_pairs={{0,24},{4,28},{8,16},{12,20},{16,8},{20,12},{24,0},{28,4},{1,25},{... | collective-permute-start | bytes 3538952 | tf_op jit(solution)/shard_map/ppermute | solution.py:497
  315.6 27.5 %collective-permute-start.32 = (bf16[768,512]{1,0:T(8,128)(2,1)}, bf16[768,512]{1,0:T(8,128)(2,1)}, u32[]{:S(2)}, u32[]{:S(2)}) collective-permute-start(bf16[768,512]{1,0:T(8,128)(2,1)} %get-tuple-element.409), channel_id=1, source_target_pairs={{0,1},{1,0},{2,3},{3,2},{4,5},{5,4},{6,7},{7,6},{8,9},{9,8},{10,11... | collective-permute-start | bytes 2359304 | tf_op jit(solution)/shard_map/ppermute | solution.py:492
  317.1 26.1 %collective-permute-start.33 = (bf16[768,512]{1,0:T(8,128)(2,1)}, bf16[768,512]{1,0:T(8,128)(2,1)}, u32[]{:S(2)}, u32[]{:S(2)}) collective-permute-start(bf16[768,512]{1,0:T(8,128)(2,1)} %get-tuple-element.408), channel_id=1, source_target_pairs={{0,2},{1,3},{2,0},{3,1},{4,6},{5,7},{6,4},{7,5},{8,10},{9,11},{10,... | collective-permute-start | bytes 2359304 | tf_op jit(solution)/shard_map/ppermute | solution.py:492
  346.3 79.2 %collective-permute-start.41 = (bf16[256,2304]{1,0:T(8,128)(2,1)}, bf16[256,2304]{1,0:T(8,128)(2,1)}, u32[]{:S(2)}, u32[]{:S(2)}) collective-permute-start(bf16[256,2304]{1,0:T(8,128)(2,1)} %add_convert_fusion.1), channel_id=1, source_target_pairs={{0,8},{4,12},{8,0},{12,4},{16,24},{20,28},{24,16},{28,20},{1,9},{5... | collective-permute-start | bytes 3538952 | tf_op jit(solution)/shard_map/ppermute | solution.py:497
  362.5 32.4 %collective-permute-start.35 = (bf16[520,768]{1,0:T(8,128)(2,1)S(1)}, bf16[520,768]{1,0:T(8,128)(2,1)S(1)}, u32[]{:S(2)}, u32[]{:S(2)}) collective-permute-start(bf16[520,768]{1,0:T(8,128)(2,1)S(1)} %dynamic-slice_convert_fusion.2), channel_id=1, source_target_pairs={{0,4},{4,0},{8,12},{12,8},{16,20},{20,16},{24,28},{28,24},{1,5},{5... | collective-permute-start | bytes 2396168 | tf_op jit(solution)/shard_map/ppermute | solution.py:497
  389.9 36.7 %collective-permute-start.38 = (bf16[768,1024]{1,0:T(8,128)(2,1)}, bf16[768,1024]{1,0:T(8,128)(2,1)}, u32[]{:S(2)}, u32[]{:S(2)}) collective-permute-start(bf16[768,1024]{1,0:T(8,128)(2,1)} %pad_maximum_fusion.3), channel_id=1, source_target_pairs={{0,2},{1,3},{2,0},{3,1},{4,6},{5,7},{6,4},{7,5},{8,10},{9,11},{10,... | collective-permute-start | bytes 4718600 | tf_op jit(solution)/shard_map/ppermute | solution.py:492
  394.6 37.1 %collective-permute-start.37 = (bf16[768,1024]{1,0:T(8,128)(2,1)}, bf16[768,1024]{1,0:T(8,128)(2,1)}, u32[]{:S(2)}, u32[]{:S(2)}) collective-permute-start(bf16[768,1024]{1,0:T(8,128)(2,1)} %pad_maximum_fusion.2), channel_id=1, source_target_pairs={{0,1},{1,0},{2,3},{3,2},{4,5},{5,4},{6,7},{7,6},{8,9},{9,8},{10,11... | collective-permute-start | bytes 4718600 | tf_op jit(solution)/shard_map/ppermute | solution.py:492
  395.1 30.4 %collective-permute-start.39 = (bf16[260,768]{1,0:T(8,128)(2,1)S(1)}, bf16[260,768]{1,0:T(8,128)(2,1)S(1)}, u32[]{:S(2)}, u32[]{:S(2)}) collective-permute-start(bf16[260,768]{1,0:T(8,128)(2,1)S(1)} %dynamic-slice_convert_fusion.3), channel_id=1, source_target_pairs={{0,8},{4,12},{8,0},{12,4},{16,24},{20,28},{24,16},{28,20},{1,9},{5... | collective-permute-start | bytes 1198088 | tf_op jit(solution)/shard_map/ppermute | solution.py:497
  395.6 29.9 %collective-permute-start.40 = (bf16[64,1024]{1,0:T(8,128)(2,1)S(1)}, bf16[64,1024]{1,0:T(8,128)(2,1)S(1)}, u32[]{:S(2)}, u32[]{:S(2)}) collective-permute-start(bf16[64,1024]{1,0:T(8,128)(2,1)S(1)} %dynamic-slice_convert_fusion.5), channel_id=1, source_target_pairs={{0,8},{4,12},{8,0},{12,4},{16,24},{20,28},{24,16},{28,20},{1,9},{5... | collective-permute-start | bytes 393224 | tf_op jit(solution)/shard_map/ppermute | solution.py:497
  434.8 63.9 %collective-permute-start.42 = (bf16[768,1024]{1,0:T(8,128)(2,1)S(1)}, bf16[768,1024]{1,0:T(8,128)(2,1)S(1)}, u32[]{:S(2)}, u32[]{:S(2)}) collective-permute-start(bf16[768,1024]{1,0:T(8,128)(2,1)S(1)} %add_convert_fusion.refs_15_.own), channel_id=1, source_target_pairs={{0,1},{1,0},{2,3},{3,2},{4,5},{5,4},{6,7},{7,6},{8,9},{9,8},{10,11... | collective-permute-start | bytes 4718600 | tf_op jit(solution)/shard_map/ppermute | solution.py:492
  435.2 63.6 %collective-permute-start.43 = (bf16[768,1024]{1,0:T(8,128)(2,1)S(1)}, bf16[768,1024]{1,0:T(8,128)(2,1)}, u32[]{:S(2)}, u32[]{:S(2)}) collective-permute-start(bf16[768,1024]{1,0:T(8,128)(2,1)S(1)} %add_convert_fusion.refs_15_.own), channel_id=1, source_target_pairs={{0,2},{1,3},{2,0},{3,1},{4,6},{5,7},{6,4},{7,5},{8,10},{9,11},{10,... | collective-permute-start | bytes 4718600 | tf_op jit(solution)/shard_map/ppermute | solution.py:492
  439.4 97.0 %collective-permute-start.55 = (bf16[512,2304]{1,0:T(8,128)(2,1)}, bf16[512,2304]{1,0:T(8,128)(2,1)}, u32[]{:S(2)}, u32[]{:S(2)}) collective-permute-start(bf16[512,2304]{1,0:T(8,128)(2,1)} %pad_maximum_fusion.1), channel_id=1, source_target_pairs={{0,4},{4,0},{8,12},{12,8},{16,20},{20,16},{24,28},{28,24},{1,5},{5... | collective-permute-start | bytes 7077896 | tf_op jit(solution)/shard_map/ppermute | solution.py:497
  439.4 31.6 %collective-permute-start.46 = (f32[1,1024]{1,0:T(1,128)S(1)}, f32[1,1024]{1,0:T(1,128)S(1)}, u32[]{:S(2)}, u32[]{:S(2)}) collective-permute-start(f32[1,1024]{1,0:T(1,128)S(1)} %add_add_fusion), channel_id=1, source_target_pairs={{0,1},{1,0},{2,3},{3,2},{4,5},{5,4},{6,7},{7,6},{8,9},{9,8},{10,11... | collective-permute-start | bytes 12296 | tf_op jit(solution)/shard_map/ppermute | solution.py:492
  441.6 57.1 %collective-permute-start.44 = (bf16[260,768]{1,0:T(8,128)(2,1)}, bf16[260,768]{1,0:T(8,128)(2,1)S(1)}, u32[]{:S(2)}, u32[]{:S(2)}) collective-permute-start(bf16[260,768]{1,0:T(8,128)(2,1)} %add_convert_fusion.6.refs_13_), channel_id=1, source_target_pairs={{0,24},{4,28},{8,16},{12,20},{16,8},{20,12},{24,0},{28,4},{1,25},{... | collective-permute-start | bytes 1198088 | tf_op jit(solution)/shard_map/ppermute | solution.py:497
  471.0 27.7 %collective-permute-start.45 = (bf16[64,1024]{1,0:T(8,128)(2,1)}, bf16[64,1024]{1,0:T(8,128)(2,1)}, u32[]{:S(2)}, u32[]{:S(2)}) collective-permute-start(bf16[64,1024]{1,0:T(8,128)(2,1)} %add_convert_fusion.8.refs_14_), channel_id=1, source_target_pairs={{0,24},{4,28},{8,16},{12,20},{16,8},{20,12},{24,0},{28,4},{1,25},{... | collective-permute-start | bytes 393224 | tf_op jit(solution)/shard_map/ppermute | solution.py:497
  (81 other events, 948.2 us)
Sparse Core Ops, SparseCore 0:
  397.5 92.1 all-reduce.3
